TPU v7x, 32 devices: a whole 2x2x4 slice. The times are simulated.
32 devices in a mesh: gx: 8 (over z, y), gy: 4 (over x, core).
Axes of the slice: x: 2, y: 2, z: 4, core: 2. Of those that a mesh axis runs over, the one named last changes fastest.
Arguments:
- intensity: float32 [512, 512, 512], P('gx', 'gy'), may hold values from -48 to 48
- template: int32 [32, 32, 32], replicated, may hold values from 0 to 1, as said below
Outputs:
- pdf: float32 [512, 512, 512], P('gx', 'gy')
Inputs may be any that keep to these rules, and one draw needn't show every extreme that they name: template marks the cells of the period near its corner, within a drawn radius, and a few other cells.
All inputs are finite; a program needn't handle non-finite values.
Results may differ from a plain program's by a relative error of at most 0.0003.
Values sent between devices are 32-bit elements; how exact they have to be, the bound alone decides.
No kernel may reach another device: no remote copies, remote signals or barrier semaphores. Data moves between devices by JAX's collectives and lax.ppermute only.
A program may use at most 192 MiB of HBM per device.

v0:
```python
import math

import jax
import jax.numpy as jnp
from jax import lax
from jax.sharding import PartitionSpec as P

SWEEPS = 2


AXIS_ORDERS = ((0, 1, 2), (0, 2, 1), (1, 0, 2), (1, 2, 0), (2, 0, 1), (2, 1, 0))


def with_halo(array, sides, width):
    for axis, dim in sides:
        peers, length = (lax.axis_size(axis), array.shape[dim])
        up = [(i, (i + 1) % peers) for i in range(peers)]
        down = [(j, i) for i, j in up]
        last = lax.slice_in_dim(array, length - width, length, axis=dim)
        leading = lax.slice_in_dim(array, 0, width, axis=dim)
        before = lax.ppermute(last, axis, up)
        after = lax.ppermute(leading, axis, down)
        array = jnp.concatenate([before, array, after], axis=dim)
    return array


def mirror(values, axis):
    return jnp.roll(jnp.flip(values, axis), 1, axis)


def symmetric_marks(marks):
    for flip_axis in range(3):
        marks = jnp.maximum(marks, mirror(marks, flip_axis))
    united = marks
    for axis_order in AXIS_ORDERS[1:]:
        united = jnp.maximum(united, jnp.transpose(marks, axis_order))
    return united


def cosine_table(length):
    position = jnp.arange(length, dtype=jnp.int32)
    phases = jnp.mod(position[:, None] * position[None, :], length)
    return jnp.cos(phases.astype(jnp.float32) * (2.0 * math.pi / length)) / math.sqrt(length)


def neighbour_mean(padded):
    beside_all = padded[2:, 1:-1, 1:-1] + padded[:-2, 1:-1, 1:-1]
    beside_all = beside_all + padded[1:-1, 2:, 1:-1] + padded[1:-1, :-2, 1:-1]
    beside_all = beside_all + padded[1:-1, 1:-1, 2:] + padded[1:-1, 1:-1, :-2]
    return beside_all / 6.0


def outer_turn(volume):
    moved = lax.all_to_all(volume, "gx", split_axis=2, concat_axis=0, tiled=True)
    return jnp.transpose(moved, (2, 1, 0))


def inner_turn(volume):
    moved = lax.all_to_all(volume, "gy", split_axis=2, concat_axis=1, tiled=True)
    return jnp.transpose(moved, (0, 2, 1))


def hole_block(united, first_rows, first_cols, rows_here, cols_here, width, length):
    period = united.shape[0]
    offset_rows = jnp.mod(first_rows - width, period)
    offset_cols = jnp.mod(first_cols - width, period)
    shifted = jnp.roll(jnp.roll(united == 1, -offset_rows, 0), -offset_cols, 1)
    span_rows = rows_here + 2 * width
    span_cols = cols_here + 2 * width
    tile_rows = -(-span_rows // period)
    tile_cols = -(-span_cols // period)
    tiled = jnp.tile(shifted, (tile_rows, tile_cols, length // period))
    return tiled


def on_device(intensity, template):
    rows_here, cols_here, length = intensity.shape
    first_rows = lax.axis_index("gx") * rows_here
    first_cols = lax.axis_index("gy") * cols_here
    united = symmetric_marks(template)
    weight = 6.0
    paired = intensity + outer_turn(intensity)
    cycled = inner_turn(paired)
    averaged = (paired + cycled + outer_turn(cycled)) / weight
    holes = hole_block(united, first_rows, first_cols, rows_here, cols_here, 0, length)
    filled = jnp.where(holes, jnp.zeros_like(averaged), averaged)
    for sweep_step in range(SWEEPS):
        padded = with_halo(filled, (("gx", 0), ("gy", 1)), 1)
        padded = jnp.pad(padded, ((0, 0), (0, 0), (1, 1)), mode="wrap")
        filled = jnp.where(holes, neighbour_mean(padded), filled)
    cosines = cosine_table(length)
    highest = lax.Precision.HIGHEST
    spectrum = jnp.dot(
        filled.reshape(rows_here * cols_here, length),
        cosines,
        precision=highest,
        preferred_element_type=jnp.float32,
    )
    spectrum = spectrum.reshape(rows_here, cols_here, length)
    sectioned = jnp.einsum(
        "xbc,xr->bcr",
        lax.all_to_all(spectrum, "gx", split_axis=2, concat_axis=0, tiled=True),
        cosines,
        precision=highest,
    )
    return jnp.einsum(
        "xcb,xr->cbr",
        lax.all_to_all(sectioned, "gy", split_axis=2, concat_axis=0, tiled=True),
        cosines,
        precision=highest,
    )


def solution(mesh):
    placed = (P("gx", "gy", None), P())
    return jax.shard_map(
        on_device, mesh=mesh, in_specs=placed, out_specs=P("gx", "gy", None), check_vma=False
    )
```

profile of v0, /device:TPU:0, one launch (start us, length us, event | category | flops | bytes accessed | tf_op | source)
XLA Modules:
  0.0 2177.5 jit_solution(2512463889612065388)
XLA Ops:
  0.0 16.5 copy.82
  16.5 370.1 %all_to_all.90 = f32[64,128,512]{1,0,2:T(8,128)S(1)} all-to-all(f32[64,128,512]{1,0,2:T(8,128)} %copy.82), channel_id=1, replica_groups=mesh['gx'=8,'gy'=4] {'gx'}, dimensions={2} | all-to-all | bytes 33554432 | tf_op jit(solution)/shard_map/all_to_all | solution.py:54
  386.6 11.7 copy.81
  398.3 11.8 bitcast_add_fusion.1
  410.1 5.7 copy-done.1
  415.8 187.5 %all_to_all.91 = f32[64,128,512]{1,0,2:T(8,128)} all-to-all(f32[64,128,512]{1,0,2:T(8,128)S(1)} %bitcast_add_fusion.1), channel_id=1, replica_groups=mesh['gx'=8,'gy'=4] {'gy'}, dimensions={2} | all-to-all | bytes 33554432 | tf_op jit(solution)/shard_map/all_to_all | solution.py:59
  603.3 16.6 copy.83
  619.9 6.3 all-to-all-start.2
  626.4 0.1 add_maximum_fusion
  626.6 0.2 slice.139
  626.7 0.1 add_maximum_fusion.1
  626.9 0.2 slice.170
  627.1 0.2 slice.142
  627.3 0.2 add_maximum_fusion.2
  627.5 0.2 copy.76
  627.7 0.5 copy.75
  628.2 0.6 copy.74
  628.7 0.3 copy.73
  629.1 0.5 fusion.37
  629.6 0.4 dynamic-slice_add_fusion
  629.9 0.3 fusion.53
  630.2 0.3 copy.78
  630.5 16.4 tile.4
  646.8 38.1 %tile.10 = pred[64,128,512]{1,0,2:T(8,128)(4,1)} reshape(pred[2,32,4,32,16,32]{3,2,1,0,5,4:T(4,128)(4,1)} %tile.4) | data formatting | bytes 8388608 | tf_op jit(solution)/shard_map/tile | solution.py:72
  684.9 304.1 %all-to-all-done.2 = f32[64,128,512]{1,0,2:T(8,128)} async-done(((f32[64,128,512]{1,0,2:T(8,128)}), f32[64,128,512]{1,0,2:T(8,128)}, u32[]{:S(2)}, u32[]{:S(2)}) %all-to-all-start.2) | async-done | bytes 16777248 | tf_op jit(solution)/shard_map/all_to_all | solution.py:54
  989.0 17.9 copy.85
  1006.9 17.3 fusion.19
  1024.2 0.4 fusion.72
  1024.6 1.5 collective-permute-start.1
  1026.1 3.4 collective-permute-start
  1029.5 7.0 collective-permute-done.1
  1036.5 2.3 collective-permute-done
  1038.9 7.0 pad_maximum_fusion
  1045.9 13.4 fusion.70
  1059.2 11.5 copy.88
  1070.7 0.1 collective-permute-start.3
  1070.8 11.5 copy.86
  1082.3 1.8 collective-permute-start.2
  1084.1 10.5 copy.89
  1094.6 10.5 copy.87
  1105.1 93.8 %fusion.12 = f32[64,128,512]{1,0,2:T(8,128)} fusion(pred[64,128,512]{1,0,2:T(8,128)(4,1)} %tile.10, f32[64,128,512]{1,0,2:T(8,128)} %copy-done, f32[66,1,512]{1,0,2:T(8,128)} %copy.87, f32[66,1,512]{1,0,2:T(8,128)} %copy.89, f32[1,128,512]{1,0,2:T(1,128)S(1)} %collective-permute-done, f32[1,128,512]{1,0,2:T(1,128)S(1)} %collective-permute-done.1), kind=kLoop, calls=%fused_computation.39 | loop fusion | flops 138412032 | bytes 38543360 | tf_op jit(solution)/shard_map/jit(_where)/select_n | solution.py:90
  1198.9 2.6 fusion.71
  1201.5 0.2 collective-permute-start.5
  1201.7 4.8 collective-permute-start.4
  1206.5 6.0 collective-permute-done.5
  1212.5 2.5 collective-permute-done.4
  1215.0 7.0 pad_maximum_fusion.1
  1222.0 13.4 fusion.69
  1235.3 11.5 copy.94
  1246.9 11.5 copy.92
  1258.4 1.8 collective-permute-start.6
  1260.1 10.5 copy.95
  1270.7 10.5 copy.93
  1281.2 97.1 %fusion.3 = f32[64,128,512]{1,0,2:T(8,128)} fusion(pred[64,128,512]{1,0,2:T(8,128)(4,1)} %tile.10, f32[64,128,512]{1,0,2:T(8,128)} %fusion.12, f32[66,1,512]{1,0,2:T(8,128)} %copy.93, f32[66,1,512]{1,0,2:T(8,128)} %copy.95, f32[1,128,512]{1,0,2:T(1,128)S(1)} %collective-permute-done.4, f32[1,128,512]{1,0,2:T(1,128)S(1)} %collective-permute-done.5), kind=kLoop, calls=%fused_computation.6 | loop fusion | flops 138412032 | bytes 38543360 | tf_op jit(solution)/shard_map/jit(_where)/select_n | solution.py:90
  1378.3 51.1 %fusion.22 = f32[64,128,512]{2,1,0:T(8,128)} fusion(f32[64,128,512]{1,0,2:T(8,128)} %fusion.3), kind=kOutput, calls=%fused_computation.75 | convolution fusion | flops 25773735936 | bytes 33554432 | tf_op jit(solution)/shard_map/dot_general | solution.py:93
  1429.4 16.5 copy.99
  1445.9 367.0 %all_to_all.92 = f32[64,128,512]{1,0,2:T(8,128)S(1)} all-to-all(f32[64,128,512]{1,0,2:T(8,128)} %copy.99), channel_id=1, replica_groups=mesh['gx'=8,'gy'=4] {'gx'}, dimensions={2} | all-to-all | bytes 33554432 | tf_op jit(solution)/shard_map/all_to_all | solution.py:102
  1812.9 18.2 copy.101
  1831.1 56.5 %fusion.20 = f32[128,64,512]{2,0,1:T(8,128)} fusion(f32[512,128,64]{1,2,0:T(8,128)S(1)} %bitcast.65), kind=kOutput, calls=%fused_computation.73 | convolution fusion | flops 25773735936 | bytes 33554432 | tf_op jit(solution)/shard_map/xbc,xr->bcr/dot_general | solution.py:100
  1887.6 16.5 copy.103
  1904.1 187.7 %all_to_all.93 = f32[128,64,512]{0,1,2:T(8,128)S(1)} all-to-all(f32[128,64,512]{0,1,2:T(8,128)} %copy.103), channel_id=1, replica_groups=mesh['gx'=8,'gy'=4] {'gy'}, dimensions={2} | all-to-all | bytes 33554432 | tf_op jit(solution)/shard_map/all_to_all | solution.py:108
  2091.8 18.7 copy.114
  2110.5 19.9 all_to_all.84
  2130.4 46.8 %fusion.33 = f32[64,128,512]{2,1,0:T(8,128)} fusion(f32[512,64,128]{0,2,1:T(8,128)} %all_to_all.84), kind=kOutput, calls=%fused_computation.89 | convolution fusion | flops 25773735936 | bytes 33554432 | tf_op jit(solution)/shard_map/xcb,xr->cbr/dot_general | solution.py:106
  (19 shorter events, 0.2 us)
Async XLA Ops:
  410.1 5.7 copy-start.1
  619.9 6.4 slice-start.1
  619.9 6.4 copy-start.3
  619.9 6.4 slice-start
  619.9 369.0 %all-to-all-start.2 = ((f32[64,128,512]{1,0,2:T(8,128)}), f32[64,128,512]{1,0,2:T(8,128)}, u32[]{:S(2)}, u32[]{:S(2)}) async-start(f32[64,128,512]{1,0,2:T(8,128)} %bitcast.64), calls=%async_computation.2 | async-start | bytes 33554432 | tf_op jit(solution)/shard_map/all_to_all | solution.py:54
  989.0 17.9 copy-start.2
  1024.2 12.3 copy-start
  1024.6 11.9 collective-permute-start.1
  1026.1 12.7 collective-permute-start
  1070.7 13.3 collective-permute-start.3
  1082.3 12.3 collective-permute-start.2
  1201.5 10.9 collective-permute-start.5
  1201.7 13.2 collective-permute-start.4
  1246.8 13.3 collective-permute-start.7
  1258.4 12.3 collective-permute-start.6
where the time goes:
time: 2190 us; the launch traced here: 2180 us
  blocking collectives  1110 us (51%)
  local copies, waits for them, and re-layouts  333 us (15%)
  waiting for transfers between devices  322 us (15%)
  other arithmetic  236 us (11%)
  matrix products  154 us (7%)
    all_to_all x1, blocking collectives, outer_turn(): lax.all_to_all(volume, 'gx', split_axis=2, concat_axis=0, tiled=True)  370 us
    all_to_all x1, blocking collectives, on_device(): lax.all_to_all(spectrum, 'gx', split_axis=2, concat_axis=0, tiled=True)  367 us
    all_to_all x1, waiting for transfers between devices, outer_turn(): lax.all_to_all(volume, 'gx', split_axis=2, concat_axis=0, tiled=True)  304 us
    select_n x2, other arithmetic, on_device(): filled = jnp.where(holes, neighbour_mean(padded), filled)  191 us
    all_to_all x1, blocking collectives, on_device(): lax.all_to_all(sectioned, 'gy', split_axis=2, concat_axis=0, tiled=True)  188 us
    all_to_all x1, blocking collectives, inner_turn(): lax.all_to_all(volume, 'gy', split_axis=2, concat_axis=1, tiled=True)  187 us
    dot_general x1, matrix products, on_device(): jnp.einsum('xbc,xr->bcr', lax.all_to_all(spectrum, 'gx', split_axis=2, co...  56.5 us
    another operation x2, local copies, waits for them, and re-layouts, hole_block(): tiled = jnp.tile(shifted, (tile_rows, tile_cols, length // period))  54.5 us
  transfers between devices with their start and end apart: 9, of which 5 were waited for; matrix products, arithmetic and copies ran while one was open for 5% of the time, Pallas kernels for 0%

commit v1 on v0

v1 whole, which is shorter than its diff:
```python
import math

import jax
import jax.numpy as jnp
from jax import lax
from jax.experimental import pallas as pl
from jax.experimental.pallas import tpu as pltpu
from jax.sharding import PartitionSpec as P

SWEEPS = 2

AXIS_ORDERS = ((0, 1, 2), (0, 2, 1), (1, 0, 2), (1, 2, 0), (2, 0, 1), (2, 1, 0))

HIGH = lax.Precision.HIGH


def halo(array, axis, dim):
    peers, length = (lax.axis_size(axis), array.shape[dim])
    up = [(i, (i + 1) % peers) for i in range(peers)]
    down = [(j, i) for i, j in up]
    last = lax.slice_in_dim(array, length - SWEEPS, length, axis=dim)
    leading = lax.slice_in_dim(array, 0, SWEEPS, axis=dim)
    return lax.ppermute(last, axis, up), lax.ppermute(leading, axis, down)


def mirror(values, axis):
    return jnp.roll(jnp.flip(values, axis), 1, axis)


def symmetric_marks(marks):
    for flip_axis in range(3):
        marks = jnp.maximum(marks, mirror(marks, flip_axis))
    united = marks
    for axis_order in AXIS_ORDERS[1:]:
        united = jnp.maximum(united, jnp.transpose(marks, axis_order))
    return united


def cosine_table(length):
    position = jnp.arange(length, dtype=jnp.int32)
    phases = jnp.mod(position[:, None] * position[None, : length // 2 + 1], length)
    return jnp.cos(phases.astype(jnp.float32) * (2.0 * math.pi / length)) / math.sqrt(length)


MARGIN = 16
CHUNK = 16
STEP_ROWS = 16
VMEM_BYTES = 56 * 1024 * 1024


def split(values):
    high = values.astype(jnp.bfloat16)
    low = (values - high.astype(jnp.float32)).astype(jnp.bfloat16)
    return high, low


def fill_kernel(
    here, above, below, top, bottom, left, right, marks, table_high, table_low,
    spectrum, edge, punched, once, high, low,
):
    step, steps = pl.program_id(0), pl.num_programs(0)
    step_rows, cols, length = here.shape
    period = marks.shape[0]
    lane = lax.broadcasted_iota(jnp.int32, (CHUNK, edge.shape[1]), 1)
    place = lax.broadcasted_iota(jnp.int32, (CHUNK, length), 1)
    signs = jnp.where(place % 2 == 0, 1.0, -1.0).astype(jnp.float32)

    def holes(row, start, size):
        row = lax.rem(step * step_rows + row, period)
        start = start % period
        if start + size <= period:
            return marks[row, pl.ds(start, size), :]
        return jnp.concatenate(
            [marks[row, pl.ds(start, period - start), :], marks[row, pl.ds(0, start + size - period), :]],
            axis=0,
        )

    def punch(row, start, values):
        kept = jnp.where(holes(row, start, values.shape[0]) > 0.0, 0.0, values)
        punched[row, pl.ds(start, values.shape[0]), :] = kept

    def punch_row(row, source, index):
        full = step * step_rows + row
        punch(row, MARGIN - 8, left[full])
        punch(row, MARGIN + cols, right[full])
        for c in range(0, cols, CHUNK):
            punch(row, MARGIN + c, source[index, pl.ds(c, CHUNK), :])

    def neighbours(ref, row, start):
        middle = ref[row, pl.ds(start, CHUNK), :]
        total = ref[row - 1, pl.ds(start, CHUNK), :] + ref[row + 1, pl.ds(start, CHUNK), :]
        total += ref[row, pl.ds(start - 1, CHUNK), :] + ref[row, pl.ds(start + 1, CHUNK), :]
        return total + pltpu.roll(middle, 1, 1) + pltpu.roll(middle, length - 1, 1)

    for edge_rows, inside, offset, outer in (
        (above, step > 0, 0, top),
        (below, step < steps - 1, step_rows + SWEEPS, bottom),
    ):
        @pl.when(inside)
        def _():
            for r in range(SWEEPS):
                punch_row(offset + r, edge_rows, r)

        @pl.when(jnp.logical_not(inside))
        def _():
            for r in range(SWEEPS):
                punch_row(offset + r, outer, r)

    @pl.loop(0, step_rows)
    def _(r):
        punch_row(r + SWEEPS, here, r)

    @pl.loop(1, step_rows + 2 * SWEEPS - 1)
    def _(r):
        for start in range(MARGIN - 8, MARGIN + cols + 8, CHUNK):
            hole = holes(r, start, CHUNK)
            total = neighbours(punched, r, start) * (hole * (1.0 / 6.0))
            once[r, pl.ds(start, CHUNK), :] = punched[r, pl.ds(start, CHUNK), :] + total

    @pl.loop(0, step_rows)
    def _(r):
        for c in range(0, cols, CHUNK):
            start = MARGIN + c
            hole = holes(r + SWEEPS, start, CHUNK)
            total = neighbours(once, r + SWEEPS, start) * (hole * (1.0 / 6.0))
            filled = punched[r + SWEEPS, pl.ds(start, CHUNK), :] + total
            first, second = split(filled)
            spot = pl.ds(pl.multiple_of(r * cols + c, CHUNK), CHUNK)
            high[spot, :] = first
            low[spot, :] = second
            alternate = jnp.sum(filled * signs, axis=1, keepdims=True)
            old = edge[pl.ds(c, CHUNK), :]
            edge[pl.ds(c, CHUNK), :] = jnp.where(lane == step * step_rows + r, alternate, old)

    rows_each = 4
    @pl.loop(0, step_rows // rows_each)
    def _(r):
        spot = pl.ds(pl.multiple_of(r * rows_each * cols, CHUNK), rows_each * cols)
        first, second = high[spot, :], low[spot, :]
        total = jnp.dot(first, table_low[...], preferred_element_type=jnp.float32)
        total += jnp.dot(second, table_high[...], preferred_element_type=jnp.float32)
        total += jnp.dot(first, table_high[...], preferred_element_type=jnp.float32)
        spectrum[pl.ds(r * rows_each, rows_each)] = total.reshape(rows_each, cols, -1)


def filled_spectrum(intensity, template, row, col, main):
    rows, cols, length = intensity.shape
    half = main.shape[1]
    united = symmetric_marks(template)
    period = united.shape[0]
    offsets = (jnp.mod(row * rows - SWEEPS, period), jnp.mod(col * cols - MARGIN, period))
    marks = jnp.roll(united, (-offsets[0], -offsets[1]), (0, 1))
    marks = jnp.tile(marks, (1, 1, length // period)).astype(jnp.float32)
    top, bottom = halo(intensity, "gx", 0)
    tall = jnp.concatenate([top, intensity, bottom], axis=0)
    left, right = halo(tall, "gy", 1)
    left = jnp.pad(left, ((0, 0), (8 - SWEEPS, 0), (0, 0)))
    right = jnp.pad(right, ((0, 0), (0, 8 - SWEEPS), (0, 0)))
    step_rows = min(STEP_ROWS, rows)
    pairs = step_rows // SWEEPS
    last = rows // SWEEPS - 1
    whole = lambda array: pl.BlockSpec(array.shape, lambda i: (0,) * array.ndim)
    rounded = lax.reduce_precision(main, 8, 7)
    high, low = rounded.astype(jnp.bfloat16), (main - rounded).astype(jnp.bfloat16)
    spectrum, edge = pl.pallas_call(
        fill_kernel,
        grid=(rows // step_rows,),
        in_specs=[
            pl.BlockSpec((step_rows, cols, length), lambda i: (i, 0, 0)),
            pl.BlockSpec((SWEEPS, cols, length), lambda i: (jnp.maximum(i * pairs - 1, 0), 0, 0)),
            pl.BlockSpec((SWEEPS, cols, length), lambda i: (jnp.minimum((i + 1) * pairs, last), 0, 0)),
        ] + [whole(array) for array in (top, bottom, left, right, marks, high, low)],
        out_specs=[
            pl.BlockSpec((step_rows, cols, half), lambda i: (i, 0, 0)),
            pl.BlockSpec((cols, 128), lambda i: (0, 0)),
        ],
        out_shape=[
            jax.ShapeDtypeStruct((rows, cols, half), jnp.float32),
            jax.ShapeDtypeStruct((cols, 128), jnp.float32),
        ],
        scratch_shapes=[
            pltpu.VMEM((step_rows + 2 * SWEEPS, cols + 2 * MARGIN, length), jnp.float32),
            pltpu.VMEM((step_rows + 2 * SWEEPS, cols + 2 * MARGIN, length), jnp.float32),
            pltpu.VMEM((step_rows * cols, length), jnp.bfloat16),
            pltpu.VMEM((step_rows * cols, length), jnp.bfloat16),
        ],
        compiler_params=pltpu.CompilerParams(vmem_limit_bytes=VMEM_BYTES),
    )(intensity, intensity, intensity, top, bottom, left, right, marks, high, low)
    return spectrum, jnp.swapaxes(edge[:, :rows], 0, 1) / math.sqrt(length)


def on_device(intensity, template):
    rows, cols, length = intensity.shape
    gx, gy = lax.axis_size("gx"), lax.axis_size("gy")
    row, col = lax.axis_index("gx"), lax.axis_index("gy")
    devices, half = gx * gy, length // 2
    block = max(devices, rows)
    blocks, own, slabs = half // block, block // devices, gx // 2
    offsets = [block * b * (b + 1) // 2 for b in range(blocks + 1)]
    width = offsets[blocks]
    table = cosine_table(length)
    main = table[:, :half]

    spectrum, edge = filled_spectrum(intensity, template, row, col, main)

    table_rows = lax.dynamic_slice_in_dim(table, row * rows, rows, 0)
    table_cols = lax.dynamic_slice_in_dim(table, col * cols, cols, 0)
    marks = [rows * (m + 1) for m in range(slabs)]
    with_edge = jnp.concatenate([spectrum, edge[:, :, None]], axis=2)
    weights_rows = jnp.stack([table_rows[:, m] for m in marks])
    weights_cols = jnp.stack([table_cols[:, m] for m in marks])
    along0 = jnp.einsum("ma,abk->mbk", weights_rows, with_edge, precision=HIGH)
    along1 = jnp.einsum("mb,abk->mak", weights_cols, with_edge, precision=HIGH)
    along2 = jnp.stack([with_edge[:, :, m] for m in marks])
    planes = jnp.einsum("bj,mbk->mjk", table_cols, along0, precision=HIGH)
    along1 = along1 + jnp.einsum("mab,bk->mak", along2, table_cols, precision=HIGH)
    planes = planes + jnp.einsum("aj,mak->mjk", table_rows, along1, precision=HIGH)
    planes = lax.psum(planes, ("gx", "gy"))
    planes = (planes + jnp.swapaxes(planes, 1, 2)) / 6.0

    pair_rows = rows // 2
    halves = spectrum.reshape(2, pair_rows, cols, half)
    core = lax.rem(col, 2)
    kept = lax.dynamic_index_in_dim(halves, core, 0, keepdims=False)
    given = lax.dynamic_index_in_dim(halves, 1 - core, 0, keepdims=False)
    got = lax.ppermute(given, "gy", [(q, q ^ 1) for q in range(gy)])
    mates = lax.dynamic_slice_in_dim(main, (col + 1 - 2 * core) * cols, cols, 0)
    section = jnp.einsum("abk,bj->ajk", kept, table_cols[:, :half], precision=HIGH)
    section = section + jnp.einsum("abk,bj->ajk", got, mates, precision=HIGH)
    section = section + jnp.swapaxes(section, 1, 2)
    packed = jnp.concatenate(
        [section[:, b * block : (b + 1) * block, : (b + 1) * block] for b in range(blocks)], axis=2
    )
    share = block // gy
    packed = jnp.swapaxes(packed.reshape(pair_rows, gy, share, width), 0, 1)
    packed = lax.all_to_all(packed, "gy", 0, 0, tiled=True)
    packed = jnp.sum(packed.reshape(gy // 2, rows, share, width), axis=0)

    packed = jnp.swapaxes(packed, 0, 1).reshape(gx, own, rows, width)
    packed = lax.all_to_all(packed, "gx", 0, 0, tiled=True)
    values = jnp.einsum(
        "geaw,gai->eiw", packed, main.reshape(gx, rows, half), precision=HIGH
    ) / 6.0

    turned = values.reshape(own, blocks, devices, own, width)
    turned = jnp.transpose(turned, (2, 1, 3, 0, 4))
    turned = lax.all_to_all(turned, ("gy", "gx"), 0, 0, tiled=True)
    turned = jnp.transpose(turned, (1, 2, 0, 3, 4)).reshape(blocks, own, block, width)
    sums = []
    for top in range(blocks):
        size = (top + 1) * block
        part = values[:, :size, offsets[top] : offsets[top] + size]
        part = part + jnp.swapaxes(part, 1, 2)
        lower = [
            turned[top, :, :, offsets[b] : offsets[b] + (b + 1) * block] for b in range(top + 1)
        ]
        sums.append(part + square(lower, block))

    messages = []
    for slab in range(slabs):
        base = slab * rows // block
        first = slab * rows
        units = []
        for b in range(blocks):
            size = (b + 1) * block
            near = sums[b][:, first : first + rows, :size] if b >= base else None
            far = sums[base][:, b * block : size, :size] if b < base else None
            if rows == block:
                units.append(far if near is None else near)
            else:
                near = jnp.zeros((own, rows, size)) if near is None else near
                far = jnp.zeros((own, block, size)) if far is None else far
                units.append(jnp.concatenate([near, far], axis=1))
        messages.append(jnp.concatenate(units, axis=2))
    messages = jnp.stack(messages + messages[::-1])
    depth = messages.shape[2]
    got = lax.all_to_all(messages, "gx", 0, 0, tiled=True)
    got = lax.all_gather(got, "gy", axis=0, tiled=True).reshape(block, depth, width)
    slab = jnp.minimum(row, gx - 1 - row)
    base = slab * rows // block
    lower = []
    for b in range(blocks):
        lanes = slice(offsets[b], offsets[b] + (b + 1) * block)
        near = jnp.swapaxes(got[:, :rows, lanes], 0, 1)
        far = got[:, depth - block :, lanes]
        start = lax.rem(slab * rows, block)
        far = lax.dynamic_slice_in_dim(far, start, rows, 0)
        lower.append(jnp.where(b >= base, near, far))
    body = square(lower, block)

    far_row, far_col = row >= slabs, col >= gy // 2
    last = planes[slabs - 1]
    across = lax.dynamic_slice_in_dim(last, slab * rows, rows, 0)
    body = jnp.concatenate([body, across[:, None, :half]], axis=1)
    body = jnp.concatenate([body, across[:, :, None]], axis=2)
    next_plane = lax.dynamic_index_in_dim(planes, slab, 0)
    body = jnp.concatenate([body, next_plane], axis=0)
    pick_rows = jnp.arange(rows)
    pick_rows = jnp.where(far_row, rows - pick_rows, pick_rows)
    pick_cols = jnp.arange(cols)
    pick_cols = jnp.where(far_col, (gy - col) * cols - pick_cols, col * cols + pick_cols)
    body = body[pick_rows][:, pick_cols]
    return jnp.concatenate([body, jnp.flip(body[:, :, 1:half], 2)], axis=2)


def square(lower, block):
    lines = []
    for b in range(len(lower)):
        parts = [lower[b]]
        for c in range(b + 1, len(lower)):
            parts.append(jnp.swapaxes(lower[c][:, :, b * block : (b + 1) * block], 1, 2))
        lines.append(jnp.concatenate(parts, axis=2))
    return jnp.concatenate(lines, axis=1)


def solution(mesh):
    placed = (P("gx", "gy", None), P())
    return jax.shard_map(
        on_device, mesh=mesh, in_specs=placed, out_specs=P("gx", "gy", None), check_vma=False
    )
```

time: 2190 us -> 902 us (0.41)
  blocking collectives: 1110 us -> 127 us
  other arithmetic: 236 us -> 103 us
  matrix products: 154 us -> 25.8 us
  waiting for transfers between devices: 322 us -> 223 us
  Pallas kernels: 0 us -> 74.2 us
  local copies, waits for them, and re-layouts: 333 us -> 309 us
    all_to_all x4 -> x2, blocking collectives: 1110 us -> 127 us  [the longest x1 64.9 us: on_device(): packed = lax.all_to_all(packed, 'gx', 0, 0, tiled=True)]
    all_to_all x1 -> x2, waiting for transfers between devices: 304 us -> 24.8 us  [the longest x1 24.4 us: on_device(): turned = lax.all_to_all(turned, ('gy', 'gx'), 0, 0, tiled=True)]
    select_n x3 -> x6, other arithmetic: 208 us -> 16.6 us  [the longest x4 16.6 us: on_device(): lower.append(jnp.where(b >= base, near, far))]
    psum x0 -> x1, waiting for transfers between devices: none -> 180 us  [on_device(): planes = lax.psum(planes, ('gx', 'gy'))]
    dot_general x3 -> x8, matrix products: 154 us -> 25.8 us  [the longest x1 6.44 us: on_device(): along1 = jnp.einsum('mb,abk->mak', weights_cols, with_edge, precision=HIGH)]
    all_to_all x6 -> x0, local copies, waits for them, and re-layouts: 103 us -> none  [the longest x2 38.6 us: on_device(): lax.all_to_all(sectioned, 'gy', split_axis=2, concat_axis=0, tiled=True)]
    pallas_call x0 -> x1, Pallas kernels: none -> 74.2 us  [filled_spectrum(): pl.pallas_call(fill_kernel, grid=(rows // step_rows,), in_specs=[pl.Block...]
    gather x0 -> x3, local copies, waits for them, and re-layouts: none -> 55.2 us  [on_device(): body = body[pick_rows][:, pick_cols]]
  transfers between devices with their start and end apart: 9 -> 9, of which waited for: 5 -> 5; matrix products, arithmetic and copies ran while one was open for 5% -> 12% of each run, Pallas kernels for 0% -> 0%
where the time goes in v1:
time: 902 us; the launch traced here: 892 us
  local copies, waits for them, and re-layouts  309 us (34%)
  waiting for transfers between devices  223 us (25%)
  blocking collectives  127 us (14%)
  other arithmetic  103 us (11%)
  Pallas kernels  74.2 us (8%)
  matrix products  25.8 us (3%)
  between operations  15.9 us (2%)
  starting transfers between devices  14.2 us (2%)
    psum x1, waiting for transfers between devices, on_device(): planes = lax.psum(planes, ('gx', 'gy'))  180 us
    pallas_call x1, Pallas kernels, filled_spectrum(): pl.pallas_call(fill_kernel, grid=(rows // step_rows,), in_specs=[pl.Block...  74.2 us
    all_to_all x1, blocking collectives, on_device(): packed = lax.all_to_all(packed, 'gx', 0, 0, tiled=True)  64.9 us
    all_to_all x1, blocking collectives, on_device(): packed = lax.all_to_all(packed, 'gy', 0, 0, tiled=True)  62.2 us
    gather x3, local copies, waits for them, and re-layouts, on_device(): body = body[pick_rows][:, pick_cols]  55.2 us
    unnamed x53, local copies, waits for them, and re-layouts  49.4 us
    transpose x11, local copies, waits for them, and re-layouts, square(): parts.append(jnp.swapaxes(lower[c][:, :, b * block:(b + 1) * block], 1, 2))  24.5 us
    all_to_all x1, waiting for transfers between devices, on_device(): turned = lax.all_to_all(turned, ('gy', 'gx'), 0, 0, tiled=True)  24.4 us
  transfers between devices with their start and end apart: 9, of which 5 were waited for; matrix products, arithmetic and copies ran while one was open for 12% of the time, Pallas kernels for 0%

profile of v1, /device:TPU:0, one launch (start us, length us, event | category | flops | bytes accessed | tf_op | source)
XLA Modules:
  0.0 892.2 jit_solution(17647836629277782857)
XLA Ops:
  7.4 2.3 fusion.75
  9.7 6.0 collective-permute-start.1
  22.2 2.9 fusion.13
  25.1 11.2 %collective-permute-done.top = f32[2,128,512]{2,1,0:T(8,128)S(1)} collective-permute-done((f32[2,128,512]{2,1,0:T(8,128)}, f32[2,128,512]{2,1,0:T(8,128)S(1)}, u32[]{:S(2)}, u32[]{:S(2)}) %collective-permute-start) | collective-permute-done | bytes 524320 | tf_op jit(solution)/shard_map/ppermute | solution.py:23
  36.3 7.7 constant_dynamic-update-slice_fusion.1
  47.1 4.1 tile.2
  51.2 7.5 convert_element_type.30.marks
  59.6 2.1 pad.8.left
  61.7 2.1 pad.9.right
  63.8 74.2 %shard_map.28 = (f32[64,128,256]{2,1,0:T(8,128)}, f32[128,128]{1,0:T(8,128)}) custom-call(f32[64,128,512]{2,1,0:T(8,128)} %below.1, f32[64,128,512]{2,1,0:T(8,128)} %below.1, f32[64,128,512]{2,1,0:T(8,128)} %below.1, f32[2,128,512]{2,1,0:T(8,128)} %copy-done.14, f32[2,128,512]{2,1,0:T(8,128)} %copy-done.13, f32[68,8,512]{2,1,0:T(8,128)} %pad.8.left, ...), custom_call_target="tpu_custom_call" | custom-call | tf_op jit(solution)/shard_map/pallas_call | solution.py:165
  138.0 4.7 dynamic-slice_bitcast_fusion
  143.3 7.1 collective-permute-done.4
  150.4 5.7 fusion.42
  156.2 6.4 fusion.3
  162.5 9.1 %copy.219 = f32[256,32,256]{0,2,1:T(8,128)} copy(f32[256,32,256]{2,0,1:T(8,128)} %fusion.3) | data formatting | bytes 16777216 | tf_op jit(solution)/shard_map/add | solution.py:229
  171.6 10.6 %bitcast_add_fusion = f32[32,256,256]{1,2,0:T(8,128)} fusion(f32[256,32,256]{2,0,1:T(8,128)} %fusion.3, f32[256,32,256]{0,2,1:T(8,128)} %copy.219), kind=kLoop, calls=%fused_computation.7 | loop fusion | flops 2097152 | bytes 25165824 | tf_op jit(solution)/shard_map/add | solution.py:230
  183.5 2.4 slice.377
  185.9 2.6 slice.378
  189.7 4.4 pad_maximum_fusion.3
  194.1 9.2 %copy.220 = f32[32,64,640]{2,1,0:T(8,128)} copy(f32[32,64,640]{1,2,0:T(8,128)} %pad_maximum_fusion.3) | data formatting | bytes 10485760 | tf_op jit(solution)/shard_map/concatenate | solution.py:231
  203.4 2.9 copy.221
  206.3 62.2 %all_to_all.20 = f32[4,32,16,640]{3,2,1,0:T(8,128)S(1)} all-to-all(f32[4,32,16,640]{3,2,1,0:T(8,128)S(1)} %copy.221), channel_id=1, replica_groups=mesh['gx'=8,'gy'=4] {'gy'}, dimensions={0} | all-to-all | bytes 10485760 | tf_op jit(solution)/shard_map/all_to_all | solution.py:236
  269.8 64.9 %all_to_all.21 = f32[8,2,64,640]{3,2,1,0:T(8,128)S(1)} all-to-all(f32[8,2,64,640]{3,2,1,0:T(8,128)S(1)} %bitcast.236), channel_id=1, replica_groups=mesh['gx'=8,'gy'=4] {'gx'}, dimensions={0} | all-to-all | bytes 5242880 | tf_op jit(solution)/shard_map/all_to_all | solution.py:240
  339.0 2.8 all-to-all-start.2
  350.6 24.4 %all-to-all-done.2 = f32[32,4,2,2,640]{4,3,2,1,0:T(2,128)S(1)} async-done(((f32[32,4,2,2,640]{4,3,2,1,0:T(2,128)}), f32[32,4,2,2,640]{4,3,2,1,0:T(2,128)S(1)}, u32[]{:S(2)}, u32[]{:S(2)}) %all-to-all-start.2) | async-done | bytes 1310752 | tf_op jit(solution)/shard_map/all_to_all | solution.py:247
  376.6 2.2 reshape.85
  419.2 3.6 all-to-all-start.3
  423.9 16.8 %copy.255 = f32[64,128,256]{0,1,2:T(8,128)} copy(f32[64,128,256]{2,1,0:T(8,128)} %get-tuple-element.7) | data formatting | bytes 16777216 | tf_op jit(solution)/shard_map/pallas_call | solution.py:165
  441.6 4.5 copy.250
  446.1 10.4 %pad_maximum_fusion.2 = f32[64,128,257]{2,1,0:T(8,128)} fusion(f32[64,128,1]{2,1,0:T(8,128)} %copy.250, f32[64,128,256]{2,1,0:T(8,128)} %get-tuple-element.7), kind=kLoop, calls=%fused_computation.4 | loop fusion | flops 2105344 | bytes 16842752 | tf_op jit(solution)/shard_map/concatenate | solution.py:209
  456.5 11.5 %copy.251 = f32[64,128,257]{1,0,2:T(8,128)} copy(f32[64,128,257]{2,1,0:T(8,128)} %pad_maximum_fusion.2) | data formatting | bytes 16842752 | tf_op jit(solution)/shard_map/concatenate | solution.py:209
  469.4 6.4 fusion.62
  476.4 2.6 fusion.55
  484.0 180.2 %all-reduce.4.cloned.1.call-done = f32[4,257,257]{1,2,0:T(8,128)} async-done(((f32[4,257,257]{1,2,0:T(8,128)}), f32[4,257,257]{1,2,0:T(8,128)}) %all-reduce.4.cloned.1.call-update) | async-done | bytes 1056800 | tf_op jit(solution)/shard_map/psum | solution.py:218
  664.3 2.1 copy.261
  667.2 5.0 copy.265
  672.2 2.8 slice.420
  676.9 4.7 slice_bitcast_fusion
  681.5 6.0 slice_bitcast_fusion.1
  690.2 2.6 bitcast_select_fusion.1
  692.8 2.9 copy.246
  695.8 6.7 copy_select_fusion.1
  702.5 3.2 slice_bitcast_fusion.4
  705.8 3.2 copy.247
  709.0 6.0 copy_select_fusion
  715.0 3.8 slice_bitcast_fusion.2
  719.0 3.0 copy.249
  721.9 2.9 copy.248
  724.8 5.9 pad_maximum_fusion.4
  730.7 6.8 copy.263
  737.5 4.9 constant_dynamic-update-slice_fusion.4
  742.4 2.9 maximum_dynamic-update-slice_fusion.1
  746.8 2.8 maximum_dynamic-update-slice_fusion
  750.2 2.3 constant_dynamic-update-slice_fusion.3
  752.5 2.4 dynamic-update-slice.4
  754.9 19.1 %pad_maximum_fusion = f32[65,257,257]{2,1,0:T(8,128)} fusion(f32[1,257,257]{2,1,0:T(8,128)S(1)} %copy.266, f32[64,257,1]{2,1,0:T(8,128)} %copy.265, f32[64,257,256]{2,1,0:T(8,128)} %dynamic-update-slice.4), kind=kLoop, calls=%fused_computation.2 | loop fusion | flops 8586370 | bytes 34345480 | tf_op jit(solution)/shard_map/concatenate | solution.py:297
  774.0 19.6 %gather_fusion = f32[64,257,257]{2,1,0:T(8,128)} fusion(f32[65,257,257]{2,1,0:T(8,128)} %pad_maximum_fusion, s32[1024]{0:T(1024)S(1)} %get-tuple-element.65), kind=kCustom, calls=%fused_computation | custom fusion | bytes 33817344 | tf_op jit(solution)/shard_map/gather | solution.py:302
  793.6 21.3 %copy.267 = f32[64,257,257]{2,0,1:T(8,128)} copy(f32[64,257,257]{2,1,0:T(8,128)} %gather_fusion) | data formatting | bytes 33817088 | tf_op jit(solution)/shard_map/gather | solution.py:302
  814.9 14.3 %gather_fusion.1 = f32[128,64,257]{2,1,0:T(8,128)} fusion(f32[64,257,257]{2,0,1:T(8,128)} %copy.267, s32[1024]{0:T(1024)S(1)} %get-tuple-element.64), kind=kCustom, calls=%fused_computation.1 | custom fusion | bytes 16843264 | tf_op jit(solution)/shard_map/gather | solution.py:302
  829.2 10.1 %slice.434 = f32[64,128,255]{2,0,1:T(8,128)} slice(f32[64,128,257]{2,0,1:T(8,128)} %bitcast.225), slice={[0:64], [0:128], [1:256]} | slice | bytes 16711680 | tf_op jit(solution)/shard_map/slice | solution.py:303
  839.3 13.2 %reverse.6 = f32[64,128,256]{2,0,1:T(8,128)} reverse(f32[64,128,256]{2,0,1:T(8,128)} %bitcast.233), dimensions={2} | reverse | bytes 16777216
  852.4 5.6 slice.477
  858.1 6.9 pad_maximum_fusion.1
  865.0 19.3 %copy.268 = f32[64,128,512]{2,1,0:T(8,128)} copy(f32[64,128,512]{2,0,1:T(8,128)S(1)} %pad_maximum_fusion.1) | data formatting | bytes 33554432 | tf_op jit(solution)/shard_map/concatenate | solution.py:303
  (154 shorter events, 86.2 us)
Async XLA Ops:
  7.4 9.4 %copy-start.15 = (s32[32,32,32]{2,1,0:T(8,128)S(1)}, s32[32,32,32]{2,1,0:T(8,128)}, u32[]{:S(2)}) copy-start(s32[32,32,32]{2,1,0:T(8,128)} %param.3) | copy-start | bytes 393220
  7.4 9.4 %slice-start = ((s32[32,32,32]{2,1,0:T(8,128)}), s32[1,32,32]{2,1,0:T(8,128)S(1)}, s32[]{:S(2)}) async-start(s32[32,32,32]{2,1,0:T(8,128)} %param.3), calls=%async_computation.6 | async-start | bytes 32768 | tf_op jit(solution)/shard_map/jit(_roll_static)/slice | solution.py:27
  9.7 34.4 %collective-permute-start.1 = (f32[2,128,512]{2,1,0:T(8,128)}, f32[2,128,512]{2,1,0:T(8,128)S(1)}, u32[]{:S(2)}, u32[]{:S(2)}) collective-permute-start(f32[2,128,512]{2,1,0:T(8,128)} %get-tuple-element.22), channel_id=1, source_target_pairs={{4,0},{8,4},{12,8},{16,12},{20,16},{24,20},{28,24},{0,28},{5,1},{9... | collective-permute-start | bytes 1572872 | tf_op jit(solution)/shard_map/ppermute | solution.py:23
  15.7 20.6 %collective-permute-start = (f32[2,128,512]{2,1,0:T(8,128)}, f32[2,128,512]{2,1,0:T(8,128)S(1)}, u32[]{:S(2)}, u32[]{:S(2)}) collective-permute-start(f32[2,128,512]{2,1,0:T(8,128)} %get-tuple-element.23), channel_id=1, source_target_pairs={{0,4},{4,8},{8,12},{12,16},{16,20},{20,24},{24,28},{28,0},{1,5},{5... | collective-permute-start | bytes 1572872 | tf_op jit(solution)/shard_map/ppermute | solution.py:23
  36.3 7.8 copy-start.14
  44.1 7.1 copy-start.13
  45.2 16.5 %collective-permute-start.3 = (f32[68,2,512]{2,1,0:T(2,128)}, f32[68,2,512]{2,1,0:T(2,128)}, u32[]{:S(2)}, u32[]{:S(2)}) collective-permute-start(f32[68,2,512]{2,1,0:T(2,128)} %get-tuple-element.17), channel_id=1, source_target_pairs={{1,0},{2,1},{3,2},{0,3},{5,4},{6,5},{7,6},{4,7},{9,8},{10,9},{11,1... | collective-permute-start | bytes 835592 | tf_op jit(solution)/shard_map/ppermute | solution.py:23
  46.3 13.2 %collective-permute-start.2 = (f32[68,2,512]{2,1,0:T(2,128)}, f32[68,2,512]{2,1,0:T(2,128)}, u32[]{:S(2)}, u32[]{:S(2)}) collective-permute-start(f32[68,2,512]{2,1,0:T(2,128)} %get-tuple-element.18), channel_id=1, source_target_pairs={{0,1},{1,2},{2,3},{3,0},{4,5},{5,6},{6,7},{7,4},{8,9},{9,10},{10,1... | collective-permute-start | bytes 835592 | tf_op jit(solution)/shard_map/ppermute | solution.py:23
  142.7 7.8 collective-permute-start.4
  150.4 5.7 copy-start
  183.5 5.0 copy-start.3
  339.0 36.0 %all-to-all-start.2 = ((f32[32,4,2,2,640]{4,3,2,1,0:T(2,128)}), f32[32,4,2,2,640]{4,3,2,1,0:T(2,128)S(1)}, u32[]{:S(2)}, u32[]{:S(2)}) async-start(f32[32,4,2,2,640]{4,3,2,1,0:T(2,128)} %bitcast.240), calls=%async_computation.2 | async-start | bytes 2621440 | tf_op jit(solution)/shard_map/all_to_all | solution.py:247
  399.9 0.8 copy-start.12
  399.9 13.1 %copy-start.16 = (f32[2,64,64]{2,1,0:T(8,128)S(1)}, f32[2,64,64]{2,1,0:T(8,128)}, u32[]{:S(2)}) copy-start(f32[2,64,64]{2,1,0:T(8,128)} %slice.407) | copy-start | bytes 98308
  407.7 4.4 copy-start.18
  407.7 5.3 copy-start.19
  407.7 7.1 copy-start.17
  419.2 63.1 %all-to-all-start.3 = ((f32[8,2,64,640]{3,2,1,0:T(8,128)}), f32[8,2,64,640]{3,2,1,0:T(8,128)S(1)}, u32[]{:S(2)}, u32[]{:S(2)}) async-start(f32[8,2,64,640]{3,2,1,0:T(8,128)} %fusion.37), calls=%async_computation.3 | async-start | bytes 5242880 | tf_op jit(solution)/shard_map/all_to_all | solution.py:277
  422.8 241.4 %all-reduce.4.cloned.1.call-start = ((), (), s32[]{:S(2)}) async-start(), calls=%async_computation.5 | async-start | bytes 3244032 | tf_op jit(solution)/shard_map/psum | solution.py:218
  469.4 7.0 copy-start.6
  481.9 190.3 %all-gather.2.cloned.1.call-start = ((), (), s32[]{:S(2)}) async-start(), calls=%async_computation.4 | async-start | bytes 13107200 | tf_op jit(solution)/shard_map/all_gather | solution.py:278
  482.4 1.6 copy-start.7
  664.3 2.1 copy-start.11
  702.5 3.3 copy-start.4
  715.0 4.0 copy-start.1
  737.5 4.9 copy-start.8
  737.5 4.9 copy-start.10
  742.4 3.3 copy-start.5
  742.4 4.4 copy-start.9
  746.8 3.4 copy-start.2
Sparse Core Ops, SparseCore 0:
  482.1 182.1 all-reduce.3
Sparse Core Ops, SparseCore 1:
  484.1 70.7 all-gather.1

commit v2 on v1

--- a/solution.py
+++ b/solution.py
@@ -215,8 +215,8 @@
     planes = jnp.einsum("bj,mbk->mjk", table_cols, along0, precision=HIGH)
     along1 = along1 + jnp.einsum("mab,bk->mak", along2, table_cols, precision=HIGH)
     planes = planes + jnp.einsum("aj,mak->mjk", table_rows, along1, precision=HIGH)
-    planes = lax.psum(planes, ("gx", "gy"))
-    planes = (planes + jnp.swapaxes(planes, 1, 2)) / 6.0
+    corner = planes[slabs - 1, half] + planes[slabs - 1, :, half]
+    corner = jnp.broadcast_to(jnp.pad(corner, (0, width - half - 1)), (1, block, width))
 
     pair_rows = rows // 2
     halves = spectrum.reshape(2, pair_rows, cols, half)
@@ -227,80 +227,208 @@
     mates = lax.dynamic_slice_in_dim(main, (col + 1 - 2 * core) * cols, cols, 0)
     section = jnp.einsum("abk,bj->ajk", kept, table_cols[:, :half], precision=HIGH)
     section = section + jnp.einsum("abk,bj->ajk", got, mates, precision=HIGH)
+    section = jnp.concatenate([section, planes[:, :half, :half]], axis=0)
     section = section + jnp.swapaxes(section, 1, 2)
     packed = jnp.concatenate(
         [section[:, b * block : (b + 1) * block, : (b + 1) * block] for b in range(blocks)], axis=2
     )
-    share = block // gy
-    packed = jnp.swapaxes(packed.reshape(pair_rows, gy, share, width), 0, 1)
+    packed = jnp.concatenate([packed, corner], axis=0)
+    layers = packed.shape[0]
+    packed = jnp.transpose(packed.reshape(layers, own, gy, gx, width), (2, 0, 1, 3, 4))
     packed = lax.all_to_all(packed, "gy", 0, 0, tiled=True)
-    packed = jnp.sum(packed.reshape(gy // 2, rows, share, width), axis=0)
-
-    packed = jnp.swapaxes(packed, 0, 1).reshape(gx, own, rows, width)
+    side = jnp.sum(packed[:, pair_rows:], axis=0)
+    packed = packed[:, :pair_rows].reshape(gy // 2, rows, own, gx, width)
+    packed = jnp.concatenate([jnp.sum(packed, axis=0), side], axis=0)
+
+    packed = jnp.transpose(packed, (2, 1, 0, 3))
     packed = lax.all_to_all(packed, "gx", 0, 0, tiled=True)
     values = jnp.einsum(
-        "geaw,gai->eiw", packed, main.reshape(gx, rows, half), precision=HIGH
-    ) / 6.0
-
-    turned = values.reshape(own, blocks, devices, own, width)
-    turned = jnp.transpose(turned, (2, 1, 3, 0, 4))
+        "geaw,gai->eiw", packed[:, :, :rows], main.reshape(gx, rows, half) / 6.0, precision=HIGH
+    )
+    side = jnp.sum(packed[:, :, rows:], axis=0) / 6.0
+    side = lax.all_gather(side, ("gy", "gx"), axis=0)
+    side = jnp.transpose(side, (2, 1, 0, 3)).reshape(slabs + 1, block, width)
+
+    turned = values.reshape(own, blocks, own, devices, width)
+    turned = jnp.transpose(turned, (3, 1, 2, 0, 4))
     turned = lax.all_to_all(turned, ("gy", "gx"), 0, 0, tiled=True)
-    turned = jnp.transpose(turned, (1, 2, 0, 3, 4)).reshape(blocks, own, block, width)
-    sums = []
-    for top in range(blocks):
-        size = (top + 1) * block
-        part = values[:, :size, offsets[top] : offsets[top] + size]
-        part = part + jnp.swapaxes(part, 1, 2)
-        lower = [
-            turned[top, :, :, offsets[b] : offsets[b] + (b + 1) * block] for b in range(top + 1)
-        ]
-        sums.append(part + square(lower, block))
-
+    turned = jnp.transpose(turned, (1, 2, 3, 0, 4)).reshape(blocks, own, block, width)
+
+    slab = jnp.minimum(row, gx - 1 - row)
+    far_row, far_col = row >= slabs, col >= gy // 2
+    pick_rows = jnp.arange(rows)
+    pick_rows = slab * rows + jnp.where(far_row, rows - pick_rows, pick_rows)
+    pick_cols = jnp.arange(cols)
+    pick_cols = jnp.where(far_col, (gy - col) * cols - pick_cols, col * cols + pick_cols)
+    last = square([side[slabs - 1][None, :, offsets[b] : offsets[b + 1]] for b in range(blocks)], block)[0]
+    rim = side[slabs, 0, : half + 1]
+    last = jnp.concatenate([last, rim[None, :half]], axis=0)
+    last = jnp.concatenate([last, rim[:, None]], axis=1)
+    across = last[pick_rows]
+    next_plane = lax.dynamic_index_in_dim(side, slab, 0, keepdims=False)
+
+    if rows == block:
+        messages = slab_messages(values, turned, offsets, slabs)
+        got = lax.all_to_all(messages, "gx", 0, 0, tiled=True)
+        got = lax.all_gather(got, "gy", axis=0, tiled=True)
+        rim_col = col == gy // 2
+        rim = across[:, pick_cols]
+        return result_block(
+            got, next_plane, across, rim, pick_cols, slab, far_row, rim_col, offsets
+        )
+
+    sums = axis_order_sums(values, turned, offsets, block)
     messages = []
-    for slab in range(slabs):
-        base = slab * rows // block
-        first = slab * rows
+    for s in range(slabs):
+        base, first = s * rows // block, s * rows
         units = []
         for b in range(blocks):
             size = (b + 1) * block
-            near = sums[b][:, first : first + rows, :size] if b >= base else None
-            far = sums[base][:, b * block : size, :size] if b < base else None
-            if rows == block:
-                units.append(far if near is None else near)
+            near = jnp.zeros((own, rows, size))
+            far = jnp.zeros((own, block, size))
+            if b >= base:
+                near = jnp.stack([sums[b][e][first : first + rows, :size] for e in range(own)])
             else:
-                near = jnp.zeros((own, rows, size)) if near is None else near
-                far = jnp.zeros((own, block, size)) if far is None else far
-                units.append(jnp.concatenate([near, far], axis=1))
+                far = jnp.stack([sums[base][e][b * block : size, :size] for e in range(own)])
+            units.append(jnp.concatenate([near, far], axis=1))
         messages.append(jnp.concatenate(units, axis=2))
     messages = jnp.stack(messages + messages[::-1])
-    depth = messages.shape[2]
     got = lax.all_to_all(messages, "gx", 0, 0, tiled=True)
-    got = lax.all_gather(got, "gy", axis=0, tiled=True).reshape(block, depth, width)
-    slab = jnp.minimum(row, gx - 1 - row)
+    got = lax.all_gather(got, "gy", axis=0, tiled=True)
+    got = jnp.swapaxes(got, 0, 1).reshape(block, rows + block, width)
     base = slab * rows // block
     lower = []
     for b in range(blocks):
-        lanes = slice(offsets[b], offsets[b] + (b + 1) * block)
+        lanes = slice(offsets[b], offsets[b + 1])
         near = jnp.swapaxes(got[:, :rows, lanes], 0, 1)
-        far = got[:, depth - block :, lanes]
-        start = lax.rem(slab * rows, block)
-        far = lax.dynamic_slice_in_dim(far, start, rows, 0)
+        far = lax.dynamic_slice_in_dim(got[:, rows:, lanes], lax.rem(slab * rows, block), rows, 0)
         lower.append(jnp.where(b >= base, near, far))
-    body = square(lower, block)
-
-    far_row, far_col = row >= slabs, col >= gy // 2
-    last = planes[slabs - 1]
-    across = lax.dynamic_slice_in_dim(last, slab * rows, rows, 0)
-    body = jnp.concatenate([body, across[:, None, :half]], axis=1)
-    body = jnp.concatenate([body, across[:, :, None]], axis=2)
-    next_plane = lax.dynamic_index_in_dim(planes, slab, 0)
-    body = jnp.concatenate([body, next_plane], axis=0)
-    pick_rows = jnp.arange(rows)
-    pick_rows = jnp.where(far_row, rows - pick_rows, pick_rows)
-    pick_cols = jnp.arange(cols)
-    pick_cols = jnp.where(far_col, (gy - col) * cols - pick_cols, col * cols + pick_cols)
-    body = body[pick_rows][:, pick_cols]
+    lower = jnp.concatenate(lower, axis=2)
+    lower = jnp.concatenate([lower, next_plane[None]], axis=0)
+    body = square([lower[:, :, offsets[b] : offsets[b + 1]] for b in range(blocks)], block)
+    body = body[pick_rows - slab * rows]
+    body = jnp.concatenate([body, across[:, None, :half]], axis=1)[:, pick_cols]
+    body = jnp.concatenate([body, across[:, pick_cols][:, :, None]], axis=2)
     return jnp.concatenate([body, jnp.flip(body[:, :, 1:half], 2)], axis=2)
+
+
+def axis_order_sums(values, turned, offsets, block):
+    sums = []
+    for top in range(len(offsets) - 1):
+        size = (top + 1) * block
+        parts = []
+        for e in range(values.shape[0]):
+            part = values[e, :size, offsets[top] : offsets[top] + size]
+            lower = [turned[top, e, :, offsets[b] : offsets[b + 1]] for b in range(top + 1)]
+            parts.append(part + part.T + square(lower, block))
+        sums.append(parts)
+    return sums
+
+
+def message_kernel(offsets, slabs, values, turned, messages):
+    blocks = len(offsets) - 1
+    block = offsets[1]
+    values, turned = values[...], turned[...]
+    own = values.shape[0]
+    sums = axis_order_sums(values, turned, offsets, block)
+    for s in range(slabs):
+        for e in range(own):
+            units = []
+            for b in range(blocks):
+                size = (b + 1) * block
+                if b >= s:
+                    units.append(sums[b][e][s * block : (s + 1) * block, :size])
+                else:
+                    units.append(sums[s][e][b * block : size, :size])
+            line = jnp.concatenate(units, axis=1)
+            for tile in range(messages.shape[1]):
+                part = line[:, tile * 128 : (tile + 1) * 128]
+                messages[s, tile, e] = part
+                messages[2 * slabs - 1 - s, tile, e] = part
+
+
+def slab_messages(values, turned, offsets, slabs):
+    own, block = values.shape[0], offsets[1]
+    shape = (2 * slabs, offsets[-1] // 128, own, block, 128)
+    return pl.pallas_call(
+        lambda *refs: message_kernel(offsets, slabs, *refs),
+        in_specs=[pl.BlockSpec(memory_space=pltpu.VMEM)] * 2,
+        out_specs=pl.BlockSpec(memory_space=pltpu.VMEM),
+        out_shape=jax.ShapeDtypeStruct(shape, jnp.float32),
+        compiler_params=pltpu.CompilerParams(vmem_limit_bytes=VMEM_BYTES),
+    )(values, turned)
+
+
+def result_kernel(
+    offsets, own, devices, places, got, next_plane, across, rim, pick, flip, out
+):
+    blocks, block = len(offsets) - 1, offsets[1]
+    tiles = offsets[-1] // 128
+    stride = tiles * own * block
+    step_rows, cols, length = out.shape
+    half = length // 2
+    slab, far_row, rim_col = places[0], places[1], places[2]
+    lane = lax.broadcasted_iota(jnp.int32, (block, 128), 1)
+    at_rim = lax.broadcasted_iota(jnp.int32, (cols, half), 0) + (1 - rim_col) == 0
+    rim_lane = lax.broadcasted_iota(jnp.int32, rim.shape, 1)
+    first_lane = lax.broadcasted_iota(jnp.int32, (cols, half), 1) == 0
+
+    @pl.loop(0, step_rows)
+    def _(r):
+        t = pl.program_id(0) * step_rows + r
+        i = jnp.where(far_row == 1, block - t, t)
+        inside = (jnp.zeros((block, 128), jnp.int32) + i) < block
+        i = jnp.minimum(i, block - 1)
+        source = lax.div(i, devices), lax.rem(i, devices)
+        parts = []
+        for tile in range(tiles):
+            start = tile * own * block
+            near = [
+                got[pl.ds(start + e * block + i, devices, stride=stride), :] for e in range(own)
+            ]
+            near = jnp.concatenate(near, axis=0)
+            far = pl.multiple_of(source[1] * stride + start + source[0] * block, block)
+            far = got[pl.ds(far, block), :]
+            kind = jnp.zeros((block, 128), jnp.int32)
+            for b in range(1, blocks):
+                kind += (lane + tile * 128 >= offsets[b]).astype(jnp.int32)
+            line = jnp.where(kind >= slab, near, far)
+            line = jnp.where(inside, line, next_plane[:, pl.ds(tile * 128, 128)])
+            parts.append(line)
+        line = jnp.concatenate(parts, axis=1)
+        plane = square([line[:, offsets[b] : offsets[b + 1]] for b in range(blocks)], block)
+        high, low = split(plane)
+        left = jnp.dot(pick[...], high, preferred_element_type=jnp.float32)
+        left += jnp.dot(pick[...], low, preferred_element_type=jnp.float32)
+        left = jnp.where(at_rim, across[pl.ds(t, 1), :], left)
+        high, low = split(left)
+        right = jnp.dot(high, flip[...], preferred_element_type=jnp.float32)
+        right += jnp.dot(low, flip[...], preferred_element_type=jnp.float32)
+        edge = jnp.sum(jnp.where(rim_lane == t, rim[...], 0.0), axis=1, keepdims=True)
+        out[r, :, pl.ds(0, half)] = left
+        out[r, :, pl.ds(half, half)] = jnp.where(first_lane, edge, right)
+
+
+def result_block(got, next_plane, across, rim, pick_cols, slab, far_row, rim_col, offsets):
+    devices, tiles, own, block, _ = got.shape
+    rows, half = across.shape[0], across.shape[1] - 1
+    cols = pick_cols.shape[0]
+    step_rows = 8
+    places = jnp.stack([slab, far_row.astype(jnp.int32), rim_col.astype(jnp.int32)])
+    cell = jnp.arange(half)
+    pick = (pick_cols[:, None] == cell[None, :]).astype(jnp.bfloat16)
+    flip = (cell[:, None] + cell[None, :] == half).astype(jnp.bfloat16)
+    rim = jnp.pad(rim.T, ((0, 0), (0, 128 - rows)))
+    whole = lambda array: pl.BlockSpec(array.shape, lambda i: (0,) * array.ndim)
+    arrays = (got.reshape(-1, 128), next_plane, across[:, :half], rim, pick, flip)
+    return pl.pallas_call(
+        lambda *refs: result_kernel(offsets, own, devices, *refs),
+        grid=(rows // step_rows,),
+        in_specs=[pl.BlockSpec(memory_space=pltpu.SMEM)] + [whole(array) for array in arrays],
+        out_specs=pl.BlockSpec((step_rows, cols, 2 * half), lambda i: (i, 0, 0)),
+        out_shape=jax.ShapeDtypeStruct((rows, cols, 2 * half), jnp.float32),
+        compiler_params=pltpu.CompilerParams(vmem_limit_bytes=VMEM_BYTES),
+    )(places, *arrays)
 
 
 def square(lower, block):
@@ -308,9 +436,10 @@
     for b in range(len(lower)):
         parts = [lower[b]]
         for c in range(b + 1, len(lower)):
-            parts.append(jnp.swapaxes(lower[c][:, :, b * block : (b + 1) * block], 1, 2))
-        lines.append(jnp.concatenate(parts, axis=2))
-    return jnp.concatenate(lines, axis=1)
+            part = lower[c][..., b * block : (b + 1) * block]
+            parts.append(jnp.swapaxes(part, -1, -2))
+        lines.append(jnp.concatenate(parts, axis=-1))
+    return jnp.concatenate(lines, axis=-2)
 
 
 def solution(mesh):

time: 902 us -> 646 us (0.72)
  local copies, waits for them, and re-layouts: 309 us -> 91.9 us
  waiting for transfers between devices: 223 us -> 8.61 us
  blocking collectives: 127 us -> 317 us
  other arithmetic: 103 us -> 38.3 us
  Pallas kernels: 74.2 us -> 135 us
    psum x1 -> x0, waiting for transfers between devices: 180 us -> none  [on_device(): planes = lax.psum(planes, ('gx', 'gy'))]
    all_to_all x0 -> x2, blocking collectives: none -> 99.6 us  [the longest x1 64 us: on_device(): got = lax.all_to_all(messages, 'gx', 0, 0, tiled=True)]
    all_gather x0 -> x1, blocking collectives: none -> 76 us  [on_device(): side = lax.all_gather(side, ('gy', 'gx'), axis=0)]
    pallas_call x0 -> x2, Pallas kernels: none -> 61.1 us  [the longest x1 55.2 us: result_block(): pl.pallas_call(lambda *refs: result_kernel(offsets, own, devices, *refs),...]
    gather x3, local copies, waits for them, and re-layouts: 55.2 us -> 1.4 us  [the longest x2 0.75 us: on_device(): across = last[pick_rows]]
    unnamed x53 -> x16, local copies, waits for them, and re-layouts: 49.4 us -> 8.17 us
    transpose x16 -> x8, local copies, waits for them, and re-layouts: 40.4 us -> 3.34 us  [the longest x1 1.48 us: on_device(): jnp.transpose(turned, (1, 2, 3, 0, 4)).reshape(blocks, own, block, width)]
    concatenate x6 -> x2, local copies, waits for them, and re-layouts: 41.2 us -> 9.71 us  [the longest x1 9.63 us: on_device(): section = jnp.concatenate([section, planes[:, :half, :half]], axis=0)]
  transfers between devices with their start and end apart: 9 -> 6, of which waited for: 5 -> 1; matrix products, arithmetic and copies ran while one was open for 12% -> 15% of each run, Pallas kernels for 0% -> 0%
where the time goes in v2:
time: 646 us; the launch traced here: 639 us
  blocking collectives  317 us (49%)
  Pallas kernels  135 us (21%)
  local copies, waits for them, and re-layouts  91.9 us (14%)
  other arithmetic  38.3 us (6%)
  matrix products  24.9 us (4%)
  between operations  14.4 us (2%)
  waiting for transfers between devices  8.61 us (1%)
  starting transfers between devices  7.91 us (1%)
    all_gather x1, blocking collectives, on_device(): side = lax.all_gather(side, ('gy', 'gx'), axis=0)  76 us
    pallas_call x1, Pallas kernels, filled_spectrum(): pl.pallas_call(fill_kernel, grid=(rows // step_rows,), in_specs=[pl.Block...  74.2 us
    all_to_all x1, blocking collectives, on_device(): packed = lax.all_to_all(packed, 'gy', 0, 0, tiled=True)  71.1 us
    all_to_all x1, blocking collectives, on_device(): packed = lax.all_to_all(packed, 'gx', 0, 0, tiled=True)  70.5 us
    all_to_all x1, blocking collectives, on_device(): got = lax.all_to_all(messages, 'gx', 0, 0, tiled=True)  64 us
    pallas_call x1, Pallas kernels, result_block(): pl.pallas_call(lambda *refs: result_kernel(offsets, own, devices, *refs),...  55.2 us
    all_to_all x1, blocking collectives, on_device(): turned = lax.all_to_all(turned, ('gy', 'gx'), 0, 0, tiled=True)  35.6 us
    pallas_call x1, local copies, waits for them, and re-layouts, filled_spectrum(): pl.pallas_call(fill_kernel, grid=(rows // step_rows,), in_specs=[pl.Block...  16.5 us
  transfers between devices with their start and end apart: 6, of which 1 were waited for; matrix products, arithmetic and copies ran while one was open for 15% of the time, Pallas kernels for 0%

profile of v2, /device:TPU:0, one launch (start us, length us, event | category | flops | bytes accessed | tf_op | source)
XLA Modules:
  0.0 638.5 jit_solution(1108084549034658612)
XLA Ops:
  6.5 2.2 fusion.67
  8.8 3.0 collective-permute-start
  11.7 3.0 collective-permute-start.1
  14.8 1.1 slice.198
  15.8 0.7 slice.197
  16.6 1.1 add_maximum_fusion
  19.0 0.5 copy.127
  19.4 0.6 copy.126
  20.0 1.1 copy.125
  21.1 1.5 bitcast_maximum_fusion
  23.0 2.9 fusion.11
  25.9 8.6 %collective-permute-done.top = f32[2,128,512]{2,1,0:T(8,128)S(1)} collective-permute-done((f32[2,128,512]{2,1,0:T(8,128)}, f32[2,128,512]{2,1,0:T(8,128)S(1)}, u32[]{:S(2)}, u32[]{:S(2)}) %collective-permute-start) | collective-permute-done | bytes 524320 | tf_op jit(solution)/shard_map/ppermute | solution.py:23
  34.5 7.7 %constant_dynamic-update-slice_fusion.1 = f32[68,128,512]{2,1,0:T(8,128)S(1)} fusion(f32[68,128,512]{2,1,0:T(8,128)S(1)} %constant_dynamic-update-slice_fusion.2, f32[64,128,512]{2,1,0:T(8,128)} %below.1), kind=kLoop, calls=%fused_computation.105 | loop fusion | bytes 33554432
  42.3 1.1 fusion.66
  43.4 1.9 collective-permute-start.3
  45.5 0.6 copy.130
  46.0 4.1 tile.2
  50.1 7.3 %convert_element_type.42.marks = f32[32,32,512]{2,1,0:T(8,128)} reshape(f32[32,32,16,32]{3,2,1,0:T(8,128)} %tile.2) | data formatting | bytes 4194304 | tf_op jit(solution)/shard_map/convert_element_type | solution.py:153
  57.5 1.1 fusion.68
  58.5 2.1 pad.16.left
  60.6 2.1 pad.17.right
  62.8 74.2 %shard_map.28 = (f32[64,128,256]{2,1,0:T(8,128)}, f32[128,128]{1,0:T(8,128)}) custom-call(f32[64,128,512]{2,1,0:T(8,128)} %below.1, f32[64,128,512]{2,1,0:T(8,128)} %below.1, f32[64,128,512]{2,1,0:T(8,128)} %below.1, f32[2,128,512]{2,1,0:T(8,128)} %copy-done.2, f32[2,128,512]{2,1,0:T(8,128)} %copy-done.3, f32[68,8,512]{2,1,0:T(8,128)} %pad.16.left, ...), custom_call_target="tpu_custom_call" | custom-call | tf_op jit(solution)/shard_map/pallas_call | solution.py:165
  136.9 4.7 dynamic-slice_bitcast_fusion
  142.1 16.5 %copy.138 = f32[64,128,256]{0,1,2:T(8,128)} copy(f32[64,128,256]{2,1,0:T(8,128)} %get-tuple-element.7) | data formatting | bytes 16777216 | tf_op jit(solution)/shard_map/pallas_call | solution.py:165
  158.6 4.5 copy.133
  163.1 10.5 %pad_maximum_fusion = f32[64,128,257]{2,1,0:T(8,128)} fusion(f32[64,128,1]{2,1,0:T(8,128)} %copy.133, f32[64,128,256]{2,1,0:T(8,128)} %get-tuple-element.7), kind=kLoop, calls=%fused_computation.2 | loop fusion | flops 2105344 | bytes 16842752 | tf_op jit(solution)/shard_map/concatenate | solution.py:209
  173.5 11.5 %copy.134 = f32[64,128,257]{1,0,2:T(8,128)} copy(f32[64,128,257]{2,1,0:T(8,128)} %pad_maximum_fusion) | data formatting | bytes 16842752 | tf_op jit(solution)/shard_map/concatenate | solution.py:209
  185.0 0.9 slice_bitcast_fusion.4
  185.9 0.4 fusion.20
  186.4 6.6 %fusion.53 = f32[4,64,257]{2,0,1:T(4,128)S(1)} fusion(f32[1,128]{1,0:T(1,128)S(1)} %bitcast.177, f32[1,128]{1,0:T(1,128)S(1)} %bitcast.178, f32[1,128]{1,0:T(1,128)S(1)} %bitcast.179, f32[1,128]{1,0:T(1,128)S(1)} %bitcast.176, f32[64,128,1]{2,1,0:T(8,128)} %copy.133, f32[64,128,256]{2,1,0:T(8,128)} %get-tuple-element.7), kind=kOutput, calls=%fused_computation.125 | convolution fusion | flops 52635136 | bytes 8686592 | tf_op jit(solution)/shard_map/mb,abk->mak/dot_general | solution.py:213
  193.0 0.4 copy-done
  193.4 2.6 fusion.46
  196.0 0.9 fusion.15
  196.9 0.9 add_bitcast_fusion.1
  198.0 5.7 fusion.33
  203.8 6.4 %add_bitcast_fusion = f32[32,256,256]{2,1,0:T(8,128)} fusion(f32[256,32,256]{2,0,1:T(8,128)S(1)} %fusion.33, f32[2,32,128,256]{3,2,1,0:T(8,128)S(1)} %bitcast.149, s32[]{:T(128)S(6)} %select_n.134, f32[512,257]{1,0:T(8,128)S(1)} %fusion.11, s32[]{:T(128)S(6)} %select_n.127), kind=kOutput, calls=%fused_computation.5 | convolution fusion | flops 1612709888 | bytes 21102600 | tf_op jit(solution)/shard_map/abk,bj->ajk/dot_general | solution.py:228
  210.2 8.1 %pad_maximum_fusion.1 = f32[36,256,256]{2,1,0:T(8,128)} fusion(f32[4,256,256]{2,1,0:T(8,128)S(1)} %slice.257, f32[32,256,256]{2,1,0:T(8,128)} %add_bitcast_fusion), kind=kLoop, calls=%fused_computation.3 | loop fusion | flops 2359296 | bytes 18874368 | tf_op jit(solution)/shard_map/concatenate | solution.py:230
  218.2 9.6 %copy.146 = f32[36,256,256]{1,2,0:T(8,128)} copy(f32[36,256,256]{2,1,0:T(8,128)} %pad_maximum_fusion.1) | data formatting | bytes 18874368 | tf_op jit(solution)/shard_map/concatenate | solution.py:230
  227.9 7.0 %bitcast_add_fusion = f32[36,256,256]{2,1,0:T(8,128)S(1)} fusion(f32[36,256,256]{1,2,0:T(8,128)} %copy.146, f32[4,256,256]{2,1,0:T(8,128)S(1)} %slice.257, f32[32,256,256]{2,1,0:T(8,128)} %add_bitcast_fusion), kind=kLoop, calls=%fused_computation.4 | loop fusion | flops 4718592 | bytes 28311552 | tf_op jit(solution)/shard_map/add | solution.py:231
  235.5 2.3 pad_maximum_fusion.2
  237.8 0.5 copy.190
  238.3 71.1 %all_to_all.20 = f32[4,37,2,8,640]{4,3,2,1,0:T(8,128)S(1)} all-to-all(f32[4,37,2,8,640]{4,3,2,1,0:T(8,128)S(1)} %bitcast.151), channel_id=1, replica_groups=mesh['gx'=8,'gy'=4] {'gy'}, dimensions={0} | all-to-all | bytes 12124160 | tf_op jit(solution)/shard_map/all_to_all | solution.py:238
  309.4 0.5 slice.264
  309.9 0.5 bitcast_reduce_fusion
  310.6 1.5 copy.148
  312.0 70.5 %all_to_all.21 = f32[8,2,69,640]{3,1,2,0:T(2,128)S(1)} all-to-all(f32[8,2,69,640]{3,1,2,0:T(2,128)S(1)} %copy.148), channel_id=1, replica_groups=mesh['gx'=8,'gy'=4] {'gx'}, dimensions={0} | all-to-all | bytes 5652480 | tf_op jit(solution)/shard_map/all_to_all | solution.py:244
  382.5 0.9 slice.266
  383.5 1.4 fusion.5
  384.9 1.0 copy.191
  386.0 35.6 %all_to_all.22 = f32[32,4,2,2,640]{4,3,2,1,0:T(2,128)S(1)} all-to-all(f32[32,4,2,2,640]{4,3,2,1,0:T(2,128)S(1)} %bitcast.160), channel_id=1, replica_groups=mesh['gx'=8,'gy'=4] {'gy','gx'}, dimensions={0} | all-to-all | bytes 2621440 | tf_op jit(solution)/shard_map/all_to_all | solution.py:254
  421.6 1.5 copy.151
  423.1 5.9 shard_map.29
  429.0 64.0 %all_to_all.23 = f32[8,5,2,64,128]{4,3,2,1,0:T(8,128)} all-to-all(f32[8,5,2,64,128]{4,3,2,1,0:T(8,128)} %shard_map.29), channel_id=1, replica_groups=mesh['gx'=8,'gy'=4] {'gx'}, dimensions={0} | all-to-all | bytes 5242880 | tf_op jit(solution)/shard_map/all_to_all | solution.py:272
  493.0 0.6 pad_add_fusion.refs_0_
  493.6 0.7 fusion.28.refs_6_
  494.3 0.7 fusion.36.refs_5_
  495.1 76.0 %all-gather = f32[64,5,640]{2,1,0:T(8,128)S(1)} all-gather(f32[2,5,640]{2,1,0:T(8,128)S(1)} %copy_multiply_fusion), channel_id=2, replica_groups=mesh['gx'=8,'gy'=4] {'gy','gx'}, dimensions={0}, use_global_device_ids=true | all-gather | bytes 844800 | tf_op jit(solution)/shard_map/all_gather | solution.py:249
  571.1 0.4 copy.192
  572.7 0.7 gather_fusion
  573.3 0.6 slice.281.refs_3_
  574.1 0.6 gather_fusion.1
  574.7 0.6 pad.19.refs_4_
  575.3 0.7 dynamic-slice_bitcast_fusion.1.refs_2_
  576.0 55.2 %shard_map.30 = f32[64,128,512]{2,1,0:T(8,128)} custom-call(s32[3]{0:T(128)} %pad_add_fusion.refs_0_, f32[20480,128]{1,0:T(8,128)} %bitcast.155, f32[64,640]{1,0:T(8,128)} %dynamic-slice_bitcast_fusion.1.refs_2_, f32[64,256]{1,0:T(8,128)} %slice.281.refs_3_, f32[128,128]{1,0:T(8,128)} %pad.19.refs_4_, bf16[128,256]{1,0:T(8,128)(2,1)} %fusion.36.refs_5_, ...), custom_call_target="tpu_custom_call" | custom-call | tf_op jit(solution)/shard_map/pallas_call | solution.py:424
  (79 shorter events, 4.6 us)
Async XLA Ops:
  6.5 569.5 %all-gather.3.cloned.1.call-start = ((), (), s32[]{:S(2)}) async-start(), calls=%async_computation.4 | async-start | bytes 13107200 | tf_op jit(solution)/shard_map/all_gather | solution.py:273
  8.8 25.7 %collective-permute-start = (f32[2,128,512]{2,1,0:T(8,128)}, f32[2,128,512]{2,1,0:T(8,128)S(1)}, u32[]{:S(2)}, u32[]{:S(2)}) collective-permute-start(f32[2,128,512]{2,1,0:T(8,128)} %get-tuple-element.23), channel_id=1, source_target_pairs={{0,4},{4,8},{8,12},{12,16},{16,20},{20,24},{24,28},{28,0},{1,5},{5... | collective-permute-start | bytes 1572872 | tf_op jit(solution)/shard_map/ppermute | solution.py:23
  11.7 30.5 %collective-permute-start.1 = (f32[2,128,512]{2,1,0:T(8,128)}, f32[2,128,512]{2,1,0:T(8,128)S(1)}, u32[]{:S(2)}, u32[]{:S(2)}) collective-permute-start(f32[2,128,512]{2,1,0:T(8,128)} %get-tuple-element.22), channel_id=1, source_target_pairs={{4,0},{8,4},{12,8},{16,12},{20,16},{24,20},{28,24},{0,28},{5,1},{9... | collective-permute-start | bytes 1572872 | tf_op jit(solution)/shard_map/ppermute | solution.py:23
  34.5 7.8 %copy-start.2 = (f32[2,128,512]{2,1,0:T(8,128)}, f32[2,128,512]{2,1,0:T(8,128)S(1)}, u32[]{:S(2)}) copy-start(f32[2,128,512]{2,1,0:T(8,128)S(1)} %collective-permute-done.top) | copy-start | bytes 1572868
  42.3 7.9 %copy-start.3 = (f32[2,128,512]{2,1,0:T(8,128)}, f32[2,128,512]{2,1,0:T(8,128)S(1)}, u32[]{:S(2)}) copy-start(f32[2,128,512]{2,1,0:T(8,128)S(1)} %collective-permute-done.1.bottom) | copy-start | bytes 1572868
  43.4 15.1 %collective-permute-start.2 = (f32[68,2,512]{2,1,0:T(2,128)}, f32[68,2,512]{2,1,0:T(2,128)}, u32[]{:S(2)}, u32[]{:S(2)}) collective-permute-start(f32[68,2,512]{2,1,0:T(2,128)} %get-tuple-element.18), channel_id=1, source_target_pairs={{0,1},{1,2},{2,3},{3,0},{4,5},{5,6},{6,7},{7,4},{8,9},{9,10},{10,1... | collective-permute-start | bytes 835592 | tf_op jit(solution)/shard_map/ppermute | solution.py:23
  43.4 17.3 %collective-permute-start.3 = (f32[68,2,512]{2,1,0:T(2,128)}, f32[68,2,512]{2,1,0:T(2,128)}, u32[]{:S(2)}, u32[]{:S(2)}) collective-permute-start(f32[68,2,512]{2,1,0:T(2,128)} %get-tuple-element.17), channel_id=1, source_target_pairs={{1,0},{2,1},{3,2},{0,3},{5,4},{6,5},{7,6},{4,7},{9,8},{10,9},{11,1... | collective-permute-start | bytes 835592 | tf_op jit(solution)/shard_map/ppermute | solution.py:23
  141.6 56.4 %collective-permute-start.4 = (f32[32,128,256]{2,1,0:T(8,128)}, f32[32,128,256]{2,1,0:T(8,128)}, u32[]{:S(2)}, u32[]{:S(2)}) collective-permute-start(f32[32,128,256]{2,1,0:T(8,128)} %dynamic-slice_bitcast_fusion), channel_id=1, source_target_pairs={{0,1},{1,0},{2,3},{3,2},{4,5},{5,4},{6,7},{7,6},{8,9},{9,8},{10,11... | collective-permute-start | bytes 12582920 | tf_op jit(solution)/shard_map/ppermute | solution.py:226
  142.1 16.5 %copy-start.4 = (f32[128,128]{1,0:T(8,128)S(1)}, f32[128,128]{1,0:T(8,128)}, u32[]{:S(2)}) copy-start(f32[128,128]{1,0:T(8,128)} %get-tuple-element.8) | copy-start | bytes 196612
  186.3 7.0 %copy-start = (f32[64,128,257]{1,0,2:T(8,128)S(1)}, f32[64,128,257]{1,0,2:T(8,128)}, u32[]{:S(2)}) copy-start(f32[64,128,257]{1,0,2:T(8,128)} %copy.134) | copy-start | bytes 25264132
  196.9 6.9 %slice-start = ((s8[8388608]{0:T(1024)(128)(4,1)}), s8[4194304]{0:T(1024)(128)(4,1)S(1)}, s32[]{:S(2)}) async-start(s8[8388608]{0:T(1024)(128)(4,1)} %bitcast.147), calls=%async_computation.5 | async-start | bytes 8388608
  198.0 5.7 slice-start.1
  384.9 38.2 %copy-start.1 = (f32[256,2,640,1]{2,0,3,1:T(8,128)}, f32[256,2,640,1]{2,0,3,1:T(8,128)S(1)}, u32[]{:S(2)}) copy-start(f32[256,2,640,1]{2,0,3,1:T(8,128)S(1)} %fusion.5) | copy-start | bytes 3932164
Sparse Core Ops, SparseCore 0:
  493.1 68.8 all-gather.2

commit v3 on v2

--- a/solution.py
+++ b/solution.py
@@ -14,13 +14,26 @@
 HIGH = lax.Precision.HIGH
 
 
-def halo(array, axis, dim):
-    peers, length = (lax.axis_size(axis), array.shape[dim])
+def ring(axis):
+    peers = lax.axis_size(axis)
     up = [(i, (i + 1) % peers) for i in range(peers)]
-    down = [(j, i) for i, j in up]
-    last = lax.slice_in_dim(array, length - SWEEPS, length, axis=dim)
-    leading = lax.slice_in_dim(array, 0, SWEEPS, axis=dim)
-    return lax.ppermute(last, axis, up), lax.ppermute(leading, axis, down)
+    return up, [(j, i) for i, j in up]
+
+
+def halos(block):
+    rows, cols, _ = block.shape
+    up, down = ring("gx")
+    right, left = ring("gy")
+    top = lax.ppermute(block[rows - SWEEPS :], "gx", up)
+    bottom = lax.ppermute(block[:SWEEPS], "gx", down)
+    before = lax.ppermute(block[:, cols - SWEEPS :], "gy", right)
+    after = lax.ppermute(block[:, :SWEEPS], "gy", left)
+    sides = jnp.concatenate([before, after], axis=1)
+    above = lax.ppermute(sides[rows - SWEEPS :], "gx", up)
+    below = lax.ppermute(sides[:SWEEPS], "gx", down)
+    sides = jnp.concatenate([above, sides, below], axis=0)
+    free = ((0, 0), (8 - SWEEPS, 8 - SWEEPS), (0, 0))
+    return top, bottom, jnp.pad(sides, free)
 
 
 def mirror(values, axis):
@@ -45,6 +58,7 @@
 MARGIN = 16
 CHUNK = 16
 STEP_ROWS = 16
+PART_ROWS = 16
 VMEM_BYTES = 56 * 1024 * 1024
 
 
@@ -55,34 +69,39 @@
 
 
 def fill_kernel(
-    here, above, below, top, bottom, left, right, marks, table_high, table_low,
-    spectrum, edge, punched, once, high, low,
+    base, here, above, below, top, bottom, sides, marks, table_high, table_low,
+    spectrum, alternate, edge, punched, once, high, low,
 ):
-    step, steps = pl.program_id(0), pl.num_programs(0)
     step_rows, cols, length = here.shape
+    step = pl.program_id(0) + base[0]
+    first_row = step * step_rows
+    local_row = pl.program_id(0) * step_rows
     period = marks.shape[0]
     lane = lax.broadcasted_iota(jnp.int32, (CHUNK, edge.shape[1]), 1)
     place = lax.broadcasted_iota(jnp.int32, (CHUNK, length), 1)
     signs = jnp.where(place % 2 == 0, 1.0, -1.0).astype(jnp.float32)
+    inner = pl.ds(8 - SWEEPS, 2 * SWEEPS)
 
     def holes(row, start, size):
-        row = lax.rem(step * step_rows + row, period)
+        row = lax.rem(first_row + row, period)
         start = start % period
         if start + size <= period:
-            return marks[row, pl.ds(start, size), :]
-        return jnp.concatenate(
-            [marks[row, pl.ds(start, period - start), :], marks[row, pl.ds(0, start + size - period), :]],
-            axis=0,
-        )
+            part = marks[row, pl.ds(start, size), :]
+        else:
+            part = jnp.concatenate(
+                [marks[row, pl.ds(start, period - start), :], marks[row, pl.ds(0, start + size - period), :]],
+                axis=0,
+            )
+        return jnp.concatenate([part] * (length // 128), axis=1)
 
     def punch(row, start, values):
         kept = jnp.where(holes(row, start, values.shape[0]) > 0.0, 0.0, values)
         punched[row, pl.ds(start, values.shape[0]), :] = kept
 
     def punch_row(row, source, index):
-        full = step * step_rows + row
-        punch(row, MARGIN - 8, left[full])
-        punch(row, MARGIN + cols, right[full])
+        full = first_row + row
+        punch(row, MARGIN - 8, sides[full, pl.ds(0, 8), :])
+        punch(row, MARGIN + cols, sides[full, pl.ds(8, 8), :])
         for c in range(0, cols, CHUNK):
             punch(row, MARGIN + c, source[index, pl.ds(c, CHUNK), :])
 
@@ -92,9 +111,10 @@
         total += ref[row, pl.ds(start - 1, CHUNK), :] + ref[row, pl.ds(start + 1, CHUNK), :]
         return total + pltpu.roll(middle, 1, 1) + pltpu.roll(middle, length - 1, 1)
 
+    last = (sides.shape[0] - 2 * SWEEPS) // step_rows - 1
     for edge_rows, inside, offset, outer in (
         (above, step > 0, 0, top),
-        (below, step < steps - 1, step_rows + SWEEPS, bottom),
+        (below, step < last, step_rows + SWEEPS, bottom),
     ):
         @pl.when(inside)
         def _():
@@ -113,26 +133,27 @@
     @pl.loop(1, step_rows + 2 * SWEEPS - 1)
     def _(r):
         for start in range(MARGIN - 8, MARGIN + cols + 8, CHUNK):
-            hole = holes(r, start, CHUNK)
-            total = neighbours(punched, r, start) * (hole * (1.0 / 6.0))
+            total = neighbours(punched, r, start) * holes(r, start, CHUNK)
             once[r, pl.ds(start, CHUNK), :] = punched[r, pl.ds(start, CHUNK), :] + total
 
     @pl.loop(0, step_rows)
     def _(r):
         for c in range(0, cols, CHUNK):
             start = MARGIN + c
-            hole = holes(r + SWEEPS, start, CHUNK)
-            total = neighbours(once, r + SWEEPS, start) * (hole * (1.0 / 6.0))
+            total = neighbours(once, r + SWEEPS, start) * holes(r + SWEEPS, start, CHUNK)
             filled = punched[r + SWEEPS, pl.ds(start, CHUNK), :] + total
             first, second = split(filled)
             spot = pl.ds(pl.multiple_of(r * cols + c, CHUNK), CHUNK)
             high[spot, :] = first
             low[spot, :] = second
-            alternate = jnp.sum(filled * signs, axis=1, keepdims=True)
+            signed = jnp.sum(filled * signs, axis=1, keepdims=True)
             old = edge[pl.ds(c, CHUNK), :]
-            edge[pl.ds(c, CHUNK), :] = jnp.where(lane == step * step_rows + r, alternate, old)
-
-    rows_each = 4
+            edge[pl.ds(c, CHUNK), :] = jnp.where(lane == local_row + r, signed, old)
+
+    rows_each = 8
+    half = spectrum.shape[2]
+    order = lax.broadcasted_iota(jnp.int32, (rows_each, cols, half), 1)
+
     @pl.loop(0, step_rows // rows_each)
     def _(r):
         spot = pl.ds(pl.multiple_of(r * rows_each * cols, CHUNK), rows_each * cols)
@@ -140,53 +161,161 @@
         total = jnp.dot(first, table_low[...], preferred_element_type=jnp.float32)
         total += jnp.dot(second, table_high[...], preferred_element_type=jnp.float32)
         total += jnp.dot(first, table_high[...], preferred_element_type=jnp.float32)
-        spectrum[pl.ds(r * rows_each, rows_each)] = total.reshape(rows_each, cols, -1)
-
-
-def filled_spectrum(intensity, template, row, col, main):
+        total = total.reshape(rows_each, cols, half)
+        spectrum[pl.ds(r * rows_each, rows_each)] = total
+        signed = jnp.sum(jnp.where(order % 2 == 0, total, -total), axis=1)
+        alternate[pl.ds(pl.multiple_of(r * rows_each, rows_each), rows_each), :] = signed
+
+
+def rounded_parts(table):
+    rounded = lax.reduce_precision(table, 8, 7)
+    return rounded.astype(jnp.bfloat16), (table - rounded).astype(jnp.bfloat16)
+
+
+def fill_arrays(intensity, template, row, col, main):
     rows, cols, length = intensity.shape
-    half = main.shape[1]
     united = symmetric_marks(template)
     period = united.shape[0]
     offsets = (jnp.mod(row * rows - SWEEPS, period), jnp.mod(col * cols - MARGIN, period))
-    marks = jnp.roll(united, (-offsets[0], -offsets[1]), (0, 1))
-    marks = jnp.tile(marks, (1, 1, length // period)).astype(jnp.float32)
-    top, bottom = halo(intensity, "gx", 0)
-    tall = jnp.concatenate([top, intensity, bottom], axis=0)
-    left, right = halo(tall, "gy", 1)
-    left = jnp.pad(left, ((0, 0), (8 - SWEEPS, 0), (0, 0)))
-    right = jnp.pad(right, ((0, 0), (0, 8 - SWEEPS), (0, 0)))
-    step_rows = min(STEP_ROWS, rows)
+    marks = jnp.roll(united, (-offsets[0], -offsets[1]), (0, 1)).astype(jnp.float32) / 6.0
+    marks = jnp.tile(marks, (1, 1, 128 // period))
+    return halos(intensity) + (marks,) + rounded_parts(main)
+
+
+def filled_spectrum(intensity, arrays, first, count):
+    rows, cols, length = intensity.shape
+    half = length // 2
+    step_rows = min(STEP_ROWS, count)
     pairs = step_rows // SWEEPS
     last = rows // SWEEPS - 1
-    whole = lambda array: pl.BlockSpec(array.shape, lambda i: (0,) * array.ndim)
-    rounded = lax.reduce_precision(main, 8, 7)
-    high, low = rounded.astype(jnp.bfloat16), (main - rounded).astype(jnp.bfloat16)
-    spectrum, edge = pl.pallas_call(
+    whole = lambda array: pl.BlockSpec(array.shape, lambda i, b: (0,) * array.ndim)
+    before = lambda i, b: (jnp.maximum((i + b[0]) * pairs - 1, 0), 0, 0)
+    after = lambda i, b: (jnp.minimum((i + b[0] + 1) * pairs, last), 0, 0)
+    padded = (step_rows + 2 * SWEEPS, cols + 2 * MARGIN, length)
+    return pl.pallas_call(
         fill_kernel,
-        grid=(rows // step_rows,),
-        in_specs=[
-            pl.BlockSpec((step_rows, cols, length), lambda i: (i, 0, 0)),
-            pl.BlockSpec((SWEEPS, cols, length), lambda i: (jnp.maximum(i * pairs - 1, 0), 0, 0)),
-            pl.BlockSpec((SWEEPS, cols, length), lambda i: (jnp.minimum((i + 1) * pairs, last), 0, 0)),
-        ] + [whole(array) for array in (top, bottom, left, right, marks, high, low)],
-        out_specs=[
-            pl.BlockSpec((step_rows, cols, half), lambda i: (i, 0, 0)),
-            pl.BlockSpec((cols, 128), lambda i: (0, 0)),
-        ],
+        grid_spec=pltpu.PrefetchScalarGridSpec(
+            num_scalar_prefetch=1,
+            grid=(count // step_rows,),
+            in_specs=[
+                pl.BlockSpec((step_rows, cols, length), lambda i, b: (i + b[0], 0, 0)),
+                pl.BlockSpec((SWEEPS, cols, length), before),
+                pl.BlockSpec((SWEEPS, cols, length), after),
+            ] + [whole(array) for array in arrays],
+            out_specs=[
+                pl.BlockSpec((step_rows, cols, half), lambda i, b: (i, 0, 0)),
+                pl.BlockSpec((step_rows, half), lambda i, b: (i, 0)),
+                pl.BlockSpec((cols, 128), lambda i, b: (0, 0)),
+            ],
+            scratch_shapes=[
+                pltpu.VMEM(padded, jnp.float32),
+                pltpu.VMEM(padded, jnp.float32),
+                pltpu.VMEM((step_rows * cols, length), jnp.bfloat16),
+                pltpu.VMEM((step_rows * cols, length), jnp.bfloat16),
+            ],
+        ),
         out_shape=[
-            jax.ShapeDtypeStruct((rows, cols, half), jnp.float32),
+            jax.ShapeDtypeStruct((count, cols, half), jnp.float32),
+            jax.ShapeDtypeStruct((count, half), jnp.float32),
             jax.ShapeDtypeStruct((cols, 128), jnp.float32),
         ],
-        scratch_shapes=[
-            pltpu.VMEM((step_rows + 2 * SWEEPS, cols + 2 * MARGIN, length), jnp.float32),
-            pltpu.VMEM((step_rows + 2 * SWEEPS, cols + 2 * MARGIN, length), jnp.float32),
-            pltpu.VMEM((step_rows * cols, length), jnp.bfloat16),
-            pltpu.VMEM((step_rows * cols, length), jnp.bfloat16),
-        ],
         compiler_params=pltpu.CompilerParams(vmem_limit_bytes=VMEM_BYTES),
-    )(intensity, intensity, intensity, top, bottom, left, right, marks, high, low)
-    return spectrum, jnp.swapaxes(edge[:, :rows], 0, 1) / math.sqrt(length)
+        cost_estimate=pl.CostEstimate(
+            flops=count * cols * length * half * 6,
+            bytes_accessed=count * cols * length * 40,
+            transcendentals=0,
+        ),
+    )((first // step_rows).reshape(1), intensity, intensity, intensity, *arrays)
+
+
+def pack(section, offsets):
+    block = offsets[1]
+    units = [section[b * block : (b + 1) * block, : (b + 1) * block] for b in range(len(offsets) - 1)]
+    return jnp.concatenate(units, axis=1)
+
+
+def three_dots(left, right):
+    total = jnp.dot(left[1], right[0], preferred_element_type=jnp.float32)
+    total += jnp.dot(left[0], right[1], preferred_element_type=jnp.float32)
+    return total + jnp.dot(left[0], right[0], preferred_element_type=jnp.float32)
+
+
+def section_kernel(
+    offsets, closing, weights, kept, got, cols_high, cols_low, rows_high, rows_low,
+    rim, corner, before, out, total, lines,
+):
+    step, steps = pl.program_id(0), pl.num_programs(0)
+    step_rows = kept.shape[0]
+    half, count = rows_high.shape
+    planes, block, width = before.shape
+    gy, _, own, gx, _ = out.shape
+
+    def place(layer, values):
+        for e in range(own):
+            for q in range(gy):
+                start = (e * gy + q) * gx
+                out[q, layer, e] = values[start : start + gx]
+
+    @pl.when(step == 0)
+    def _():
+        total[...] = before[...]
+
+    @pl.loop(0, step_rows)
+    def _(r):
+        layer = step * step_rows + r
+        values = jnp.concatenate([kept[r], got[r]], axis=0)
+        section = three_dots((cols_high[...], cols_low[...]), split(values))
+        section = section + section.T
+        line = pack(section, offsets)
+        place(layer, line)
+        for m in range(planes):
+            total[m] += weights[m, layer] * line
+        for m in range(planes - 1):
+            row = (m + 1) * (half // planes)
+            lines[m, pl.ds(layer, 1), :] = section[row : row + 1]
+
+    @pl.when(step == steps - 1)
+    def _():
+        for m in range(planes - 1):
+            plane = three_dots((rows_high[...], rows_low[...]), split(lines[m]))
+            total[m] += pack(plane + plane.T, offsets)
+        if closing:
+            total[planes - 1] += pack(rim[...] + rim[...].T, offsets)
+            for m in range(planes):
+                place(count + m, total[m])
+            place(count + planes, jnp.zeros((block, width), jnp.float32) + corner[...])
+
+
+def packed_section(kept, got, table_pair, table_rows, marks, rim, corner, before, offsets, shape, closing):
+    count, cols, half = kept.shape
+    planes, block, width = before.shape
+    gx, gy = shape
+    step_rows = 4
+    layers = count + (planes + 1 if closing else 0)
+    whole = lambda array: pl.BlockSpec(array.shape, lambda i: (0,) * array.ndim)
+    weights = jnp.stack([table_rows[:, m] for m in marks])
+    arrays = rounded_parts(table_pair.T) + rounded_parts(table_rows[:, :half].T)
+    arrays += (rim, corner[None], before)
+    outs = [
+        jax.ShapeDtypeStruct((gy, layers, block // (gx * gy), gx, width), jnp.float32),
+        jax.ShapeDtypeStruct(before.shape, jnp.float32),
+    ]
+    rows_spec = pl.BlockSpec((step_rows, cols, half), lambda i: (i, 0, 0))
+    return pl.pallas_call(
+        lambda *refs: section_kernel(offsets, closing, *refs),
+        grid=(count // step_rows,),
+        in_specs=[pl.BlockSpec(memory_space=pltpu.SMEM), rows_spec, rows_spec]
+        + [whole(array) for array in arrays],
+        out_specs=[whole(out) for out in outs],
+        out_shape=outs,
+        scratch_shapes=[pltpu.VMEM((planes, count, half), jnp.float32)],
+        compiler_params=pltpu.CompilerParams(vmem_limit_bytes=VMEM_BYTES),
+        cost_estimate=pl.CostEstimate(
+            flops=count * 12 * cols * half * half,
+            bytes_accessed=count * cols * half * 60,
+            transcendentals=0,
+        ),
+    )(weights, kept, got, *arrays)
 
 
 def on_device(intensity, template):
@@ -201,51 +330,55 @@
     table = cosine_table(length)
     main = table[:, :half]
 
-    spectrum, edge = filled_spectrum(intensity, template, row, col, main)
-
-    table_rows = lax.dynamic_slice_in_dim(table, row * rows, rows, 0)
+    pair_rows = rows // 2
+    parts = max(pair_rows // PART_ROWS, 1)
+    count = pair_rows // parts
+    core = lax.rem(col, 2)
+    arrays = fill_arrays(intensity, template, row, col, main)
+    given_first, kept_first = (1 - core) * pair_rows, core * pair_rows
+    given, kept, got = [], [], []
+    for c in range(parts):
+        given.append(filled_spectrum(intensity, arrays, given_first + c * count, count))
+        got.append(lax.ppermute(given[c][0], "gy", [(q, q ^ 1) for q in range(gy)]))
+        kept.append(filled_spectrum(intensity, arrays, kept_first + c * count, count))
+
     table_cols = lax.dynamic_slice_in_dim(table, col * cols, cols, 0)
+    given_rows = lax.dynamic_slice_in_dim(table, row * rows + given_first, pair_rows, 0)
+    kept_rows = lax.dynamic_slice_in_dim(table, row * rows + kept_first, pair_rows, 0)
+    ordered_rows = jnp.concatenate([given_rows, kept_rows], axis=0)
+    alternate = jnp.concatenate([piece[1] for piece in given + kept], axis=0) / math.sqrt(length)
+    edge = jnp.concatenate([piece[2][:, :count] for piece in given + kept], axis=1)
+    edge = jnp.einsum("ba,bk->ak", edge / math.sqrt(length), table_cols, precision=HIGH)
+    edge = edge + jnp.concatenate([alternate, edge[:, half:]], axis=1)
+    rim = jnp.einsum("aj,ak->jk", ordered_rows[:, :half], edge[:, :half], precision=HIGH)
+    corner = 2.0 * jnp.einsum("a,ak->k", ordered_rows[:, half], edge, precision=HIGH)
+    corner = corner + jnp.einsum("aj,a->j", ordered_rows, edge[:, half], precision=HIGH)
+    corner = jnp.pad(corner, (0, width - half - 1))
+
     marks = [rows * (m + 1) for m in range(slabs)]
-    with_edge = jnp.concatenate([spectrum, edge[:, :, None]], axis=2)
-    weights_rows = jnp.stack([table_rows[:, m] for m in marks])
-    weights_cols = jnp.stack([table_cols[:, m] for m in marks])
-    along0 = jnp.einsum("ma,abk->mbk", weights_rows, with_edge, precision=HIGH)
-    along1 = jnp.einsum("mb,abk->mak", weights_cols, with_edge, precision=HIGH)
-    along2 = jnp.stack([with_edge[:, :, m] for m in marks])
-    planes = jnp.einsum("bj,mbk->mjk", table_cols, along0, precision=HIGH)
-    along1 = along1 + jnp.einsum("mab,bk->mak", along2, table_cols, precision=HIGH)
-    planes = planes + jnp.einsum("aj,mak->mjk", table_rows, along1, precision=HIGH)
-    corner = planes[slabs - 1, half] + planes[slabs - 1, :, half]
-    corner = jnp.broadcast_to(jnp.pad(corner, (0, width - half - 1)), (1, block, width))
-
-    pair_rows = rows // 2
-    halves = spectrum.reshape(2, pair_rows, cols, half)
-    core = lax.rem(col, 2)
-    kept = lax.dynamic_index_in_dim(halves, core, 0, keepdims=False)
-    given = lax.dynamic_index_in_dim(halves, 1 - core, 0, keepdims=False)
-    got = lax.ppermute(given, "gy", [(q, q ^ 1) for q in range(gy)])
     mates = lax.dynamic_slice_in_dim(main, (col + 1 - 2 * core) * cols, cols, 0)
-    section = jnp.einsum("abk,bj->ajk", kept, table_cols[:, :half], precision=HIGH)
-    section = section + jnp.einsum("abk,bj->ajk", got, mates, precision=HIGH)
-    section = jnp.concatenate([section, planes[:, :half, :half]], axis=0)
-    section = section + jnp.swapaxes(section, 1, 2)
-    packed = jnp.concatenate(
-        [section[:, b * block : (b + 1) * block, : (b + 1) * block] for b in range(blocks)], axis=2
-    )
-    packed = jnp.concatenate([packed, corner], axis=0)
-    layers = packed.shape[0]
-    packed = jnp.transpose(packed.reshape(layers, own, gy, gx, width), (2, 0, 1, 3, 4))
-    packed = lax.all_to_all(packed, "gy", 0, 0, tiled=True)
-    side = jnp.sum(packed[:, pair_rows:], axis=0)
-    packed = packed[:, :pair_rows].reshape(gy // 2, rows, own, gx, width)
-    packed = jnp.concatenate([jnp.sum(packed, axis=0), side], axis=0)
-
-    packed = jnp.transpose(packed, (2, 1, 0, 3))
-    packed = lax.all_to_all(packed, "gx", 0, 0, tiled=True)
-    values = jnp.einsum(
-        "geaw,gai->eiw", packed[:, :, :rows], main.reshape(gx, rows, half) / 6.0, precision=HIGH
-    )
-    side = jnp.sum(packed[:, :, rows:], axis=0) / 6.0
+    table_pair = jnp.concatenate([table_cols[:, :half], mates], axis=0)
+    table_parts = main.reshape(gx, 2, parts, count, half) / 6.0
+    side = jnp.zeros((slabs, block, width), jnp.float32)
+    values = 0.0
+    for c in range(parts):
+        closing = c == parts - 1
+        packed, side = packed_section(
+            kept[c][0], got[c], table_pair, kept_rows[c * count : (c + 1) * count], marks,
+            rim, corner, side, offsets, (gx, gy), closing,
+        )
+        packed = lax.all_to_all(packed, "gy", 0, 0, tiled=True)
+        lines = packed[:, :count].reshape(gy // 2, 2 * count, own, gx, width)
+        lines = jnp.sum(lines, axis=0)
+        if closing:
+            lines = jnp.concatenate([lines, jnp.sum(packed[:, count:], axis=0)], axis=0)
+        lines = jnp.transpose(lines, (2, 1, 0, 3))
+        lines = lax.all_to_all(lines, "gx", 0, 0, tiled=True)
+        table_part = table_parts[:, :, c].reshape(gx, 2 * count, half)
+        values = values + jnp.einsum(
+            "geaw,gai->eiw", lines[:, :, : 2 * count], table_part, precision=HIGH
+        )
+    side = jnp.sum(lines[:, :, 2 * count :], axis=0) / 6.0
     side = lax.all_gather(side, ("gy", "gx"), axis=0)
     side = jnp.transpose(side, (2, 1, 0, 3)).reshape(slabs + 1, block, width)
 

time: 646 us -> 566 us (0.88)
  blocking collectives: 317 us -> 176 us
  waiting for transfers between devices: 8.61 us -> 117 us
  local copies, waits for them, and re-layouts: 91.9 us -> 34.3 us
  Pallas kernels: 135 us -> 170 us
  starting transfers between devices: 7.91 us -> 28.6 us
  other arithmetic: 38.3 us -> 17.8 us
  matrix products: 24.9 us -> 6.74 us
    all_to_all x2 -> x0, blocking collectives: 142 us -> none  [the longest x1 71.1 us: on_device(): packed = lax.all_to_all(packed, 'gy', 0, 0, tiled=True)]
    all_to_all x0 -> x4, waiting for transfers between devices: none -> 117 us  [the longest x2 61.2 us: on_device(): lines = lax.all_to_all(lines, 'gx', 0, 0, tiled=True)]
    pallas_call x1 -> x6, Pallas kernels: 74.2 us -> 109 us  [the longest x4 87.1 us: filled_spectrum(): pl.pallas_call(fill_kernel, grid_spec=pltpu.PrefetchScalarGridSpec(num_sc...]
    concatenate x3 -> x0, local copies, waits for them, and re-layouts: 21.2 us -> none  [the longest x1 11.5 us: on_device(): with_edge = jnp.concatenate([spectrum, edge[:, :, None]], axis=2)]
    dot_general x8 -> x6, matrix products: 24.9 us -> 6.74 us  [the longest x2 4.01 us: on_device(): jnp.einsum('geaw,gai->eiw', lines[:, :, :2 * count], table_part, precisio...]
    concatenate x4 -> x2, other arithmetic: 21.2 us -> 3.19 us  [the longest x1 2.85 us: halos(): sides = jnp.concatenate([above, sides, below], axis=0)]
    pallas_call x1 -> x0, local copies, waits for them, and re-layouts: 16.5 us -> none  [filled_spectrum(): pl.pallas_call(fill_kernel, grid=(rows // step_rows,), in_specs=[pl.Block...]
    all_to_all x0 -> x4, starting transfers between devices: none -> 15.3 us  [the longest x2 7.88 us: on_device(): lines = lax.all_to_all(lines, 'gx', 0, 0, tiled=True)]
  transfers between devices with their start and end apart: 6 -> 13, of which waited for: 1 -> 4; matrix products, arithmetic and copies ran while one was open for 15% -> 9% of each run, Pallas kernels for 0% -> 15%
where the time goes in v3:
time: 566 us; the launch traced here: 564 us
  blocking collectives  176 us (31%)
  Pallas kernels  170 us (30%)
  waiting for transfers between devices  117 us (21%)
  local copies, waits for them, and re-layouts  34.3 us (6%)
  starting transfers between devices  28.6 us (5%)
  other arithmetic  17.8 us (3%)
  between operations  14 us (2%)
  matrix products  6.74 us (1%)
    pallas_call x4, Pallas kernels, filled_spectrum(): pl.pallas_call(fill_kernel, grid_spec=pltpu.PrefetchScalarGridSpec(num_sc...  87.1 us
    all_gather x1, blocking collectives, on_device(): side = lax.all_gather(side, ('gy', 'gx'), axis=0)  76.1 us
    all_to_all x1, blocking collectives, on_device(): got = lax.all_to_all(messages, 'gx', 0, 0, tiled=True)  64 us
    all_to_all x2, waiting for transfers between devices, on_device(): lines = lax.all_to_all(lines, 'gx', 0, 0, tiled=True)  61.2 us
    all_to_all x2, waiting for transfers between devices, on_device(): packed = lax.all_to_all(packed, 'gy', 0, 0, tiled=True)  56.2 us
    pallas_call x1, Pallas kernels, result_block(): pl.pallas_call(lambda *refs: result_kernel(offsets, own, devices, *refs),...  55.2 us
    all_to_all x1, blocking collectives, on_device(): turned = lax.all_to_all(turned, ('gy', 'gx'), 0, 0, tiled=True)  35.8 us
    pallas_call x2, Pallas kernels, packed_section(): pl.pallas_call(lambda *refs: section_kernel(offsets, closing, *refs), gri...  21.6 us
  transfers between devices with their start and end apart: 13, of which 4 were waited for; matrix products, arithmetic and copies ran while one was open for 9% of the time, Pallas kernels for 15%

profile of v3, /device:TPU:0, one launch (start us, length us, event | category | flops | bytes accessed | tf_op | source)
XLA Modules:
  0.0 564.5 jit_solution(13556052888439486558)
XLA Ops:
  6.5 2.6 fusion.51
  9.6 2.0 collective-permute-start.3
  11.6 2.3 fusion.52
  13.9 5.3 collective-permute-start.1
  21.1 1.3 copy.109
  22.4 1.1 copy.108
  23.5 2.1 fusion.7
  25.6 1.3 fusion.53
  26.9 1.7 bitcast_maximum_fusion
  29.2 0.9 fusion.21
  30.1 0.7 pad_maximum_fusion.3
  30.9 4.8 collective-permute-start.5
  35.7 1.3 copy.113
  37.0 1.4 tile.4
  38.5 1.7 tile.10.marks
  40.1 1.8 copy.114.table_high
  41.9 1.8 copy.115.table_low
  43.7 2.8 select_maximum_fusion.sides
  46.6 0.8 copy-done.1
  47.6 21.7 %shard_map.29 = (f32[16,128,256]{2,1,0:T(8,128)}, f32[16,256]{1,0:T(8,128)}, f32[128,128]{1,0:T(8,128)}) custom-call(s32[1]{0:T(128)} %bitcast.16.base, f32[64,128,512]{2,1,0:T(8,128)} %below.7, f32[64,128,512]{2,1,0:T(8,128)} %below.7, f32[64,128,512]{2,1,0:T(8,128)} %below.7, f32[2,128,512]{2,1,0:T(8,128)} %copy-done.2, f32[2,128,512]{2,1,0:T(8,128)} %copy-done.1, ...), custom_call_target="tpu_custom_call" | custom-call | flops 1610612736 | bytes 41943040 | tf_op jit(solution)/shard_map/pallas_call | solution.py:195
  69.3 0.6 pad_maximum_fusion.4.refs_0_
  69.9 0.9 constant_dynamic-slice_fusion.1
  70.8 0.7 fusion.15
  71.7 21.9 %shard_map.30 = (f32[16,128,256]{2,1,0:T(8,128)}, f32[16,256]{1,0:T(8,128)}, f32[128,128]{1,0:T(8,128)}) custom-call(s32[1]{0:T(128)} %bitcast.19.base, f32[64,128,512]{2,1,0:T(8,128)} %below.7, f32[64,128,512]{2,1,0:T(8,128)} %below.7, f32[64,128,512]{2,1,0:T(8,128)} %below.7, f32[2,128,512]{2,1,0:T(8,128)} %copy-done.2, f32[2,128,512]{2,1,0:T(8,128)} %copy-done.1, ...), custom_call_target="tpu_custom_call" | custom-call | flops 1610612736 | bytes 41943040 | tf_op jit(solution)/shard_map/pallas_call | solution.py:195
  94.1 21.7 %shard_map.28 = (f32[16,128,256]{2,1,0:T(8,128)}, f32[16,256]{1,0:T(8,128)}, f32[128,128]{1,0:T(8,128)}) custom-call(s32[1]{0:T(128)} %bitcast.10.base, f32[64,128,512]{2,1,0:T(8,128)} %below.7, f32[64,128,512]{2,1,0:T(8,128)} %below.7, f32[64,128,512]{2,1,0:T(8,128)} %below.7, f32[2,128,512]{2,1,0:T(8,128)} %copy-done.2, f32[2,128,512]{2,1,0:T(8,128)} %copy-done.1, ...), custom_call_target="tpu_custom_call" | custom-call | flops 1610612736 | bytes 41943040 | tf_op jit(solution)/shard_map/pallas_call | solution.py:195
  115.9 21.7 %shard_map.31 = (f32[16,128,256]{2,1,0:T(8,128)}, f32[16,256]{1,0:T(8,128)}, f32[128,128]{1,0:T(8,128)}) custom-call(s32[1]{0:T(128)} %bitcast.20.base, f32[64,128,512]{2,1,0:T(8,128)} %below.7, f32[64,128,512]{2,1,0:T(8,128)} %below.7, f32[64,128,512]{2,1,0:T(8,128)} %below.7, f32[2,128,512]{2,1,0:T(8,128)} %copy-done.2, f32[2,128,512]{2,1,0:T(8,128)} %copy-done.1, ...), custom_call_target="tpu_custom_call" | custom-call | flops 1610612736 | bytes 41943040 | tf_op jit(solution)/shard_map/pallas_call | solution.py:195
  137.6 1.2 fusion.18
  138.9 0.7 maximum_multiply_fusion.2
  140.3 0.6 broadcast_in_dim.14.refs_8_
  140.9 1.0 fusion.22.refs_7_
  141.9 0.9 broadcast_in_dim.15.refs_9_
  142.8 10.6 %shard_map.32 = (f32[4,16,2,8,640]{4,3,2,1,0:T(8,128)}, f32[4,64,640]{2,1,0:T(8,128)}) custom-call(f32[4,16]{1,0:T(4,128)} %pad_maximum_fusion.4.refs_0_, f32[16,128,256]{2,1,0:T(8,128)} %get-tuple-element.20.refs_1_, f32[16,128,256]{2,1,0:T(8,128)} %collective-permute-done.6.refs_2_, bf16[256,256]{1,0:T(8,128)(2,1)} %get-tuple-element.62.refs_3_, ...), custom_call_target="tpu_custom_call" | custom-call | flops 1610612736 | bytes 31457280 | tf_op jit(solution)/shard_map/pallas_call | solution.py:304
  153.4 3.7 all-to-all-start
  157.1 0.6 pad_maximum_fusion.5.refs_0_
  157.6 10.9 %shard_map.33 = (f32[4,21,2,8,640]{4,3,2,1,0:T(8,128)}, f32[4,64,640]{2,1,0:T(8,128)}) custom-call(f32[4,16]{1,0:T(4,128)} %pad_maximum_fusion.5.refs_0_, f32[16,128,256]{2,1,0:T(8,128)} %get-tuple-element.31.refs_1_, f32[16,128,256]{2,1,0:T(8,128)} %collective-permute-done.7.refs_2_, bf16[256,256]{1,0:T(8,128)(2,1)} %get-tuple-element.62.refs_3_, ...), custom_call_target="tpu_custom_call" | custom-call | flops 1610612736 | bytes 31457280 | tf_op jit(solution)/shard_map/pallas_call | solution.py:304
  168.6 19.7 %all-to-all-done = f32[4,16,2,8,640]{4,3,2,1,0:T(8,128)S(1)} async-done(((f32[4,16,2,8,640]{4,3,2,1,0:T(8,128)}), f32[4,16,2,8,640]{4,3,2,1,0:T(8,128)S(1)}, u32[]{:S(2)}, u32[]{:S(2)}) %all-to-all-start) | async-done | bytes 2621472 | tf_op jit(solution)/shard_map/all_to_all | solution.py:370
  188.3 1.5 copy-done
  189.8 3.7 all-to-all-start.2
  193.6 2.1 bitcast_reduce_fusion.1
  195.7 1.5 copy.122
  197.2 36.5 %all-to-all-done.2 = f32[4,21,2,8,640]{4,3,2,1,0:T(8,128)S(1)} async-done(((f32[4,21,2,8,640]{4,3,2,1,0:T(8,128)}), f32[4,21,2,8,640]{4,3,2,1,0:T(8,128)S(1)}, u32[]{:S(2)}, u32[]{:S(2)}) %all-to-all-start.2) | async-done | bytes 3440672 | tf_op jit(solution)/shard_map/all_to_all | solution.py:370
  233.6 4.3 all-to-all-start.1
  238.5 1.9 copy.124
  240.4 29.0 %all-to-all-done.1 = f32[8,2,32,640]{3,2,1,0:T(8,128)} async-done(((f32[8,2,32,640]{3,2,1,0:T(8,128)}), f32[8,2,32,640]{3,2,1,0:T(8,128)}, u32[]{:S(2)}, u32[]{:S(2)}) %all-to-all-start.1) | async-done | bytes 1310752 | tf_op jit(solution)/shard_map/all_to_all | solution.py:376
  269.4 3.6 all-to-all-start.3
  273.5 3.2 convolution_bitcast_fusion
  276.7 32.2 %all-to-all-done.3 = f32[8,2,37,640]{3,1,2,0:T(2,128)S(1)} async-done(((f32[8,2,37,640]{3,1,2,0:T(2,128)}), f32[8,2,37,640]{3,1,2,0:T(2,128)S(1)}, u32[]{:S(2)}, u32[]{:S(2)}) %all-to-all-start.3) | async-done | bytes 1515552 | tf_op jit(solution)/shard_map/all_to_all | solution.py:376
  309.4 0.8 copy-done.14
  310.2 0.8 fusion.1
  311.1 1.0 copy.150
  312.1 35.8 %all_to_all.30 = f32[32,4,2,2,640]{4,3,2,1,0:T(2,128)S(1)} all-to-all(f32[32,4,2,2,640]{4,3,2,1,0:T(2,128)S(1)} %bitcast.157), channel_id=1, replica_groups=mesh['gx'=8,'gy'=4] {'gy','gx'}, dimensions={0} | all-to-all | bytes 2621440 | tf_op jit(solution)/shard_map/all_to_all | solution.py:387
  347.9 1.5 copy.127
  349.4 5.9 %shard_map.34 = f32[8,5,2,64,128]{4,3,2,1,0:T(8,128)} custom-call(f32[2,256,640]{2,1,0:T(8,128)} %bitcast.153, f32[4,2,64,640]{3,2,1,0:T(8,128)} %bitcast.154), custom_call_target="tpu_custom_call" | custom-call | tf_op jit(solution)/shard_map/pallas_call | solution.py:486
  355.3 64.0 %all_to_all.31 = f32[8,5,2,64,128]{4,3,2,1,0:T(8,128)} all-to-all(f32[8,5,2,64,128]{4,3,2,1,0:T(8,128)} %shard_map.34), channel_id=1, replica_groups=mesh['gx'=8,'gy'=4] {'gx'}, dimensions={0} | all-to-all | bytes 5242880 | tf_op jit(solution)/shard_map/all_to_all | solution.py:405
  419.3 0.6 pad_add_fusion.refs_0_
  419.9 0.7 fusion.16.refs_6_
  420.6 0.7 fusion.26.refs_5_
  421.4 76.1 %all-gather = f32[64,5,640]{2,1,0:T(8,128)S(1)} all-gather(f32[2,5,640]{2,1,0:T(8,128)S(1)} %copy_multiply_fusion), channel_id=2, replica_groups=mesh['gx'=8,'gy'=4] {'gy','gx'}, dimensions={0}, use_global_device_ids=true | all-gather | bytes 844800 | tf_op jit(solution)/shard_map/all_gather | solution.py:382
  499.1 0.7 gather_fusion
  499.8 0.6 slice.336.refs_3_
  500.5 0.6 gather_fusion.1
  501.1 0.6 pad.14.refs_4_
  501.8 0.7 dynamic-slice_bitcast_fusion.refs_2_
  502.4 55.2 %shard_map.35 = f32[64,128,512]{2,1,0:T(8,128)} custom-call(s32[3]{0:T(128)} %pad_add_fusion.refs_0_, f32[20480,128]{1,0:T(8,128)} %bitcast.148, f32[64,640]{1,0:T(8,128)} %dynamic-slice_bitcast_fusion.refs_2_, f32[64,256]{1,0:T(8,128)} %slice.336.refs_3_, f32[128,128]{1,0:T(8,128)} %pad.14.refs_4_, bf16[128,256]{1,0:T(8,128)(2,1)} %fusion.26.refs_5_, ...), custom_call_target="tpu_custom_call" | custom-call | tf_op jit(solution)/shard_map/pallas_call | solution.py:557
  (107 shorter events, 7.7 us)
Async XLA Ops:
  6.5 12.7 %slice-start.1 = ((s32[32,32,32]{2,1,0:T(8,128)}), s32[31,32,32]{2,1,0:T(8,128)S(1)}, s32[]{:S(2)}) async-start(s32[32,32,32]{2,1,0:T(8,128)} %param.3), calls=%async_computation.8 | async-start | bytes 1015808 | tf_op jit(solution)/shard_map/jit(_roll_static)/slice | solution.py:40
  9.2 20.9 %collective-permute-start.2 = (f32[64,2,512]{2,1,0:T(2,128)}, f32[64,2,512]{2,1,0:T(2,128)S(1)}, u32[]{:S(2)}, u32[]{:S(2)}) collective-permute-start(f32[64,2,512]{2,1,0:T(2,128)} %get-tuple-element.35), channel_id=1, source_target_pairs={{0,1},{1,2},{2,3},{3,0},{4,5},{5,6},{6,7},{7,4},{8,9},{9,10},{10,1... | collective-permute-start | bytes 786440 | tf_op jit(solution)/shard_map/ppermute | solution.py:29
  9.6 9.6 %copy-start.6 = (s32[32,32,32]{2,1,0:T(8,128)S(1)}, s32[32,32,32]{2,1,0:T(8,128)}, u32[]{:S(2)}) copy-start(s32[32,32,32]{2,1,0:T(8,128)} %param.3) | copy-start | bytes 393220
  9.6 9.6 %slice-start = ((s32[32,32,32]{2,1,0:T(8,128)}), s32[1,32,32]{2,1,0:T(8,128)S(1)}, s32[]{:S(2)}) async-start(s32[32,32,32]{2,1,0:T(8,128)} %param.3), calls=%async_computation.7 | async-start | bytes 32768 | tf_op jit(solution)/shard_map/jit(_roll_static)/slice | solution.py:40
  9.6 20.4 %collective-permute-start.3 = (f32[64,2,512]{2,1,0:T(2,128)}, f32[64,2,512]{2,1,0:T(2,128)}, u32[]{:S(2)}, u32[]{:S(2)}) collective-permute-start(f32[64,2,512]{2,1,0:T(2,128)} %get-tuple-element.36), channel_id=1, source_target_pairs={{1,0},{2,1},{3,2},{0,3},{5,4},{6,5},{7,6},{4,7},{9,8},{10,9},{11,1... | collective-permute-start | bytes 786440 | tf_op jit(solution)/shard_map/ppermute | solution.py:30
  13.9 32.7 %collective-permute-start.1 = (f32[2,128,512]{2,1,0:T(8,128)}, f32[2,128,512]{2,1,0:T(8,128)S(1)}, u32[]{:S(2)}, u32[]{:S(2)}) collective-permute-start(f32[2,128,512]{2,1,0:T(8,128)} %get-tuple-element.37), channel_id=1, source_target_pairs={{4,0},{8,4},{12,8},{16,12},{20,16},{24,20},{28,24},{0,28},{5,1},{9... | collective-permute-start | bytes 1572872 | tf_op jit(solution)/shard_map/ppermute | solution.py:28
  19.2 27.4 %collective-permute-start = (f32[2,128,512]{2,1,0:T(8,128)}, f32[2,128,512]{2,1,0:T(8,128)S(1)}, u32[]{:S(2)}, u32[]{:S(2)}) collective-permute-start(f32[2,128,512]{2,1,0:T(8,128)} %get-tuple-element.38), channel_id=1, source_target_pairs={{0,4},{4,8},{8,12},{12,16},{16,20},{20,24},{24,28},{28,0},{1,5},{5... | collective-permute-start | bytes 1572872 | tf_op jit(solution)/shard_map/ppermute | solution.py:27
  25.5 10.1 %copy-start.3 = (f32[512,257]{0,1:T(8,128)}, f32[512,257]{0,1:T(8,128)S(1)}, u32[]{:S(2)}) copy-start(f32[512,257]{0,1:T(8,128)S(1)} %fusion.7) | copy-start | bytes 1579012
  30.8 12.9 %collective-permute-start.4 = (f32[2,4,512]{2,1,0:T(4,128)S(1)}, f32[2,4,512]{2,1,0:T(4,128)S(1)}, u32[]{:S(2)}, u32[]{:S(2)}) collective-permute-start(f32[2,4,512]{2,1,0:T(4,128)S(1)} %get-tuple-element.59), channel_id=1, source_target_pairs={{0,4},{4,8},{8,12},{12,16},{16,20},{20,24},{24,28},{28,0},{1,5},{5... | collective-permute-start | bytes 49160 | tf_op jit(solution)/shard_map/ppermute | solution.py:32
  30.9 12.9 %collective-permute-start.5 = (f32[2,4,512]{2,1,0:T(4,128)S(1)}, f32[2,4,512]{2,1,0:T(4,128)S(1)}, u32[]{:S(2)}, u32[]{:S(2)}) collective-permute-start(f32[2,4,512]{2,1,0:T(4,128)S(1)} %get-tuple-element.60), channel_id=1, source_target_pairs={{4,0},{8,4},{12,8},{16,12},{20,16},{24,20},{28,24},{0,28},{5,1},{9... | collective-permute-start | bytes 49160 | tf_op jit(solution)/shard_map/ppermute | solution.py:33
  46.6 0.8 copy-start.1
  46.6 1.0 copy-start.2
  47.6 22.3 %copy-start.4 = (f32[512,257]{0,1:T(8,128)S(1)}, f32[512,257]{0,1:T(8,128)}, u32[]{:S(2)}) copy-start(f32[512,257]{0,1:T(8,128)} %copy-done.3) | copy-start | bytes 1579012
  69.3 72.6 %collective-permute-start.6 = (f32[16,128,256]{2,1,0:T(8,128)}, f32[16,128,256]{2,1,0:T(8,128)}, u32[]{:S(2)}, u32[]{:S(2)}) collective-permute-start(f32[16,128,256]{2,1,0:T(8,128)} %get-tuple-element.21), channel_id=1, source_target_pairs={{0,1},{1,0},{2,3},{3,2},{4,5},{5,4},{6,7},{7,6},{8,9},{9,8},{10,11... | collective-permute-start | bytes 6291464 | tf_op jit(solution)/shard_map/ppermute | solution.py:342
  93.6 64.0 %collective-permute-start.7 = (f32[16,128,256]{2,1,0:T(8,128)}, f32[16,128,256]{2,1,0:T(8,128)}, u32[]{:S(2)}, u32[]{:S(2)}) collective-permute-start(f32[16,128,256]{2,1,0:T(8,128)} %get-tuple-element.32), channel_id=1, source_target_pairs={{0,1},{1,0},{2,3},{3,2},{4,5},{5,4},{6,7},{7,6},{8,9},{9,8},{10,11... | collective-permute-start | bytes 6291464 | tf_op jit(solution)/shard_map/ppermute | solution.py:342
  115.8 21.8 %copy-start.8 = (f32[128,128]{1,0:T(8,128)S(1)}, f32[128,128]{1,0:T(8,128)}, u32[]{:S(2)}) copy-start(f32[128,128]{1,0:T(8,128)} %get-tuple-element.22) | copy-start | bytes 196612
  115.8 21.8 %copy-start.9 = (f32[128,128]{1,0:T(8,128)S(1)}, f32[128,128]{1,0:T(8,128)}, u32[]{:S(2)}) copy-start(f32[128,128]{1,0:T(8,128)} %get-tuple-element.23) | copy-start | bytes 196612
  115.8 21.8 %copy-start.10 = (f32[128,128]{1,0:T(8,128)S(1)}, f32[128,128]{1,0:T(8,128)}, u32[]{:S(2)}) copy-start(f32[128,128]{1,0:T(8,128)} %get-tuple-element.24) | copy-start | bytes 196612
  115.9 23.0 %copy-start.11 = (f32[16,256]{1,0:T(8,128)S(1)}, f32[16,256]{1,0:T(8,128)}, u32[]{:S(2)}) copy-start(f32[16,256]{1,0:T(8,128)} %get-tuple-element.26) | copy-start | bytes 49156
  115.9 23.0 %copy-start.12 = (f32[16,256]{1,0:T(8,128)S(1)}, f32[16,256]{1,0:T(8,128)}, u32[]{:S(2)}) copy-start(f32[16,256]{1,0:T(8,128)} %get-tuple-element.27) | copy-start | bytes 49156
  115.9 23.0 %copy-start.13 = (f32[16,256]{1,0:T(8,128)S(1)}, f32[16,256]{1,0:T(8,128)}, u32[]{:S(2)}) copy-start(f32[16,256]{1,0:T(8,128)} %get-tuple-element.28) | copy-start | bytes 49156
  153.4 34.9 %all-to-all-start = ((f32[4,16,2,8,640]{4,3,2,1,0:T(8,128)}), f32[4,16,2,8,640]{4,3,2,1,0:T(8,128)S(1)}, u32[]{:S(2)}, u32[]{:S(2)}) async-start(f32[4,16,2,8,640]{4,3,2,1,0:T(8,128)} %get-tuple-element.30), calls=%async_computation | async-start | bytes 5242880 | tf_op jit(solution)/shard_map/all_to_all | solution.py:370
  188.3 1.5 copy-start
  189.8 43.8 %all-to-all-start.2 = ((f32[4,21,2,8,640]{4,3,2,1,0:T(8,128)}), f32[4,21,2,8,640]{4,3,2,1,0:T(8,128)S(1)}, u32[]{:S(2)}, u32[]{:S(2)}) async-start(f32[4,21,2,8,640]{4,3,2,1,0:T(8,128)} %get-tuple-element.34), calls=%async_computation.2 | async-start | bytes 6881280 | tf_op jit(solution)/shard_map/all_to_all | solution.py:370
  233.6 35.7 %all-to-all-start.1 = ((f32[8,2,32,640]{3,2,1,0:T(8,128)}), f32[8,2,32,640]{3,2,1,0:T(8,128)}, u32[]{:S(2)}, u32[]{:S(2)}) async-start(f32[8,2,32,640]{3,2,1,0:T(8,128)} %copy.122), calls=%async_computation.1 | async-start | bytes 2621440 | tf_op jit(solution)/shard_map/all_to_all | solution.py:376
  240.4 32.9 %copy-start.7 = (f32[512,256]{0,1:T(8,128)S(1)}, f32[512,256]{0,1:T(8,128)}, u32[]{:S(2)}) copy-start(f32[512,256]{0,1:T(8,128)} %get-tuple-element.54) | copy-start | bytes 1572868
  269.4 39.6 %all-to-all-start.3 = ((f32[8,2,37,640]{3,1,2,0:T(2,128)}), f32[8,2,37,640]{3,1,2,0:T(2,128)S(1)}, u32[]{:S(2)}, u32[]{:S(2)}) async-start(f32[8,2,37,640]{3,1,2,0:T(2,128)} %copy.124), calls=%async_computation.3 | async-start | bytes 3031040 | tf_op jit(solution)/shard_map/all_to_all | solution.py:376
  273.0 229.5 %all-gather.3.cloned.1.call-start = ((), (), s32[]{:S(2)}) async-start(), calls=%async_computation.6 | async-start | bytes 13107200 | tf_op jit(solution)/shard_map/all_gather | solution.py:406
  308.9 1.3 copy-start.14
  311.1 36.8 %copy-start.5 = (f32[256,2,640]{2,0,1:T(8,128)}, f32[256,2,640]{2,0,1:T(8,128)S(1)}, u32[]{:S(2)}) copy-start(f32[256,2,640]{2,0,1:T(8,128)S(1)} %fusion.1) | copy-start | bytes 3932164
Sparse Core Ops, SparseCore 0:
  419.4 68.8 all-gather.2

commit v4 on v3

--- a/solution.py
+++ b/solution.py
@@ -70,17 +70,19 @@
 
 def fill_kernel(
     base, here, above, below, top, bottom, sides, marks, table_high, table_low,
-    spectrum, alternate, edge, punched, once, high, low,
+    spectrum, alternate, edge, punched, once, high, low, folded,
 ):
     step_rows, cols, length = here.shape
     step = pl.program_id(0) + base[0]
     first_row = step * step_rows
     local_row = pl.program_id(0) * step_rows
     period = marks.shape[0]
-    lane = lax.broadcasted_iota(jnp.int32, (CHUNK, edge.shape[1]), 1)
-    place = lax.broadcasted_iota(jnp.int32, (CHUNK, length), 1)
-    signs = jnp.where(place % 2 == 0, 1.0, -1.0).astype(jnp.float32)
-    inner = pl.ds(8 - SWEEPS, 2 * SWEEPS)
+    lane = lax.broadcasted_iota(jnp.int32, (128, 128), 1)
+    signs = jnp.where(lax.broadcasted_iota(jnp.int32, (128, 128), 0) % 2 == 0, 1.0, -1.0)
+
+    @pl.when(pl.program_id(0) == 0)
+    def _():
+        edge[...] = jnp.zeros_like(edge)
 
     def holes(row, start, size):
         row = lax.rem(first_row + row, period)
@@ -130,7 +132,7 @@
     def _(r):
         punch_row(r + SWEEPS, here, r)
 
-    @pl.loop(1, step_rows + 2 * SWEEPS - 1)
+    @pl.loop(1, step_rows + 2 * SWEEPS - 1, unroll=2)
     def _(r):
         for start in range(MARGIN - 8, MARGIN + cols + 8, CHUNK):
             total = neighbours(punched, r, start) * holes(r, start, CHUNK)
@@ -146,9 +148,15 @@
             spot = pl.ds(pl.multiple_of(r * cols + c, CHUNK), CHUNK)
             high[spot, :] = first
             low[spot, :] = second
-            signed = jnp.sum(filled * signs, axis=1, keepdims=True)
-            old = edge[pl.ds(c, CHUNK), :]
-            edge[pl.ds(c, CHUNK), :] = jnp.where(lane == local_row + r, signed, old)
+            wrapped = filled[:, :128]
+            for tile in range(1, length // 128):
+                wrapped += filled[:, tile * 128 : (tile + 1) * 128]
+            folded[pl.ds(c, CHUNK), :] = wrapped
+        column = jnp.where(lane == local_row + r, signs, 0.0).astype(jnp.bfloat16)
+        first, second = split(folded[...])
+        total = jnp.dot(first, column, preferred_element_type=jnp.float32)
+        total += jnp.dot(second, column, preferred_element_type=jnp.float32)
+        edge[...] += total
 
     rows_each = 8
     half = spectrum.shape[2]
@@ -212,6 +220,7 @@
                 pltpu.VMEM(padded, jnp.float32),
                 pltpu.VMEM((step_rows * cols, length), jnp.bfloat16),
                 pltpu.VMEM((step_rows * cols, length), jnp.bfloat16),
+                pltpu.VMEM((cols, 128), jnp.float32),
             ],
         ),
         out_shape=[
@@ -241,7 +250,7 @@
 
 
 def section_kernel(
-    offsets, closing, weights, kept, got, cols_high, cols_low, rows_high, rows_low,
+    offsets, closing, me, weights, kept, got, cols_high, cols_low, rows_high, rows_low,
     rim, corner, before, out, total, lines,
 ):
     step, steps = pl.program_id(0), pl.num_programs(0)
@@ -254,13 +263,13 @@
         for e in range(own):
             for q in range(gy):
                 start = (e * gy + q) * gx
-                out[q, layer, e] = values[start : start + gx]
+                out[q ^ me[0], layer, e] = values[start : start + gx]
 
     @pl.when(step == 0)
     def _():
         total[...] = before[...]
 
-    @pl.loop(0, step_rows)
+    @pl.loop(0, step_rows, unroll=True)
     def _(r):
         layer = step * step_rows + r
         values = jnp.concatenate([kept[r], got[r]], axis=0)
@@ -286,7 +295,7 @@
             place(count + planes, jnp.zeros((block, width), jnp.float32) + corner[...])
 
 
-def packed_section(kept, got, table_pair, table_rows, marks, rim, corner, before, offsets, shape, closing):
+def packed_section(col, kept, got, table_pair, table_rows, marks, rim, corner, before, offsets, shape, closing):
     count, cols, half = kept.shape
     planes, block, width = before.shape
     gx, gy = shape
@@ -304,7 +313,7 @@
     return pl.pallas_call(
         lambda *refs: section_kernel(offsets, closing, *refs),
         grid=(count // step_rows,),
-        in_specs=[pl.BlockSpec(memory_space=pltpu.SMEM), rows_spec, rows_spec]
+        in_specs=[pl.BlockSpec(memory_space=pltpu.SMEM)] * 2 + [rows_spec, rows_spec]
         + [whole(array) for array in arrays],
         out_specs=[whole(out) for out in outs],
         out_shape=outs,
@@ -315,7 +324,7 @@
             bytes_accessed=count * cols * half * 60,
             transcendentals=0,
         ),
-    )(weights, kept, got, *arrays)
+    )(col.reshape(1), weights, kept, got, *arrays)
 
 
 def on_device(intensity, template):
@@ -337,55 +346,57 @@
     arrays = fill_arrays(intensity, template, row, col, main)
     given_first, kept_first = (1 - core) * pair_rows, core * pair_rows
     given, kept, got = [], [], []
-    for c in range(parts):
-        given.append(filled_spectrum(intensity, arrays, given_first + c * count, count))
-        got.append(lax.ppermute(given[c][0], "gy", [(q, q ^ 1) for q in range(gy)]))
-        kept.append(filled_spectrum(intensity, arrays, kept_first + c * count, count))
+
+    def fill_part(c, after):
+        starts = given_first + c * count, kept_first + c * count
+        if after is not None:
+            starts, after = lax.optimization_barrier((starts, after))
+        given.append(filled_spectrum(intensity, arrays, starts[0], count))
+        got.append(lax.ppermute(given[c][0], "gy", swap(gy, 1)))
+        kept.append(filled_spectrum(intensity, arrays, starts[1], count))
+        return after
 
     table_cols = lax.dynamic_slice_in_dim(table, col * cols, cols, 0)
-    given_rows = lax.dynamic_slice_in_dim(table, row * rows + given_first, pair_rows, 0)
     kept_rows = lax.dynamic_slice_in_dim(table, row * rows + kept_first, pair_rows, 0)
-    ordered_rows = jnp.concatenate([given_rows, kept_rows], axis=0)
-    alternate = jnp.concatenate([piece[1] for piece in given + kept], axis=0) / math.sqrt(length)
-    edge = jnp.concatenate([piece[2][:, :count] for piece in given + kept], axis=1)
-    edge = jnp.einsum("ba,bk->ak", edge / math.sqrt(length), table_cols, precision=HIGH)
-    edge = edge + jnp.concatenate([alternate, edge[:, half:]], axis=1)
-    rim = jnp.einsum("aj,ak->jk", ordered_rows[:, :half], edge[:, :half], precision=HIGH)
-    corner = 2.0 * jnp.einsum("a,ak->k", ordered_rows[:, half], edge, precision=HIGH)
-    corner = corner + jnp.einsum("aj,a->j", ordered_rows, edge[:, half], precision=HIGH)
-    corner = jnp.pad(corner, (0, width - half - 1))
-
     marks = [rows * (m + 1) for m in range(slabs)]
     mates = lax.dynamic_slice_in_dim(main, (col + 1 - 2 * core) * cols, cols, 0)
     table_pair = jnp.concatenate([table_cols[:, :half], mates], axis=0)
     table_parts = main.reshape(gx, 2, parts, count, half) / 6.0
+    table_parts = jnp.where(core == 0, table_parts, table_parts[:, ::-1])
     side = jnp.zeros((slabs, block, width), jnp.float32)
-    values = 0.0
+    rim, corner = jnp.zeros((half, half), jnp.float32), jnp.zeros((width,), jnp.float32)
+    values, packed = 0.0, None
     for c in range(parts):
         closing = c == parts - 1
+        packed = fill_part(c, packed)
+        if c > 0:
+            values = values + first_axis(packed, count, table_parts[:, :, c - 1])[0]
+        if closing:
+            given_rows = lax.dynamic_slice_in_dim(table, row * rows + given_first, pair_rows, 0)
+            ordered_rows = jnp.concatenate([given_rows, kept_rows], axis=0)
+            alternate = jnp.concatenate([piece[1] for piece in given + kept], axis=0) / math.sqrt(length)
+            edge = jnp.concatenate([piece[2][:, :count] for piece in given + kept], axis=1)
+            edge = jnp.einsum("ba,bk->ak", edge / math.sqrt(length), table_cols, precision=HIGH)
+            edge = edge + jnp.concatenate([alternate, edge[:, half:]], axis=1)
+            rim = jnp.einsum("aj,ak->jk", ordered_rows[:, :half], edge[:, :half], precision=HIGH)
+            corner = 2.0 * jnp.einsum("a,ak->k", ordered_rows[:, half], edge, precision=HIGH)
+            corner = corner + jnp.einsum("aj,a->j", ordered_rows, edge[:, half], precision=HIGH)
+            corner = jnp.pad(corner, (0, width - half - 1))
+
         packed, side = packed_section(
-            kept[c][0], got[c], table_pair, kept_rows[c * count : (c + 1) * count], marks,
+            col, kept[c][0], got[c], table_pair, kept_rows[c * count : (c + 1) * count], marks,
             rim, corner, side, offsets, (gx, gy), closing,
         )
-        packed = lax.all_to_all(packed, "gy", 0, 0, tiled=True)
-        lines = packed[:, :count].reshape(gy // 2, 2 * count, own, gx, width)
-        lines = jnp.sum(lines, axis=0)
-        if closing:
-            lines = jnp.concatenate([lines, jnp.sum(packed[:, count:], axis=0)], axis=0)
-        lines = jnp.transpose(lines, (2, 1, 0, 3))
-        lines = lax.all_to_all(lines, "gx", 0, 0, tiled=True)
-        table_part = table_parts[:, :, c].reshape(gx, 2 * count, half)
-        values = values + jnp.einsum(
-            "geaw,gai->eiw", lines[:, :, : 2 * count], table_part, precision=HIGH
-        )
-    side = jnp.sum(lines[:, :, 2 * count :], axis=0) / 6.0
+    last_values, side = first_axis(packed, count, table_parts[:, :, parts - 1])
+    values = values + last_values
     side = lax.all_gather(side, ("gy", "gx"), axis=0)
     side = jnp.transpose(side, (2, 1, 0, 3)).reshape(slabs + 1, block, width)
 
     turned = values.reshape(own, blocks, own, devices, width)
     turned = jnp.transpose(turned, (3, 1, 2, 0, 4))
-    turned = lax.all_to_all(turned, ("gy", "gx"), 0, 0, tiled=True)
-    turned = jnp.transpose(turned, (1, 2, 3, 0, 4)).reshape(blocks, own, block, width)
+    turned = [turned[:, b, :, :, : offsets[b + 1]] for b in range(blocks)]
+    turned = lax.all_to_all(jnp.concatenate(turned, axis=3), ("gy", "gx"), 0, 0, tiled=True)
+    turned = jnp.transpose(turned, (1, 2, 0, 3)).reshape(own, block, -1)
 
     slab = jnp.minimum(row, gx - 1 - row)
     far_row, far_col = row >= slabs, col >= gy // 2
@@ -402,12 +413,14 @@
 
     if rows == block:
         messages = slab_messages(values, turned, offsets, slabs)
-        got = lax.all_to_all(messages, "gx", 0, 0, tiled=True)
-        got = lax.all_gather(got, "gy", axis=0, tiled=True)
+        got = []
+        for group in tile_groups(messages.shape[1]):
+            piece = lax.all_to_all(messages[:, group], "gx", 0, 0, tiled=True)
+            got.append(gathered(piece, gy))
         rim_col = col == gy // 2
         rim = across[:, pick_cols]
         return result_block(
-            got, next_plane, across, rim, pick_cols, slab, far_row, rim_col, offsets
+            got, next_plane, across, rim, pick_cols, slab, far_row, rim_col, col, offsets
         )
 
     sums = axis_order_sums(values, turned, offsets, block)
@@ -446,15 +459,17 @@
 
 
 def axis_order_sums(values, turned, offsets, block):
+    start = 0
     sums = []
     for top in range(len(offsets) - 1):
         size = (top + 1) * block
         parts = []
         for e in range(values.shape[0]):
             part = values[e, :size, offsets[top] : offsets[top] + size]
-            lower = [turned[top, e, :, offsets[b] : offsets[b + 1]] for b in range(top + 1)]
+            lower = [turned[e, :, start + offsets[b] : start + offsets[b + 1]] for b in range(top + 1)]
             parts.append(part + part.T + square(lower, block))
         sums.append(parts)
+        start += offsets[top + 1]
     return sums
 
 
@@ -493,20 +508,36 @@
 
 
 def result_kernel(
-    offsets, own, devices, places, got, next_plane, across, rim, pick, flip, out
+    offsets, own, devices, groups, places, next_plane, across, rim, pick, flip, *refs
 ):
     blocks, block = len(offsets) - 1, offsets[1]
     tiles = offsets[-1] // 128
-    stride = tiles * own * block
+    peers = (len(refs) - 2) // len(groups) - 1
+    pieces, out = refs[: peers * len(groups)], refs[peers * len(groups)]
+    held, sems = refs[peers * len(groups) + 1 : -1], refs[-1]
     step_rows, cols, length = out.shape
     half = length // 2
-    slab, far_row, rim_col = places[0], places[1], places[2]
+    slab, far_row, rim_col, me = places[0], places[1], places[2], places[3]
     lane = lax.broadcasted_iota(jnp.int32, (block, 128), 1)
     at_rim = lax.broadcasted_iota(jnp.int32, (cols, half), 0) + (1 - rim_col) == 0
     rim_lane = lax.broadcasted_iota(jnp.int32, rim.shape, 1)
     first_lane = lax.broadcasted_iota(jnp.int32, (cols, half), 1) == 0
 
-    @pl.loop(0, step_rows)
+    @pl.when(pl.program_id(0) == 0)
+    def _():
+        copies = []
+        for g in range(len(groups)):
+            for peer in range(peers):
+                piece = pieces[g * peers + peer]
+                size = piece.shape[0]
+                spot = pl.ds(pl.multiple_of((me ^ peer) * size, size), size)
+                copies.append(pltpu.make_async_copy(piece, held[g].at[spot], sems.at[g, peer]))
+        for copy in copies:
+            copy.start()
+        for copy in copies:
+            copy.wait()
+
+    @pl.loop(0, step_rows, unroll=4)
     def _(r):
         t = pl.program_id(0) * step_rows + r
         i = jnp.where(far_row == 1, block - t, t)
@@ -514,20 +545,23 @@
         i = jnp.minimum(i, block - 1)
         source = lax.div(i, devices), lax.rem(i, devices)
         parts = []
-        for tile in range(tiles):
-            start = tile * own * block
-            near = [
-                got[pl.ds(start + e * block + i, devices, stride=stride), :] for e in range(own)
-            ]
-            near = jnp.concatenate(near, axis=0)
-            far = pl.multiple_of(source[1] * stride + start + source[0] * block, block)
-            far = got[pl.ds(far, block), :]
-            kind = jnp.zeros((block, 128), jnp.int32)
-            for b in range(1, blocks):
-                kind += (lane + tile * 128 >= offsets[b]).astype(jnp.int32)
-            line = jnp.where(kind >= slab, near, far)
-            line = jnp.where(inside, line, next_plane[:, pl.ds(tile * 128, 128)])
-            parts.append(line)
+        for g, group in enumerate(groups):
+            stride = (group.stop - group.start) * own * block
+            for tile in range(group.start, group.stop):
+                start = (tile - group.start) * own * block
+                near = [
+                    held[g][pl.ds(start + e * block + i, devices, stride=stride), :]
+                    for e in range(own)
+                ]
+                near = jnp.concatenate(near, axis=0)
+                far = pl.multiple_of(source[1] * stride + start + source[0] * block, block)
+                far = held[g][pl.ds(far, block), :]
+                kind = jnp.zeros((block, 128), jnp.int32)
+                for b in range(1, blocks):
+                    kind += (lane + tile * 128 >= offsets[b]).astype(jnp.int32)
+                line = jnp.where(kind >= slab, near, far)
+                line = jnp.where(inside, line, next_plane[:, pl.ds(tile * 128, 128)])
+                parts.append(line)
         line = jnp.concatenate(parts, axis=1)
         plane = square([line[:, offsets[b] : offsets[b + 1]] for b in range(blocks)], block)
         high, low = split(plane)
@@ -542,26 +576,65 @@
         out[r, :, pl.ds(half, half)] = jnp.where(first_lane, edge, right)
 
 
-def result_block(got, next_plane, across, rim, pick_cols, slab, far_row, rim_col, offsets):
-    devices, tiles, own, block, _ = got.shape
+def result_block(got, next_plane, across, rim, pick_cols, slab, far_row, rim_col, col, offsets):
+    gx, _, own, block, _ = got[0][0].shape
+    groups = tile_groups(offsets[-1] // 128)
+    devices = gx * len(got[0])
     rows, half = across.shape[0], across.shape[1] - 1
     cols = pick_cols.shape[0]
     step_rows = 8
-    places = jnp.stack([slab, far_row.astype(jnp.int32), rim_col.astype(jnp.int32)])
+    places = jnp.stack([slab, far_row.astype(jnp.int32), rim_col.astype(jnp.int32), col])
     cell = jnp.arange(half)
     pick = (pick_cols[:, None] == cell[None, :]).astype(jnp.bfloat16)
     flip = (cell[:, None] + cell[None, :] == half).astype(jnp.bfloat16)
     rim = jnp.pad(rim.T, ((0, 0), (0, 128 - rows)))
     whole = lambda array: pl.BlockSpec(array.shape, lambda i: (0,) * array.ndim)
-    arrays = (got.reshape(-1, 128), next_plane, across[:, :half], rim, pick, flip)
+    arrays = (next_plane, across[:, :half], rim, pick, flip)
+    pieces = [piece.reshape(-1, 128) for group in got for piece in group]
     return pl.pallas_call(
-        lambda *refs: result_kernel(offsets, own, devices, *refs),
+        lambda *refs: result_kernel(offsets, own, devices, groups, *refs),
         grid=(rows // step_rows,),
-        in_specs=[pl.BlockSpec(memory_space=pltpu.SMEM)] + [whole(array) for array in arrays],
+        in_specs=[pl.BlockSpec(memory_space=pltpu.SMEM)] + [whole(array) for array in arrays]
+        + [pl.BlockSpec(memory_space=pl.ANY)] * len(pieces),
         out_specs=pl.BlockSpec((step_rows, cols, 2 * half), lambda i: (i, 0, 0)),
         out_shape=jax.ShapeDtypeStruct((rows, cols, 2 * half), jnp.float32),
+        scratch_shapes=[
+            pltpu.VMEM((devices * (group.stop - group.start) * own * block, 128), jnp.float32)
+            for group in groups
+        ] + [pltpu.SemaphoreType.DMA((len(groups), len(got[0])))],
         compiler_params=pltpu.CompilerParams(vmem_limit_bytes=VMEM_BYTES),
-    )(places, *arrays)
+    )(places, *arrays, *pieces)
+
+
+def tile_groups(tiles):
+    middle = (tiles + 1) // 2
+    return [slice(0, middle), slice(middle, tiles)]
+
+
+def swap(peers, bit):
+    return [(q, q ^ bit) for q in range(peers)]
+
+
+def gathered(piece, peers):
+    pieces, bit = {0: piece}, peers // 2
+    while bit:
+        for place in list(pieces):
+            pieces[place ^ bit] = lax.ppermute(pieces[place], "gy", swap(peers, bit))
+        bit //= 2
+    return [pieces[place] for place in range(peers)]
+
+
+def first_axis(packed, count, table):
+    gy, _, own, gx, width = packed.shape
+    half = table.shape[-1]
+    got = [packed[0]] + [lax.ppermute(packed[p], "gy", swap(gy, p)) for p in range(1, gy)]
+    lines = [sum(got[p][:count] for p in range(first, gy, 2)) for first in range(2)]
+    lines = jnp.concatenate(lines + [sum(piece[count:] for piece in got)], axis=0)
+    lines = jnp.transpose(lines, (2, 1, 0, 3))
+    lines = lax.all_to_all(lines, "gx", 0, 0, tiled=True)
+    table = table.reshape(gx, 2 * count, half)
+    values = jnp.einsum("geaw,gai->eiw", lines[:, :, : 2 * count], table, precision=HIGH)
+    return values, jnp.sum(lines[:, :, 2 * count :], axis=0) / 6.0
 
 
 def square(lower, block):

time: 566 us -> 500 us (0.88)
  blocking collectives: 176 us -> 108 us
  Pallas kernels: 170 us -> 123 us
  waiting for transfers between devices: 117 us -> 147 us
  local copies, waits for them, and re-layouts: 34.3 us -> 51.5 us
  between operations: 14 us -> 0.94 us
  starting transfers between devices: 28.6 us -> 38 us
    ppermute x2 -> x14, waiting for transfers between devices: 0.01 us -> 82.1 us  [the longest x6 65.5 us: first_axis(): lax.ppermute(packed[p], 'gy', swap(gy, p))]
    all_to_all x2 -> x1, blocking collectives: 99.8 us -> 22.4 us  [on_device(): lax.all_to_all(jnp.concatenate(turned, axis=3), ('gy', 'gx'), 0, 0, tiled...]
    all_to_all x4, waiting for transfers between devices: 117 us -> 65.4 us  [the longest x2 34.7 us: on_device(): piece = lax.all_to_all(messages[:, group], 'gx', 0, 0, tiled=True)]
    pallas_call x4, Pallas kernels: 87.1 us -> 65.8 us  [filled_spectrum(): pl.pallas_call(fill_kernel, grid_spec=pltpu.PrefetchScalarGridSpec(num_sc...]
    pallas_call x1, Pallas kernels: 55.2 us -> 35.6 us  [result_block(): pl.pallas_call(lambda *refs: result_kernel(offsets, own, devices, groups,...]
    all_gather x1, blocking collectives: 76.1 us -> 85.7 us  [on_device(): side = lax.all_gather(side, ('gy', 'gx'), axis=0)]
    ppermute x2 -> x14, starting transfers between devices: 0.51 us -> 6.9 us  [the longest x6 4.42 us: first_axis(): lax.ppermute(packed[p], 'gy', swap(gy, p))]
    slice x4 -> x6, local copies, waits for them, and re-layouts: 1.36 us -> 7.25 us  [the longest x2 5.08 us: on_device(): piece = lax.all_to_all(messages[:, group], 'gx', 0, 0, tiled=True)]
  transfers between devices with their start and end apart: 13 -> 24, of which waited for: 4 -> 9; matrix products, arithmetic and copies ran while one was open for 9% -> 12% of each run, Pallas kernels for 15% -> 7%
where the time goes in v4:
time: 500 us; the launch traced here: 498 us
  waiting for transfers between devices  147 us (29%)
  Pallas kernels  123 us (25%)
  blocking collectives  108 us (22%)
  local copies, waits for them, and re-layouts  51.5 us (10%)
  starting transfers between devices  38 us (8%)
  other arithmetic  21.9 us (4%)
  matrix products  7.15 us (1%)
    all_gather x1, blocking collectives, on_device(): side = lax.all_gather(side, ('gy', 'gx'), axis=0)  85.7 us
    pallas_call x4, Pallas kernels, filled_spectrum(): pl.pallas_call(fill_kernel, grid_spec=pltpu.PrefetchScalarGridSpec(num_sc...  65.8 us
    ppermute x6, waiting for transfers between devices, first_axis(): lax.ppermute(packed[p], 'gy', swap(gy, p))  65.5 us
    pallas_call x1, Pallas kernels, result_block(): pl.pallas_call(lambda *refs: result_kernel(offsets, own, devices, groups,...  35.6 us
    all_to_all x2, waiting for transfers between devices, on_device(): piece = lax.all_to_all(messages[:, group], 'gx', 0, 0, tiled=True)  34.7 us
    all_to_all x2, waiting for transfers between devices, first_axis(): lines = lax.all_to_all(lines, 'gx', 0, 0, tiled=True)  30.7 us
    all_to_all x1, blocking collectives, on_device(): lax.all_to_all(jnp.concatenate(turned, axis=3), ('gy', 'gx'), 0, 0, tiled...  22.4 us
    ppermute x6, waiting for transfers between devices, gathered(): pieces[place ^ bit] = lax.ppermute(pieces[place], 'gy', swap(peers, bit))  16.6 us
  transfers between devices with their start and end apart: 24, of which 9 were waited for; matrix products, arithmetic and copies ran while one was open for 12% of the time, Pallas kernels for 7%

profile of v4, /device:TPU:0, one launch (start us, length us, event | category | flops | bytes accessed | tf_op | source)
XLA Modules:
  0.0 498.2 jit_solution(11277579645450361424)
XLA Ops:
  0.0 2.6 fusion.52
  3.0 2.0 collective-permute-start.3
  5.0 2.2 fusion.53
  7.3 5.3 %collective-permute-start.1 = (f32[2,128,512]{2,1,0:T(8,128)}, f32[2,128,512]{2,1,0:T(8,128)S(1)}, u32[]{:S(2)}, u32[]{:S(2)}) collective-permute-start(f32[2,128,512]{2,1,0:T(8,128)} %get-tuple-element.43), channel_id=1, source_target_pairs={{4,0},{8,4},{12,8},{16,12},{20,16},{24,20},{28,24},{0,28},{5,1},{9... | collective-permute-start | bytes 1572872 | tf_op jit(solution)/shard_map/ppermute | solution.py:28
  14.4 1.3 copy.145
  15.8 1.1 copy.144
  16.9 2.1 fusion.8
  19.0 1.9 bitcast_maximum_fusion
  20.8 0.9 fusion.54
  23.0 4.8 collective-permute-start.5
  28.0 1.3 copy.149
  31.0 1.4 tile.4
  32.4 1.7 tile.10.marks
  34.1 2.8 select_maximum_fusion.sides
  37.9 16.4 %shard_map.29 = (f32[16,128,256]{2,1,0:T(8,128)}, f32[16,256]{1,0:T(8,128)}, f32[128,128]{1,0:T(8,128)}) custom-call(s32[1]{0:T(128)} %bitcast.18.base, f32[64,128,512]{2,1,0:T(8,128)} %below.7, f32[64,128,512]{2,1,0:T(8,128)} %below.7, f32[64,128,512]{2,1,0:T(8,128)} %below.7, f32[2,128,512]{2,1,0:T(8,128)} %copy-done.1, f32[2,128,512]{2,1,0:T(8,128)} %copy-done, ...), custom_call_target="tpu_custom_call" | custom-call | flops 1610612736 | bytes 41943040 | tf_op jit(solution)/shard_map/pallas_call | solution.py:203
  55.0 0.8 fusion.22
  55.9 0.9 constant_dynamic-slice_fusion.1
  57.5 16.5 %shard_map.28 = (f32[16,128,256]{2,1,0:T(8,128)}, f32[16,256]{1,0:T(8,128)}, f32[128,128]{1,0:T(8,128)}) custom-call(s32[1]{0:T(128)} %bitcast.12.base, f32[64,128,512]{2,1,0:T(8,128)} %below.7, f32[64,128,512]{2,1,0:T(8,128)} %below.7, f32[64,128,512]{2,1,0:T(8,128)} %below.7, f32[2,128,512]{2,1,0:T(8,128)} %copy-done.1, f32[2,128,512]{2,1,0:T(8,128)} %copy-done, ...), custom_call_target="tpu_custom_call" | custom-call | flops 1610612736 | bytes 41943040 | tf_op jit(solution)/shard_map/pallas_call | solution.py:203
  75.4 0.9 broadcast_in_dim.17.refs_10_
  76.3 8.0 %shard_map.30 = (f32[4,16,2,8,640]{4,3,2,1,0:T(8,128)}, f32[4,64,640]{2,1,0:T(8,128)}) custom-call(s32[1]{0:T(128)} %bitcast.3.refs_0_, f32[4,16]{1,0:T(4,128)} %pad_maximum_fusion.5.refs_1_, f32[16,128,256]{2,1,0:T(8,128)} %get-tuple-element.23.refs_2_, f32[16,128,256]{2,1,0:T(8,128)} %collective-permute-done.6.refs_3_, ...), custom_call_target="tpu_custom_call" | custom-call | flops 1610612736 | bytes 31457280 | tf_op jit(solution)/shard_map/pallas_call | solution.py:313
  84.3 16.4 %shard_map.32 = (f32[16,128,256]{2,1,0:T(8,128)}, f32[16,256]{1,0:T(8,128)}, f32[128,128]{1,0:T(8,128)}) custom-call(s32[1]{0:T(128)} %bitcast.22.base, f32[64,128,512]{2,1,0:T(8,128)} %below.7, f32[64,128,512]{2,1,0:T(8,128)} %below.7, f32[64,128,512]{2,1,0:T(8,128)} %below.7, f32[2,128,512]{2,1,0:T(8,128)} %copy-done.1, f32[2,128,512]{2,1,0:T(8,128)} %copy-done, ...), custom_call_target="tpu_custom_call" | custom-call | flops 1610612736 | bytes 41943040 | tf_op jit(solution)/shard_map/pallas_call | solution.py:203
  102.0 16.4 %shard_map.31 = (f32[16,128,256]{2,1,0:T(8,128)}, f32[16,256]{1,0:T(8,128)}, f32[128,128]{1,0:T(8,128)}) custom-call(s32[1]{0:T(128)} %bitcast.21.base, f32[64,128,512]{2,1,0:T(8,128)} %below.7, f32[64,128,512]{2,1,0:T(8,128)} %below.7, f32[64,128,512]{2,1,0:T(8,128)} %below.7, f32[2,128,512]{2,1,0:T(8,128)} %copy-done.1, f32[2,128,512]{2,1,0:T(8,128)} %copy-done, ...), custom_call_target="tpu_custom_call" | custom-call | flops 1610612736 | bytes 41943040 | tf_op jit(solution)/shard_map/pallas_call | solution.py:203
  118.4 1.2 fusion.19
  121.7 1.0 fusion.23.refs_8_
  122.7 8.3 %shard_map.33 = (f32[4,21,2,8,640]{4,3,2,1,0:T(8,128)}, f32[4,64,640]{2,1,0:T(8,128)}) custom-call(s32[1]{0:T(128)} %bitcast.3.refs_0_, f32[4,16]{1,0:T(4,128)} %pad_maximum_fusion.4.refs_1_, f32[16,128,256]{2,1,0:T(8,128)} %get-tuple-element.27.refs_2_, f32[16,128,256]{2,1,0:T(8,128)} %collective-permute-done.7.refs_3_, ...), custom_call_target="tpu_custom_call" | custom-call | flops 1610612736 | bytes 31457280 | tf_op jit(solution)/shard_map/pallas_call | solution.py:313
  131.0 1.9 slice_bitcast_fusion.1
  133.0 1.6 collective-permute-start.10
  135.4 18.7 %collective-permute-done.10 = f32[21,2,8,640]{3,2,1,0:T(8,128)S(1)} collective-permute-done((f32[21,2,8,640]{3,2,1,0:T(8,128)S(1)}, f32[21,2,8,640]{3,2,1,0:T(8,128)S(1)}, u32[]{:S(2)}, u32[]{:S(2)}) %collective-permute-start.10) | collective-permute-done | bytes 860192 | tf_op jit(solution)/shard_map/ppermute | solution.py:630
  154.1 18.8 %collective-permute-done.8 = f32[21,2,8,640]{3,2,1,0:T(8,128)S(1)} collective-permute-done((f32[21,2,8,640]{3,2,1,0:T(8,128)S(1)}, f32[21,2,8,640]{3,2,1,0:T(8,128)S(1)}, u32[]{:S(2)}, u32[]{:S(2)}) %collective-permute-start.8) | collective-permute-done | bytes 860192 | tf_op jit(solution)/shard_map/ppermute | solution.py:630
  172.9 1.0 slice_add_fusion.2
  173.9 1.2 slice_add_fusion.1
  175.1 1.9 copy.158
  177.1 5.9 %all-to-all-start = ((f32[8,2,37,640]{3,1,2,0:T(2,128)}), f32[8,2,37,640]{3,1,2,0:T(2,128)S(1)}, u32[]{:S(2)}, u32[]{:S(2)}) async-start(f32[8,2,37,640]{3,1,2,0:T(2,128)} %copy.158), calls=%async_computation | async-start | bytes 3031040 | tf_op jit(solution)/shard_map/all_to_all | solution.py:634
  183.0 1.6 slice_bitcast_fusion.5
  185.3 1.5 collective-permute-start.11
  186.8 14.8 %collective-permute-done.13 = f32[16,2,8,640]{3,2,1,0:T(8,128)S(1)} collective-permute-done((f32[16,2,8,640]{3,2,1,0:T(8,128)S(1)}, f32[16,2,8,640]{3,2,1,0:T(8,128)S(1)}, u32[]{:S(2)}, u32[]{:S(2)}) %collective-permute-start.13) | collective-permute-done | bytes 655392 | tf_op jit(solution)/shard_map/ppermute | solution.py:630
  201.7 13.0 %collective-permute-done.11 = f32[16,2,8,640]{3,2,1,0:T(8,128)S(1)} collective-permute-done((f32[16,2,8,640]{3,2,1,0:T(8,128)S(1)}, f32[16,2,8,640]{3,2,1,0:T(8,128)S(1)}, u32[]{:S(2)}, u32[]{:S(2)}) %collective-permute-start.11) | collective-permute-done | bytes 655392 | tf_op jit(solution)/shard_map/ppermute | solution.py:630
  214.7 1.2 bitcast_add_fusion
  215.9 1.7 copy.171
  218.5 4.7 all-to-all-start.1
  224.0 1.9 convolution_bitcast_fusion
  225.9 29.9 %all-to-all-done.1 = f32[8,2,32,640]{3,1,2,0:T(2,128)} async-done(((f32[8,2,32,640]{3,1,2,0:T(2,128)}), f32[8,2,32,640]{3,1,2,0:T(2,128)}, u32[]{:S(2)}, u32[]{:S(2)}) %all-to-all-start.1) | async-done | bytes 1310752 | tf_op jit(solution)/shard_map/all_to_all | solution.py:634
  255.8 2.5 fusion.1
  258.4 1.0 copy.187
  259.6 2.0 concatenate.89
  261.6 22.4 %all_to_all.25 = f32[32,2,2,1280]{3,2,1,0:T(2,128)S(1)} all-to-all(f32[32,2,2,1280]{3,2,1,0:T(2,128)S(1)} %concatenate.89), channel_id=1, replica_groups=mesh['gx'=8,'gy'=4] {'gy','gx'}, dimensions={0} | all-to-all | bytes 1310720 | tf_op jit(solution)/shard_map/all_to_all | solution.py:398
  284.0 1.0 copy.175
  285.0 5.5 %shard_map.34 = f32[8,5,2,64,128]{4,3,2,1,0:T(8,128)} custom-call(f32[2,256,640]{2,1,0:T(8,128)} %bitcast.176, f32[2,64,1280]{2,1,0:T(8,128)} %bitcast.183), custom_call_target="tpu_custom_call" | custom-call | tf_op jit(solution)/shard_map/pallas_call | solution.py:501
  290.5 2.8 slice.432
  293.2 3.6 all-to-all-start.3
  296.8 2.3 slice.433
  299.2 34.7 %all-to-all-done.3 = f32[8,3,2,64,128]{4,3,2,1,0:T(8,128)S(1)} async-done(((f32[8,3,2,64,128]{4,3,2,1,0:T(8,128)}), f32[8,3,2,64,128]{4,3,2,1,0:T(8,128)S(1)}, u32[]{:S(2)}, u32[]{:S(2)}) %all-to-all-start.3) | async-done | bytes 1572896 | tf_op jit(solution)/shard_map/all_to_all | solution.py:418
  333.9 4.2 all-to-all-start.4
  340.7 1.2 collective-permute-start.15
  342.0 85.7 %all-gather = f32[64,5,640]{2,1,0:T(8,128)S(1)} all-gather(f32[2,5,640]{2,1,0:T(8,128)S(1)} %copy.159), channel_id=2, replica_groups=mesh['gx'=8,'gy'=4] {'gy','gx'}, dimensions={0}, use_global_device_ids=true | all-gather | bytes 844800 | tf_op jit(solution)/shard_map/all_gather | solution.py:392
  428.2 1.0 copy.161
  432.2 16.6 %collective-permute-done.18 = f32[8,2,2,64,128]{4,3,2,1,0:T(8,128)} collective-permute-done((f32[8,2,2,64,128]{4,3,2,1,0:T(8,128)}, f32[8,2,2,64,128]{4,3,2,1,0:T(8,128)}, u32[]{:S(2)}, u32[]{:S(2)}) %collective-permute-start.18) | collective-permute-done | bytes 1048608 | tf_op jit(solution)/shard_map/ppermute | solution.py:622
  453.6 0.9 pad_maximum_fusion
  454.5 1.4 gather_fusion
  455.9 1.5 slice.424.refs_2_
  457.4 1.0 copy.169
  459.7 1.6 dynamic-slice_bitcast_fusion.refs_1_
  461.3 1.1 copy-done.8
  462.4 35.6 %shard_map.35 = f32[64,128,512]{2,1,0:T(8,128)} custom-call(s32[4]{0:T(128)} %pad_add_fusion.refs_0_, f32[64,640]{1,0:T(8,128)} %dynamic-slice_bitcast_fusion.refs_1_, f32[64,256]{1,0:T(8,128)} %slice.424.refs_2_, f32[128,128]{1,0:T(8,128)} %pad.14.refs_3_, bf16[128,256]{1,0:T(8,128)(2,1)} %fusion.27.refs_4_, bf16[256,256]{1,0:T(8,128)(2,1)} %fusion.17.refs_5_, ...), custom_call_target="tpu_custom_call" | custom-call | tf_op jit(solution)/shard_map/pallas_call | solution.py:594
  (142 shorter events, 28.0 us)
Async XLA Ops:
  2.6 19.6 %collective-permute-start.2 = (f32[64,2,512]{2,1,0:T(2,128)}, f32[64,2,512]{2,1,0:T(2,128)S(1)}, u32[]{:S(2)}, u32[]{:S(2)}) collective-permute-start(f32[64,2,512]{2,1,0:T(2,128)} %get-tuple-element.41), channel_id=1, source_target_pairs={{0,1},{1,2},{2,3},{3,0},{4,5},{5,6},{6,7},{7,4},{8,9},{9,10},{10,1... | collective-permute-start | bytes 786440 | tf_op jit(solution)/shard_map/ppermute | solution.py:29
  3.0 9.6 %slice-start.1 = ((s32[32,32,32]{2,1,0:T(8,128)}), s32[31,32,32]{2,1,0:T(8,128)S(1)}, s32[]{:S(2)}) async-start(s32[32,32,32]{2,1,0:T(8,128)} %param.3), calls=%async_computation.6 | async-start | bytes 1015808 | tf_op jit(solution)/shard_map/jit(_roll_static)/slice | solution.py:40
  3.0 19.1 %collective-permute-start.3 = (f32[64,2,512]{2,1,0:T(2,128)}, f32[64,2,512]{2,1,0:T(2,128)}, u32[]{:S(2)}, u32[]{:S(2)}) collective-permute-start(f32[64,2,512]{2,1,0:T(2,128)} %get-tuple-element.42), channel_id=1, source_target_pairs={{1,0},{2,1},{3,2},{0,3},{5,4},{6,5},{7,6},{4,7},{9,8},{10,9},{11,1... | collective-permute-start | bytes 786440 | tf_op jit(solution)/shard_map/ppermute | solution.py:30
  7.3 5.4 %copy-start.7 = (s32[32,32,32]{2,1,0:T(8,128)S(1)}, s32[32,32,32]{2,1,0:T(8,128)}, u32[]{:S(2)}) copy-start(s32[32,32,32]{2,1,0:T(8,128)} %param.3) | copy-start | bytes 393220
  7.3 5.4 %slice-start = ((s32[32,32,32]{2,1,0:T(8,128)}), s32[1,32,32]{2,1,0:T(8,128)S(1)}, s32[]{:S(2)}) async-start(s32[32,32,32]{2,1,0:T(8,128)} %param.3), calls=%async_computation.5 | async-start | bytes 32768 | tf_op jit(solution)/shard_map/jit(_roll_static)/slice | solution.py:40
  7.3 29.7 %collective-permute-start.1 = (f32[2,128,512]{2,1,0:T(8,128)}, f32[2,128,512]{2,1,0:T(8,128)S(1)}, u32[]{:S(2)}, u32[]{:S(2)}) collective-permute-start(f32[2,128,512]{2,1,0:T(8,128)} %get-tuple-element.43), channel_id=1, source_target_pairs={{4,0},{8,4},{12,8},{16,12},{20,16},{24,20},{28,24},{0,28},{5,1},{9... | collective-permute-start | bytes 1572872 | tf_op jit(solution)/shard_map/ppermute | solution.py:28
  12.6 24.3 %collective-permute-start = (f32[2,128,512]{2,1,0:T(8,128)}, f32[2,128,512]{2,1,0:T(8,128)S(1)}, u32[]{:S(2)}, u32[]{:S(2)}) collective-permute-start(f32[2,128,512]{2,1,0:T(8,128)} %get-tuple-element.44), channel_id=1, source_target_pairs={{0,4},{4,8},{8,12},{12,16},{16,20},{20,24},{24,28},{28,0},{1,5},{5... | collective-permute-start | bytes 1572872 | tf_op jit(solution)/shard_map/ppermute | solution.py:27
  18.9 1.9 copy-start.2
  22.9 11.2 %collective-permute-start.4 = (f32[2,4,512]{2,1,0:T(4,128)S(1)}, f32[2,4,512]{2,1,0:T(4,128)S(1)}, u32[]{:S(2)}, u32[]{:S(2)}) collective-permute-start(f32[2,4,512]{2,1,0:T(4,128)S(1)} %get-tuple-element.70), channel_id=1, source_target_pairs={{0,4},{4,8},{8,12},{12,16},{16,20},{20,24},{24,28},{28,0},{1,5},{5... | collective-permute-start | bytes 49160 | tf_op jit(solution)/shard_map/ppermute | solution.py:32
  23.0 11.1 %collective-permute-start.5 = (f32[2,4,512]{2,1,0:T(4,128)S(1)}, f32[2,4,512]{2,1,0:T(4,128)S(1)}, u32[]{:S(2)}, u32[]{:S(2)}) collective-permute-start(f32[2,4,512]{2,1,0:T(4,128)S(1)} %get-tuple-element.71), channel_id=1, source_target_pairs={{4,0},{8,4},{12,8},{16,12},{20,16},{24,20},{28,24},{0,28},{5,1},{9... | collective-permute-start | bytes 49160 | tf_op jit(solution)/shard_map/ppermute | solution.py:33
  36.9 0.8 copy-start
  36.9 1.0 copy-start.1
  37.9 16.4 %copy-start.3 = (f32[512,257]{0,1:T(8,128)S(1)}, f32[512,257]{0,1:T(8,128)}, u32[]{:S(2)}) copy-start(f32[512,257]{0,1:T(8,128)} %copy-done.2) | copy-start | bytes 1579012
  54.3 19.8 %collective-permute-start.6 = (f32[16,128,256]{2,1,0:T(8,128)}, f32[16,128,256]{2,1,0:T(8,128)}, u32[]{:S(2)}, u32[]{:S(2)}) collective-permute-start(f32[16,128,256]{2,1,0:T(8,128)} %get-tuple-element.24), channel_id=1, source_target_pairs={{0,1},{1,0},{2,3},{3,2},{4,5},{5,4},{6,7},{7,6},{8,9},{9,8},{10,11... | collective-permute-start | bytes 6291464 | tf_op jit(solution)/shard_map/ppermute | solution.py:355
  100.7 22.0 %collective-permute-start.7 = (f32[16,128,256]{2,1,0:T(8,128)}, f32[16,128,256]{2,1,0:T(8,128)}, u32[]{:S(2)}, u32[]{:S(2)}) collective-permute-start(f32[16,128,256]{2,1,0:T(8,128)} %get-tuple-element.29), channel_id=1, source_target_pairs={{0,1},{1,0},{2,3},{3,2},{4,5},{5,4},{6,7},{7,6},{8,9},{9,8},{10,11... | collective-permute-start | bytes 6291464 | tf_op jit(solution)/shard_map/ppermute | solution.py:355
  101.9 16.5 %copy-start.9 = (f32[128,128]{1,0:T(8,128)S(1)}, f32[128,128]{1,0:T(8,128)}, u32[]{:S(2)}) copy-start(f32[128,128]{1,0:T(8,128)} %get-tuple-element.30) | copy-start | bytes 196612
  101.9 16.5 %copy-start.10 = (f32[128,128]{1,0:T(8,128)S(1)}, f32[128,128]{1,0:T(8,128)}, u32[]{:S(2)}) copy-start(f32[128,128]{1,0:T(8,128)} %get-tuple-element.32) | copy-start | bytes 196612
  101.9 16.5 %copy-start.11 = (f32[128,128]{1,0:T(8,128)S(1)}, f32[128,128]{1,0:T(8,128)}, u32[]{:S(2)}) copy-start(f32[128,128]{1,0:T(8,128)} %get-tuple-element.31) | copy-start | bytes 196612
  102.0 17.7 %copy-start.12 = (f32[16,256]{1,0:T(8,128)S(1)}, f32[16,256]{1,0:T(8,128)}, u32[]{:S(2)}) copy-start(f32[16,256]{1,0:T(8,128)} %get-tuple-element.34) | copy-start | bytes 49156
  102.0 17.7 %copy-start.13 = (f32[16,256]{1,0:T(8,128)S(1)}, f32[16,256]{1,0:T(8,128)}, u32[]{:S(2)}) copy-start(f32[16,256]{1,0:T(8,128)} %get-tuple-element.36) | copy-start | bytes 49156
  102.0 17.7 %copy-start.14 = (f32[16,256]{1,0:T(8,128)S(1)}, f32[16,256]{1,0:T(8,128)}, u32[]{:S(2)}) copy-start(f32[16,256]{1,0:T(8,128)} %get-tuple-element.35) | copy-start | bytes 49156
  132.9 2.5 collective-permute-start.9
  133.0 21.0 %collective-permute-start.10 = (f32[21,2,8,640]{3,2,1,0:T(8,128)S(1)}, f32[21,2,8,640]{3,2,1,0:T(8,128)S(1)}, u32[]{:S(2)}, u32[]{:S(2)}) collective-permute-start(f32[21,2,8,640]{3,2,1,0:T(8,128)S(1)} %get-tuple-element.46), channel_id=1, source_target_pairs={{0,3},{1,2},{2,1},{3,0},{4,7},{5,6},{6,5},{7,4},{8,11},{9,10},{10,... | collective-permute-start | bytes 2580488 | tf_op jit(solution)/shard_map/ppermute | solution.py:630
  134.6 38.3 %collective-permute-start.8 = (f32[21,2,8,640]{3,2,1,0:T(8,128)S(1)}, f32[21,2,8,640]{3,2,1,0:T(8,128)S(1)}, u32[]{:S(2)}, u32[]{:S(2)}) collective-permute-start(f32[21,2,8,640]{3,2,1,0:T(8,128)S(1)} %get-tuple-element.47), channel_id=1, source_target_pairs={{0,2},{1,3},{2,0},{3,1},{4,6},{5,7},{6,4},{7,5},{8,10},{9,11},{10,... | collective-permute-start | bytes 2580488 | tf_op jit(solution)/shard_map/ppermute | solution.py:630
  177.1 41.4 %all-to-all-start = ((f32[8,2,37,640]{3,1,2,0:T(2,128)}), f32[8,2,37,640]{3,1,2,0:T(2,128)S(1)}, u32[]{:S(2)}, u32[]{:S(2)}) async-start(f32[8,2,37,640]{3,1,2,0:T(2,128)} %copy.158), calls=%async_computation | async-start | bytes 3031040 | tf_op jit(solution)/shard_map/all_to_all | solution.py:634
  184.6 17.0 %collective-permute-start.13 = (f32[16,2,8,640]{3,2,1,0:T(8,128)S(1)}, f32[16,2,8,640]{3,2,1,0:T(8,128)S(1)}, u32[]{:S(2)}, u32[]{:S(2)}) collective-permute-start(f32[16,2,8,640]{3,2,1,0:T(8,128)S(1)} %get-tuple-element.49), channel_id=1, source_target_pairs={{0,3},{1,2},{2,1},{3,0},{4,7},{5,6},{6,5},{7,4},{8,11},{9,10},{10,... | collective-permute-start | bytes 1966088 | tf_op jit(solution)/shard_map/ppermute | solution.py:630
  184.7 17.0 %collective-permute-start.12 = (f32[16,2,8,640]{3,2,1,0:T(8,128)S(1)}, f32[16,2,8,640]{3,2,1,0:T(8,128)S(1)}, u32[]{:S(2)}, u32[]{:S(2)}) collective-permute-start(f32[16,2,8,640]{3,2,1,0:T(8,128)S(1)} %get-tuple-element.50), channel_id=1, source_target_pairs={{0,1},{1,0},{2,3},{3,2},{4,5},{5,4},{6,7},{7,6},{8,9},{9,8},{10,11... | collective-permute-start | bytes 1966088 | tf_op jit(solution)/shard_map/ppermute | solution.py:630
  185.3 29.4 %collective-permute-start.11 = (f32[16,2,8,640]{3,2,1,0:T(8,128)S(1)}, f32[16,2,8,640]{3,2,1,0:T(8,128)S(1)}, u32[]{:S(2)}, u32[]{:S(2)}) collective-permute-start(f32[16,2,8,640]{3,2,1,0:T(8,128)S(1)} %get-tuple-element.48), channel_id=1, source_target_pairs={{0,2},{1,3},{2,0},{3,1},{4,6},{5,7},{6,4},{7,5},{8,10},{9,11},{10,... | collective-permute-start | bytes 1966088 | tf_op jit(solution)/shard_map/ppermute | solution.py:630
  217.7 5.5 %copy-start.6 = (f32[512,256]{0,1:T(8,128)S(1)}, f32[512,256]{0,1:T(8,128)}, u32[]{:S(2)}) copy-start(f32[512,256]{0,1:T(8,128)} %get-tuple-element.57) | copy-start | bytes 1572868
  218.5 37.3 %all-to-all-start.1 = ((f32[8,2,32,640]{3,1,2,0:T(2,128)}), f32[8,2,32,640]{3,1,2,0:T(2,128)}, u32[]{:S(2)}, u32[]{:S(2)}) async-start(f32[8,2,32,640]{3,1,2,0:T(2,128)} %copy.171), calls=%async_computation.1 | async-start | bytes 2621440 | tf_op jit(solution)/shard_map/all_to_all | solution.py:634
  258.3 1.2 copy-start.5
  293.2 40.6 %all-to-all-start.3 = ((f32[8,3,2,64,128]{4,3,2,1,0:T(8,128)}), f32[8,3,2,64,128]{4,3,2,1,0:T(8,128)S(1)}, u32[]{:S(2)}, u32[]{:S(2)}) async-start(f32[8,3,2,64,128]{4,3,2,1,0:T(8,128)} %slice.432), calls=%async_computation.3 | async-start | bytes 3145728 | tf_op jit(solution)/shard_map/all_to_all | solution.py:418
  333.9 96.9 %copy-start.4 = (f32[8,3,2,64,128]{4,3,2,1,0:T(8,128)}, f32[8,3,2,64,128]{4,3,2,1,0:T(8,128)S(1)}, u32[]{:S(2)}) copy-start(f32[8,3,2,64,128]{4,3,2,1,0:T(8,128)S(1)} %all-to-all-done.3) | copy-start | bytes 4718596
  333.9 95.4 %all-to-all-start.4 = ((f32[8,2,2,64,128]{4,3,2,1,0:T(8,128)}), f32[8,2,2,64,128]{4,3,2,1,0:T(8,128)}, u32[]{:S(2)}, u32[]{:S(2)}) async-start(f32[8,2,2,64,128]{4,3,2,1,0:T(8,128)} %slice.433), calls=%async_computation.4 | async-start | bytes 2097152 | tf_op jit(solution)/shard_map/all_to_all | solution.py:418
  340.7 90.1 %collective-permute-start.15 = (f32[8,3,2,64,128]{4,3,2,1,0:T(8,128)S(1)}, f32[8,3,2,64,128]{4,3,2,1,0:T(8,128)}, u32[]{:S(2)}, u32[]{:S(2)}) collective-permute-start(f32[8,3,2,64,128]{4,3,2,1,0:T(8,128)S(1)} %all-to-all-done.3), channel_id=1, source_target_pairs={{0,2},{1,3},{2,0},{3,1},{4,6},{5,7},{6,4},{7,5},{8,10},{9,11},{10,... | collective-permute-start | bytes 4718600 | tf_op jit(solution)/shard_map/ppermute | solution.py:622
  429.3 19.5 %collective-permute-start.18 = (f32[8,2,2,64,128]{4,3,2,1,0:T(8,128)}, f32[8,2,2,64,128]{4,3,2,1,0:T(8,128)}, u32[]{:S(2)}, u32[]{:S(2)}) collective-permute-start(f32[8,2,2,64,128]{4,3,2,1,0:T(8,128)} %all-to-all-done.4), channel_id=1, source_target_pairs={{0,2},{1,3},{2,0},{3,1},{4,6},{5,7},{6,4},{7,5},{8,10},{9,11},{10,... | collective-permute-start | bytes 3145736 | tf_op jit(solution)/shard_map/ppermute | solution.py:622
  430.8 30.5 %collective-permute-start.14 = (f32[8,3,2,64,128]{4,3,2,1,0:T(8,128)S(1)}, f32[8,3,2,64,128]{4,3,2,1,0:T(8,128)S(1)}, u32[]{:S(2)}, u32[]{:S(2)}) collective-permute-start(f32[8,3,2,64,128]{4,3,2,1,0:T(8,128)S(1)} %all-to-all-done.3), channel_id=1, source_target_pairs={{0,1},{1,0},{2,3},{3,2},{4,5},{5,4},{6,7},{7,6},{8,9},{9,8},{10,11... | collective-permute-start | bytes 4718600 | tf_op jit(solution)/shard_map/ppermute | solution.py:622
  430.9 30.4 %collective-permute-start.16 = (f32[8,3,2,64,128]{4,3,2,1,0:T(8,128)}, f32[8,3,2,64,128]{4,3,2,1,0:T(8,128)}, u32[]{:S(2)}, u32[]{:S(2)}) collective-permute-start(f32[8,3,2,64,128]{4,3,2,1,0:T(8,128)} %collective-permute-done.15), channel_id=1, source_target_pairs={{0,1},{1,0},{2,3},{3,2},{4,5},{5,4},{6,7},{7,6},{8,9},{9,8},{10,11... | collective-permute-start | bytes 4718600 | tf_op jit(solution)/shard_map/ppermute | solution.py:622
  432.1 29.2 %collective-permute-start.17 = (f32[8,2,2,64,128]{4,3,2,1,0:T(8,128)}, f32[8,2,2,64,128]{4,3,2,1,0:T(8,128)}, u32[]{:S(2)}, u32[]{:S(2)}) collective-permute-start(f32[8,2,2,64,128]{4,3,2,1,0:T(8,128)} %all-to-all-done.4), channel_id=1, source_target_pairs={{0,1},{1,0},{2,3},{3,2},{4,5},{5,4},{6,7},{7,6},{8,9},{9,8},{10,11... | collective-permute-start | bytes 3145736 | tf_op jit(solution)/shard_map/ppermute | solution.py:622
  448.7 12.5 %collective-permute-start.19 = (f32[8,2,2,64,128]{4,3,2,1,0:T(8,128)}, f32[8,2,2,64,128]{4,3,2,1,0:T(8,128)}, u32[]{:S(2)}, u32[]{:S(2)}) collective-permute-start(f32[8,2,2,64,128]{4,3,2,1,0:T(8,128)} %collective-permute-done.18), channel_id=1, source_target_pairs={{0,1},{1,0},{2,3},{3,2},{4,5},{5,4},{6,7},{7,6},{8,9},{9,8},{10,11... | collective-permute-start | bytes 3145736 | tf_op jit(solution)/shard_map/ppermute | solution.py:622
  461.3 1.2 copy-start.8

commit v5 on v4

--- a/solution.py
+++ b/solution.py
@@ -369,8 +369,10 @@
     for c in range(parts):
         closing = c == parts - 1
         packed = fill_part(c, packed)
+        held = kept[c][0]
         if c > 0:
-            values = values + first_axis(packed, count, table_parts[:, :, c - 1])[0]
+            held, lines = lax.optimization_barrier((held, exchanged(packed)))
+            values = values + first_axis(lines, count, table_parts[:, :, c - 1])[0]
         if closing:
             given_rows = lax.dynamic_slice_in_dim(table, row * rows + given_first, pair_rows, 0)
             ordered_rows = jnp.concatenate([given_rows, kept_rows], axis=0)
@@ -384,14 +386,11 @@
             corner = jnp.pad(corner, (0, width - half - 1))
 
         packed, side = packed_section(
-            col, kept[c][0], got[c], table_pair, kept_rows[c * count : (c + 1) * count], marks,
+            col, held, got[c], table_pair, kept_rows[c * count : (c + 1) * count], marks,
             rim, corner, side, offsets, (gx, gy), closing,
         )
-    last_values, side = first_axis(packed, count, table_parts[:, :, parts - 1])
+    last_values, side = first_axis(exchanged(packed), count, table_parts[:, :, parts - 1])
     values = values + last_values
-    side = lax.all_gather(side, ("gy", "gx"), axis=0)
-    side = jnp.transpose(side, (2, 1, 0, 3)).reshape(slabs + 1, block, width)
-
     turned = values.reshape(own, blocks, own, devices, width)
     turned = jnp.transpose(turned, (3, 1, 2, 0, 4))
     turned = [turned[:, b, :, :, : offsets[b + 1]] for b in range(blocks)]
@@ -404,25 +403,32 @@
     pick_rows = slab * rows + jnp.where(far_row, rows - pick_rows, pick_rows)
     pick_cols = jnp.arange(cols)
     pick_cols = jnp.where(far_col, (gy - col) * cols - pick_cols, col * cols + pick_cols)
-    last = square([side[slabs - 1][None, :, offsets[b] : offsets[b + 1]] for b in range(blocks)], block)[0]
-    rim = side[slabs, 0, : half + 1]
-    last = jnp.concatenate([last, rim[None, :half]], axis=0)
-    last = jnp.concatenate([last, rim[:, None]], axis=1)
-    across = last[pick_rows]
-    next_plane = lax.dynamic_index_in_dim(side, slab, 0, keepdims=False)
 
     if rows == block:
-        messages = slab_messages(values, turned, offsets, slabs)
         got = []
-        for group in tile_groups(messages.shape[1]):
-            piece = lax.all_to_all(messages[:, group], "gx", 0, 0, tiled=True)
-            got.append(gathered(piece, gy))
+        for messages in slab_messages(values, turned, side, offsets, slabs):
+            got.append(gathered(lax.all_to_all(messages, "gx", 0, 0, tiled=True), gy))
+        tiles = width // 128
+        start = tile_groups(tiles)[0].stop * own * block
+        side = jnp.stack([piece[:, start : start + 3 * own * tiles] for piece in got[0]])
+        bit = gy // 2
+        while bit:
+            paired = side.reshape((-1, 2, bit) + side.shape[1:])
+            side = jnp.where((col & bit) == 0, paired, paired[:, ::-1]).reshape(side.shape)
+            bit //= 2
+        side = side.reshape(devices, own, 3, width)
+        side = jnp.transpose(side, (2, 1, 0, 3)).reshape(3, block, width)
+        next_plane, across = side[0], rim_rows(side[1:], offsets, pick_rows)
         rim_col = col == gy // 2
         rim = across[:, pick_cols]
         return result_block(
             got, next_plane, across, rim, pick_cols, slab, far_row, rim_col, col, offsets
         )
 
+    side = lax.all_gather(side, ("gy", "gx"), axis=0)
+    side = jnp.transpose(side, (2, 1, 0, 3)).reshape(slabs + 1, block, width)
+    across = rim_rows(side[slabs - 1 :], offsets, pick_rows)
+    next_plane = lax.dynamic_index_in_dim(side, slab, 0, keepdims=False)
     sums = axis_order_sums(values, turned, offsets, block)
     messages = []
     for s in range(slabs):
@@ -458,6 +464,15 @@
     return jnp.concatenate([body, jnp.flip(body[:, :, 1:half], 2)], axis=2)
 
 
+def rim_rows(side, offsets, pick_rows):
+    blocks, block = len(offsets) - 1, offsets[1]
+    half = blocks * block
+    last = square([side[0][:, offsets[b] : offsets[b + 1]] for b in range(blocks)], block)
+    rim = side[1, 0, : half + 1]
+    last = jnp.concatenate([last, rim[None, :half]], axis=0)
+    return jnp.concatenate([last, rim[:, None]], axis=1)[pick_rows]
+
+
 def axis_order_sums(values, turned, offsets, block):
     start = 0
     sums = []
@@ -473,13 +488,16 @@
     return sums
 
 
-def message_kernel(offsets, slabs, values, turned, messages):
-    blocks = len(offsets) - 1
-    block = offsets[1]
+def message_kernel(offsets, slabs, values, turned, side, *messages):
+    blocks, block = len(offsets) - 1, offsets[1]
     values, turned = values[...], turned[...]
     own = values.shape[0]
     sums = axis_order_sums(values, turned, offsets, block)
+    groups = tile_groups(offsets[-1] // 128)
+    side_start = groups[0].stop * own * block
+    messages[0][:, side_start:] = jnp.zeros_like(messages[0][:, side_start:])
     for s in range(slabs):
+        places = s, 2 * slabs - 1 - s
         for e in range(own):
             units = []
             for b in range(blocks):
@@ -489,22 +507,31 @@
                 else:
                     units.append(sums[s][e][b * block : size, :size])
             line = jnp.concatenate(units, axis=1)
-            for tile in range(messages.shape[1]):
-                part = line[:, tile * 128 : (tile + 1) * 128]
-                messages[s, tile, e] = part
-                messages[2 * slabs - 1 - s, tile, e] = part
-
-
-def slab_messages(values, turned, offsets, slabs):
-    own, block = values.shape[0], offsets[1]
-    shape = (2 * slabs, offsets[-1] // 128, own, block, 128)
+            for group, out in zip(groups, messages):
+                for tile in range(group.start, group.stop):
+                    start = ((tile - group.start) * own + e) * block
+                    for place in places:
+                        out[place, start : start + block] = line[:, tile * 128 : (tile + 1) * 128]
+            row = side_start + 3 * e * groups[-1].stop
+            for plane in (s, slabs - 1, slabs):
+                for tile in range(groups[-1].stop):
+                    part = side[e, plane : plane + 1, tile * 128 : (tile + 1) * 128]
+                    for place in places:
+                        messages[0][place, row : row + 1] = part
+                    row += 1
+
+
+def slab_messages(values, turned, side, offsets, slabs):
+    own, block, tiles = values.shape[0], offsets[1], offsets[-1] // 128
+    sizes = [(group.stop - group.start) * own * block for group in tile_groups(tiles)]
+    sizes[0] += -(-3 * own * tiles // 8) * 8
     return pl.pallas_call(
         lambda *refs: message_kernel(offsets, slabs, *refs),
-        in_specs=[pl.BlockSpec(memory_space=pltpu.VMEM)] * 2,
-        out_specs=pl.BlockSpec(memory_space=pltpu.VMEM),
-        out_shape=jax.ShapeDtypeStruct(shape, jnp.float32),
+        in_specs=[pl.BlockSpec(memory_space=pltpu.VMEM)] * 3,
+        out_specs=[pl.BlockSpec(memory_space=pltpu.VMEM)] * 2,
+        out_shape=[jax.ShapeDtypeStruct((2 * slabs, size, 128), jnp.float32) for size in sizes],
         compiler_params=pltpu.CompilerParams(vmem_limit_bytes=VMEM_BYTES),
-    )(values, turned)
+    )(values, turned, side)
 
 
 def result_kernel(
@@ -546,7 +573,7 @@
         source = lax.div(i, devices), lax.rem(i, devices)
         parts = []
         for g, group in enumerate(groups):
-            stride = (group.stop - group.start) * own * block
+            stride = held[g].shape[0] // devices
             for tile in range(group.start, group.stop):
                 start = (tile - group.start) * own * block
                 near = [
@@ -554,7 +581,7 @@
                     for e in range(own)
                 ]
                 near = jnp.concatenate(near, axis=0)
-                far = pl.multiple_of(source[1] * stride + start + source[0] * block, block)
+                far = pl.multiple_of(source[1] * stride + start + source[0] * block, 8)
                 far = held[g][pl.ds(far, block), :]
                 kind = jnp.zeros((block, 128), jnp.int32)
                 for b in range(1, blocks):
@@ -577,9 +604,11 @@
 
 
 def result_block(got, next_plane, across, rim, pick_cols, slab, far_row, rim_col, col, offsets):
-    gx, _, own, block, _ = got[0][0].shape
+    block = offsets[1]
+    gx = got[0][0].shape[0]
     groups = tile_groups(offsets[-1] // 128)
     devices = gx * len(got[0])
+    own = block // devices
     rows, half = across.shape[0], across.shape[1] - 1
     cols = pick_cols.shape[0]
     step_rows = 8
@@ -599,8 +628,7 @@
         out_specs=pl.BlockSpec((step_rows, cols, 2 * half), lambda i: (i, 0, 0)),
         out_shape=jax.ShapeDtypeStruct((rows, cols, 2 * half), jnp.float32),
         scratch_shapes=[
-            pltpu.VMEM((devices * (group.stop - group.start) * own * block, 128), jnp.float32)
-            for group in groups
+            pltpu.VMEM((devices * group[0].shape[1], 128), jnp.float32) for group in got
         ] + [pltpu.SemaphoreType.DMA((len(groups), len(got[0])))],
         compiler_params=pltpu.CompilerParams(vmem_limit_bytes=VMEM_BYTES),
     )(places, *arrays, *pieces)
@@ -624,10 +652,14 @@
     return [pieces[place] for place in range(peers)]
 
 
-def first_axis(packed, count, table):
-    gy, _, own, gx, width = packed.shape
+def exchanged(packed):
+    gy = packed.shape[0]
+    return [packed[0]] + [lax.ppermute(packed[p], "gy", swap(gy, p)) for p in range(1, gy)]
+
+
+def first_axis(got, count, table):
+    gy, (_, own, gx, width) = len(got), got[0].shape
     half = table.shape[-1]
-    got = [packed[0]] + [lax.ppermute(packed[p], "gy", swap(gy, p)) for p in range(1, gy)]
     lines = [sum(got[p][:count] for p in range(first, gy, 2)) for first in range(2)]
     lines = jnp.concatenate(lines + [sum(piece[count:] for piece in got)], axis=0)
     lines = jnp.transpose(lines, (2, 1, 0, 3))

time: 500 us -> 454 us (0.908)
  blocking collectives: 108 us -> 43.8 us
  waiting for transfers between devices: 147 us -> 180 us
  local copies, waits for them, and re-layouts: 51.5 us -> 39.9 us
    all_gather x1 -> x0, blocking collectives: 85.7 us -> none  [on_device(): side = lax.all_gather(side, ('gy', 'gx'), axis=0)]
    all_to_all x2, waiting for transfers between devices: 30.7 us -> 59.4 us  [first_axis(): lines = lax.all_to_all(lines, 'gx', 0, 0, tiled=True)]
    all_to_all x1, blocking collectives: 22.4 us -> 43.8 us  [on_device(): got.append(gathered(lax.all_to_all(messages, 'gx', 0, 0, tiled=True), gy))]
    ppermute x6, waiting for transfers between devices: 65.5 us -> 46.5 us  [exchanged(): lax.ppermute(packed[p], 'gy', swap(gy, p))]
    ppermute x6, waiting for transfers between devices: 16.6 us -> 31.4 us  [gathered(): pieces[place ^ bit] = lax.ppermute(pieces[place], 'gy', swap(peers, bit))]
    all_to_all x2, waiting for transfers between devices: 34.7 us -> 42.8 us  [the longest x1 24.3 us: on_device(): got.append(gathered(lax.all_to_all(messages, 'gx', 0, 0, tiled=True), gy))]
  transfers between devices with their start and end apart: 24 -> 24, of which waited for: 9 -> 10; matrix products, arithmetic and copies ran while one was open for 12% -> 11% of each run, Pallas kernels for 7% -> 7%
where the time goes in v5:
time: 454 us; the launch traced here: 453 us
  waiting for transfers between devices  180 us (40%)
  Pallas kernels  123 us (27%)
  blocking collectives  43.8 us (10%)
  local copies, waits for them, and re-layouts  39.9 us (9%)
  starting transfers between devices  36.9 us (8%)
  other arithmetic  20.9 us (5%)
  matrix products  7.14 us (2%)
    pallas_call x4, Pallas kernels, filled_spectrum(): pl.pallas_call(fill_kernel, grid_spec=pltpu.PrefetchScalarGridSpec(num_sc...  65.8 us
    all_to_all x2, waiting for transfers between devices, first_axis(): lines = lax.all_to_all(lines, 'gx', 0, 0, tiled=True)  59.4 us
    ppermute x6, waiting for transfers between devices, exchanged(): lax.ppermute(packed[p], 'gy', swap(gy, p))  46.5 us
    all_to_all x1, blocking collectives, on_device(): got.append(gathered(lax.all_to_all(messages, 'gx', 0, 0, tiled=True), gy))  43.8 us
    pallas_call x1, Pallas kernels, result_block(): pl.pallas_call(lambda *refs: result_kernel(offsets, own, devices, groups,...  35.8 us
    ppermute x6, waiting for transfers between devices, gathered(): pieces[place ^ bit] = lax.ppermute(pieces[place], 'gy', swap(peers, bit))  31.4 us
    all_to_all x1, waiting for transfers between devices, on_device(): got.append(gathered(lax.all_to_all(messages, 'gx', 0, 0, tiled=True), gy))  24.3 us
    all_to_all x1, waiting for transfers between devices, on_device(): lax.all_to_all(jnp.concatenate(turned, axis=3), ('gy', 'gx'), 0, 0, tiled...  18.5 us
  transfers between devices with their start and end apart: 24, of which 10 were waited for; matrix products, arithmetic and copies ran while one was open for 11% of the time, Pallas kernels for 7%

profile of v5, /device:TPU:0, one launch (start us, length us, event | category | flops | bytes accessed | tf_op | source)
XLA Modules:
  0.0 453.0 jit_solution(1344822602004744710)
XLA Ops:
  0.0 2.6 fusion.53
  3.1 2.0 collective-permute-start.3
  5.1 2.2 fusion.54
  7.3 5.3 %collective-permute-start.1 = (f32[2,128,512]{2,1,0:T(8,128)}, f32[2,128,512]{2,1,0:T(8,128)S(1)}, u32[]{:S(2)}, u32[]{:S(2)}) collective-permute-start(f32[2,128,512]{2,1,0:T(8,128)} %get-tuple-element.57), channel_id=1, source_target_pairs={{4,0},{8,4},{12,8},{16,12},{20,16},{24,20},{28,24},{0,28},{5,1},{9... | collective-permute-start | bytes 1572872 | tf_op jit(solution)/shard_map/ppermute | solution.py:28
  14.4 1.3 copy.118
  15.8 1.1 copy.117
  16.9 2.1 fusion.8
  19.0 1.9 bitcast_maximum_fusion
  20.8 0.9 fusion.12
  22.9 4.8 %collective-permute-start.5 = (f32[2,4,512]{2,1,0:T(4,128)S(1)}, f32[2,4,512]{2,1,0:T(4,128)S(1)}, u32[]{:S(2)}, u32[]{:S(2)}) collective-permute-start(f32[2,4,512]{2,1,0:T(4,128)S(1)} %get-tuple-element.88), channel_id=1, source_target_pairs={{4,0},{8,4},{12,8},{16,12},{20,16},{24,20},{28,24},{0,28},{5,1},{9... | collective-permute-start | bytes 49160 | tf_op jit(solution)/shard_map/ppermute | solution.py:33
  27.9 1.3 copy.122
  29.2 0.8 copy.124.table_low
  30.1 0.8 copy.123.table_high
  30.9 1.4 tile.4
  32.3 1.7 tile.10.marks
  34.0 2.9 select_maximum_fusion.sides
  36.9 0.8 copy-done
  37.9 16.4 %shard_map.29 = (f32[16,128,256]{2,1,0:T(8,128)}, f32[16,256]{1,0:T(8,128)}, f32[128,128]{1,0:T(8,128)}) custom-call(s32[1]{0:T(128)} %bitcast.17.base, f32[64,128,512]{2,1,0:T(8,128)} %below.7, f32[64,128,512]{2,1,0:T(8,128)} %below.7, f32[64,128,512]{2,1,0:T(8,128)} %below.7, f32[2,128,512]{2,1,0:T(8,128)} %copy-done.1, f32[2,128,512]{2,1,0:T(8,128)} %copy-done, ...), custom_call_target="tpu_custom_call" | custom-call | flops 1610612736 | bytes 41943040 | tf_op jit(solution)/shard_map/pallas_call | solution.py:203
  55.0 0.9 fusion.23
  55.9 0.7 fusion.17
  56.6 16.6 %shard_map.28 = (f32[16,128,256]{2,1,0:T(8,128)}, f32[16,256]{1,0:T(8,128)}, f32[128,128]{1,0:T(8,128)}) custom-call(s32[1]{0:T(128)} %bitcast.11.base, f32[64,128,512]{2,1,0:T(8,128)} %below.7, f32[64,128,512]{2,1,0:T(8,128)} %below.7, f32[64,128,512]{2,1,0:T(8,128)} %below.7, f32[2,128,512]{2,1,0:T(8,128)} %copy-done.1, f32[2,128,512]{2,1,0:T(8,128)} %copy-done, ...), custom_call_target="tpu_custom_call" | custom-call | flops 1610612736 | bytes 41943040 | tf_op jit(solution)/shard_map/pallas_call | solution.py:203
  74.5 0.9 broadcast_in_dim.9.refs_10_
  75.3 8.0 %shard_map.30 = (f32[4,16,2,8,640]{4,3,2,1,0:T(8,128)}, f32[4,64,640]{2,1,0:T(8,128)}) custom-call(s32[1]{0:T(128)} %bitcast.3.refs_0_, f32[4,16]{1,0:T(4,128)} %pad_maximum_fusion.5.refs_1_, f32[16,128,256]{2,1,0:T(8,128)} %get-tuple-element.30.refs_2_, f32[16,128,256]{2,1,0:T(8,128)} %collective-permute-done.6.refs_3_, ...), custom_call_target="tpu_custom_call" | custom-call | flops 1610612736 | bytes 31457280 | tf_op jit(solution)/shard_map/pallas_call | solution.py:313
  83.3 16.4 %shard_map.32 = (f32[16,128,256]{2,1,0:T(8,128)}, f32[16,256]{1,0:T(8,128)}, f32[128,128]{1,0:T(8,128)}) custom-call(s32[1]{0:T(128)} %bitcast.34.base, f32[64,128,512]{2,1,0:T(8,128)} %below.7, f32[64,128,512]{2,1,0:T(8,128)} %below.7, f32[64,128,512]{2,1,0:T(8,128)} %below.7, f32[2,128,512]{2,1,0:T(8,128)} %copy-done.1, f32[2,128,512]{2,1,0:T(8,128)} %copy-done, ...), custom_call_target="tpu_custom_call" | custom-call | flops 1610612736 | bytes 41943040 | tf_op jit(solution)/shard_map/pallas_call | solution.py:203
  100.9 2.7 slice_bitcast_fusion.3
  103.7 1.1 collective-permute-start.9
  105.6 16.4 %shard_map.31 = (f32[16,128,256]{2,1,0:T(8,128)}, f32[16,256]{1,0:T(8,128)}, f32[128,128]{1,0:T(8,128)}) custom-call(s32[1]{0:T(128)} %bitcast.20.base, f32[64,128,512]{2,1,0:T(8,128)} %below.7, f32[64,128,512]{2,1,0:T(8,128)} %below.7, f32[64,128,512]{2,1,0:T(8,128)} %below.7, f32[2,128,512]{2,1,0:T(8,128)} %copy-done.1, f32[2,128,512]{2,1,0:T(8,128)} %copy-done, ...), custom_call_target="tpu_custom_call" | custom-call | flops 1610612736 | bytes 41943040 | tf_op jit(solution)/shard_map/pallas_call | solution.py:203
  122.0 1.2 fusion.20
  125.2 1.0 fusion.24.refs_8_
  126.2 8.8 %collective-permute-done.8 = f32[16,2,8,640]{3,2,1,0:T(8,128)} collective-permute-done((f32[16,2,8,640]{3,2,1,0:T(8,128)S(1)}, f32[16,2,8,640]{3,2,1,0:T(8,128)}, u32[]{:S(2)}, u32[]{:S(2)}) %collective-permute-start.8) | collective-permute-done | bytes 655392 | tf_op jit(solution)/shard_map/ppermute | solution.py:657
  135.1 8.3 %shard_map.33 = (f32[4,21,2,8,640]{4,3,2,1,0:T(8,128)}, f32[4,64,640]{2,1,0:T(8,128)}) custom-call(s32[1]{0:T(128)} %bitcast.3.refs_0_, f32[4,16]{1,0:T(4,128)} %pad_maximum_fusion.6.refs_1_, f32[16,128,256]{2,1,0:T(8,128)} %get-tuple-element.40.refs_2_, f32[16,128,256]{2,1,0:T(8,128)} %collective-permute-done.10.refs_3_, ...), custom_call_target="tpu_custom_call" | custom-call | flops 1610612736 | bytes 31457280 | tf_op jit(solution)/shard_map/pallas_call | solution.py:313
  143.4 1.9 slice_bitcast_fusion.1
  145.4 1.6 collective-permute-start.13
  147.7 18.7 %collective-permute-done.13 = f32[21,2,8,640]{3,2,1,0:T(8,128)S(1)} collective-permute-done((f32[21,2,8,640]{3,2,1,0:T(8,128)S(1)}, f32[21,2,8,640]{3,2,1,0:T(8,128)S(1)}, u32[]{:S(2)}, u32[]{:S(2)}) %collective-permute-start.13) | collective-permute-done | bytes 860192 | tf_op jit(solution)/shard_map/ppermute | solution.py:657
  166.5 18.8 %collective-permute-done.11 = f32[21,2,8,640]{3,2,1,0:T(8,128)S(1)} collective-permute-done((f32[21,2,8,640]{3,2,1,0:T(8,128)S(1)}, f32[21,2,8,640]{3,2,1,0:T(8,128)S(1)}, u32[]{:S(2)}, u32[]{:S(2)}) %collective-permute-start.11) | collective-permute-done | bytes 860192 | tf_op jit(solution)/shard_map/ppermute | solution.py:657
  185.3 1.0 slice_add_fusion.2
  186.3 1.2 slice_add_fusion.1
  187.5 1.9 copy.133
  189.4 6.0 %all-to-all-start.1 = ((f32[8,2,37,640]{3,1,2,0:T(2,128)}), f32[8,2,37,640]{3,1,2,0:T(2,128)S(1)}, u32[]{:S(2)}, u32[]{:S(2)}) async-start(f32[8,2,37,640]{3,1,2,0:T(2,128)} %copy.133), calls=%async_computation.1 | async-start | bytes 3031040 | tf_op jit(solution)/shard_map/all_to_all | solution.py:666
  195.4 1.2 add.215
  196.6 1.4 add.216
  198.0 1.7 copy.129
  199.8 31.1 %all-to-all-done.1 = f32[8,2,37,640]{3,1,2,0:T(2,128)S(1)} async-done(((f32[8,2,37,640]{3,1,2,0:T(2,128)}), f32[8,2,37,640]{3,1,2,0:T(2,128)S(1)}, u32[]{:S(2)}, u32[]{:S(2)}) %all-to-all-start.1) | async-done | bytes 1515552 | tf_op jit(solution)/shard_map/all_to_all | solution.py:666
  230.9 4.5 all-to-all-start
  236.2 1.9 convolution_bitcast_fusion
  238.1 28.3 %all-to-all-done = f32[8,2,32,640]{3,1,2,0:T(2,128)} async-done(((f32[8,2,32,640]{3,1,2,0:T(2,128)}), f32[8,2,32,640]{3,1,2,0:T(2,128)}, u32[]{:S(2)}, u32[]{:S(2)}) %all-to-all-start) | async-done | bytes 1310752 | tf_op jit(solution)/shard_map/all_to_all | solution.py:666
  266.4 2.6 fusion.1
  268.9 1.0 copy.161
  270.1 2.4 concatenate.80
  272.5 2.6 all-to-all-start.2
  275.8 18.5 %all-to-all-done.2 = f32[32,2,2,1280]{3,2,1,0:T(2,128)S(1)} async-done(((f32[32,2,2,1280]{3,2,1,0:T(2,128)}), f32[32,2,2,1280]{3,2,1,0:T(2,128)S(1)}, u32[]{:S(2)}, u32[]{:S(2)}) %all-to-all-start.2) | async-done | bytes 655392 | tf_op jit(solution)/shard_map/all_to_all | solution.py:397
  294.3 1.0 copy.136
  295.3 5.5 %shard_map.34 = (f32[8,416,128]{2,1,0:T(8,128)}, f32[8,256,128]{2,1,0:T(8,128)}) custom-call(f32[2,256,640]{2,1,0:T(8,128)} %bitcast.174, f32[2,64,1280]{2,1,0:T(8,128)} %bitcast.181, f32[2,5,640]{2,1,0:T(8,128)} %copy_multiply_fusion.refs_2_), custom_call_target="tpu_custom_call" | custom-call | tf_op jit(solution)/shard_map/pallas_call | solution.py:528
  300.7 43.8 %all_to_all.25 = f32[8,416,128]{2,1,0:T(8,128)S(1)} all-to-all(f32[8,416,128]{2,1,0:T(8,128)} %get-tuple-element.53), channel_id=1, replica_groups=mesh['gx'=8,'gy'=4] {'gx'}, dimensions={0} | all-to-all | bytes 3407872 | tf_op jit(solution)/shard_map/all_to_all | solution.py:410
  344.5 3.6 all-to-all-start.4
  348.1 1.2 collective-permute-start.15
  349.3 24.3 %all-to-all-done.4 = f32[8,256,128]{2,1,0:T(8,128)S(1)} async-done(((f32[8,256,128]{2,1,0:T(8,128)}), f32[8,256,128]{2,1,0:T(8,128)S(1)}, u32[]{:S(2)}, u32[]{:S(2)}) %all-to-all-start.4) | async-done | bytes 1048608 | tf_op jit(solution)/shard_map/all_to_all | solution.py:410
  373.6 1.3 collective-permute-start.18
  374.9 13.4 %collective-permute-done.15 = f32[8,416,128]{2,1,0:T(8,128)} collective-permute-done((f32[8,416,128]{2,1,0:T(8,128)S(1)}, f32[8,416,128]{2,1,0:T(8,128)}, u32[]{:S(2)}, u32[]{:S(2)}) %collective-permute-start.15) | collective-permute-done | bytes 1703968 | tf_op jit(solution)/shard_map/ppermute | solution.py:650
  390.9 17.9 %collective-permute-done.18 = f32[8,256,128]{2,1,0:T(8,128)} collective-permute-done((f32[8,256,128]{2,1,0:T(8,128)S(1)}, f32[8,256,128]{2,1,0:T(8,128)}, u32[]{:S(2)}, u32[]{:S(2)}) %collective-permute-start.18) | collective-permute-done | bytes 1048608 | tf_op jit(solution)/shard_map/ppermute | solution.py:650
  408.9 0.9 slice_bitcast_fusion.10
  409.8 0.9 slice_bitcast_fusion.11
  410.7 0.9 slice_bitcast_fusion.9
  417.0 35.8 %shard_map.35 = f32[64,128,512]{2,1,0:T(8,128)} custom-call(s32[4]{0:T(128)} %pad_add_fusion.refs_0_, f32[64,640]{1,0:T(8,128)} %bitcast.190, f32[64,256]{1,0:T(8,128)} %slice.465.refs_2_, f32[128,128]{1,0:T(8,128)} %pad.14.refs_3_, bf16[128,256]{1,0:T(8,128)(2,1)} %fusion.28.refs_4_, bf16[256,256]{1,0:T(8,128)(2,1)} %fusion.18.refs_5_, ...), custom_call_target="tpu_custom_call" | custom-call | tf_op jit(solution)/shard_map/pallas_call | solution.py:623
  (145 shorter events, 20.1 us)
Async XLA Ops:
  2.6 10.0 %slice-start.1 = ((s32[32,32,32]{2,1,0:T(8,128)}), s32[31,32,32]{2,1,0:T(8,128)S(1)}, s32[]{:S(2)}) async-start(s32[32,32,32]{2,1,0:T(8,128)} %param.3), calls=%async_computation.6 | async-start | bytes 1015808 | tf_op jit(solution)/shard_map/jit(_roll_static)/slice | solution.py:40
  2.6 19.5 %collective-permute-start.2 = (f32[64,2,512]{2,1,0:T(2,128)}, f32[64,2,512]{2,1,0:T(2,128)S(1)}, u32[]{:S(2)}, u32[]{:S(2)}) collective-permute-start(f32[64,2,512]{2,1,0:T(2,128)} %get-tuple-element.55), channel_id=1, source_target_pairs={{0,1},{1,2},{2,3},{3,0},{4,5},{5,6},{6,7},{7,4},{8,9},{9,10},{10,1... | collective-permute-start | bytes 786440 | tf_op jit(solution)/shard_map/ppermute | solution.py:29
  3.1 9.6 %copy-start.8 = (s32[32,32,32]{2,1,0:T(8,128)S(1)}, s32[32,32,32]{2,1,0:T(8,128)}, u32[]{:S(2)}) copy-start(s32[32,32,32]{2,1,0:T(8,128)} %param.3) | copy-start | bytes 393220
  3.1 9.6 %slice-start = ((s32[32,32,32]{2,1,0:T(8,128)}), s32[1,32,32]{2,1,0:T(8,128)S(1)}, s32[]{:S(2)}) async-start(s32[32,32,32]{2,1,0:T(8,128)} %param.3), calls=%async_computation.5 | async-start | bytes 32768 | tf_op jit(solution)/shard_map/jit(_roll_static)/slice | solution.py:40
  3.1 19.1 %collective-permute-start.3 = (f32[64,2,512]{2,1,0:T(2,128)}, f32[64,2,512]{2,1,0:T(2,128)}, u32[]{:S(2)}, u32[]{:S(2)}) collective-permute-start(f32[64,2,512]{2,1,0:T(2,128)} %get-tuple-element.56), channel_id=1, source_target_pairs={{1,0},{2,1},{3,2},{0,3},{5,4},{6,5},{7,6},{4,7},{9,8},{10,9},{11,1... | collective-permute-start | bytes 786440 | tf_op jit(solution)/shard_map/ppermute | solution.py:30
  7.3 29.6 %collective-permute-start.1 = (f32[2,128,512]{2,1,0:T(8,128)}, f32[2,128,512]{2,1,0:T(8,128)S(1)}, u32[]{:S(2)}, u32[]{:S(2)}) collective-permute-start(f32[2,128,512]{2,1,0:T(8,128)} %get-tuple-element.57), channel_id=1, source_target_pairs={{4,0},{8,4},{12,8},{16,12},{20,16},{24,20},{28,24},{0,28},{5,1},{9... | collective-permute-start | bytes 1572872 | tf_op jit(solution)/shard_map/ppermute | solution.py:28
  12.6 24.3 %collective-permute-start = (f32[2,128,512]{2,1,0:T(8,128)}, f32[2,128,512]{2,1,0:T(8,128)S(1)}, u32[]{:S(2)}, u32[]{:S(2)}) collective-permute-start(f32[2,128,512]{2,1,0:T(8,128)} %get-tuple-element.58), channel_id=1, source_target_pairs={{0,4},{4,8},{8,12},{12,16},{16,20},{20,24},{24,28},{28,0},{1,5},{5... | collective-permute-start | bytes 1572872 | tf_op jit(solution)/shard_map/ppermute | solution.py:27
  18.9 2.8 copy-start.3
  22.9 11.2 %collective-permute-start.4 = (f32[2,4,512]{2,1,0:T(4,128)S(1)}, f32[2,4,512]{2,1,0:T(4,128)S(1)}, u32[]{:S(2)}, u32[]{:S(2)}) collective-permute-start(f32[2,4,512]{2,1,0:T(4,128)S(1)} %get-tuple-element.87), channel_id=1, source_target_pairs={{0,4},{4,8},{8,12},{12,16},{16,20},{20,24},{24,28},{28,0},{1,5},{5... | collective-permute-start | bytes 49160 | tf_op jit(solution)/shard_map/ppermute | solution.py:32
  22.9 11.1 %collective-permute-start.5 = (f32[2,4,512]{2,1,0:T(4,128)S(1)}, f32[2,4,512]{2,1,0:T(4,128)S(1)}, u32[]{:S(2)}, u32[]{:S(2)}) collective-permute-start(f32[2,4,512]{2,1,0:T(4,128)S(1)} %get-tuple-element.88), channel_id=1, source_target_pairs={{4,0},{8,4},{12,8},{16,12},{20,16},{24,20},{28,24},{0,28},{5,1},{9... | collective-permute-start | bytes 49160 | tf_op jit(solution)/shard_map/ppermute | solution.py:33
  36.9 0.8 copy-start
  36.9 1.0 copy-start.1
  37.9 16.4 %copy-start.4 = (f32[512,257]{0,1:T(8,128)S(1)}, f32[512,257]{0,1:T(8,128)}, u32[]{:S(2)}) copy-start(f32[512,257]{0,1:T(8,128)} %copy-done.3) | copy-start | bytes 1579012
  37.9 18.0 %copy-start.7 = (f32[512,256]{0,1:T(8,128)S(1)}, f32[512,256]{0,1:T(8,128)}, u32[]{:S(2)}) copy-start(f32[512,256]{0,1:T(8,128)} %get-tuple-element.76) | copy-start | bytes 1572868
  54.2 18.9 %collective-permute-start.6 = (f32[16,128,256]{2,1,0:T(8,128)}, f32[16,128,256]{2,1,0:T(8,128)}, u32[]{:S(2)}, u32[]{:S(2)}) collective-permute-start(f32[16,128,256]{2,1,0:T(8,128)} %get-tuple-element.31), channel_id=1, source_target_pairs={{0,1},{1,0},{2,3},{3,2},{4,5},{5,4},{6,7},{7,6},{8,9},{9,8},{10,11... | collective-permute-start | bytes 6291464 | tf_op jit(solution)/shard_map/ppermute | solution.py:355
  99.7 35.4 %collective-permute-start.10 = (f32[16,128,256]{2,1,0:T(8,128)}, f32[16,128,256]{2,1,0:T(8,128)}, u32[]{:S(2)}, u32[]{:S(2)}) collective-permute-start(f32[16,128,256]{2,1,0:T(8,128)} %get-tuple-element.42), channel_id=1, source_target_pairs={{0,1},{1,0},{2,3},{3,2},{4,5},{5,4},{6,7},{7,6},{8,9},{9,8},{10,11... | collective-permute-start | bytes 6291464 | tf_op jit(solution)/shard_map/ppermute | solution.py:355
  103.7 22.6 %collective-permute-start.9 = (f32[16,2,8,640]{3,2,1,0:T(8,128)}, f32[16,2,8,640]{3,2,1,0:T(8,128)}, u32[]{:S(2)}, u32[]{:S(2)}) collective-permute-start(f32[16,2,8,640]{3,2,1,0:T(8,128)} %get-tuple-element.62), channel_id=1, source_target_pairs={{0,3},{1,2},{2,1},{3,0},{4,7},{5,6},{6,5},{7,4},{8,11},{9,10},{10,... | collective-permute-start | bytes 1966088 | tf_op jit(solution)/shard_map/ppermute | solution.py:657
  104.8 30.3 %collective-permute-start.8 = (f32[16,2,8,640]{3,2,1,0:T(8,128)S(1)}, f32[16,2,8,640]{3,2,1,0:T(8,128)}, u32[]{:S(2)}, u32[]{:S(2)}) collective-permute-start(f32[16,2,8,640]{3,2,1,0:T(8,128)S(1)} %get-tuple-element.63), channel_id=1, source_target_pairs={{0,2},{1,3},{2,0},{3,1},{4,6},{5,7},{6,4},{7,5},{8,10},{9,11},{10,... | collective-permute-start | bytes 1966088 | tf_op jit(solution)/shard_map/ppermute | solution.py:657
  105.3 29.7 %collective-permute-start.7 = (f32[16,2,8,640]{3,2,1,0:T(8,128)S(1)}, f32[16,2,8,640]{3,2,1,0:T(8,128)}, u32[]{:S(2)}, u32[]{:S(2)}) collective-permute-start(f32[16,2,8,640]{3,2,1,0:T(8,128)S(1)} %get-tuple-element.64), channel_id=1, source_target_pairs={{0,1},{1,0},{2,3},{3,2},{4,5},{5,4},{6,7},{7,6},{8,9},{9,8},{10,11... | collective-permute-start | bytes 1966088 | tf_op jit(solution)/shard_map/ppermute | solution.py:657
  105.5 16.5 %copy-start.9 = (f32[128,128]{1,0:T(8,128)S(1)}, f32[128,128]{1,0:T(8,128)}, u32[]{:S(2)}) copy-start(f32[128,128]{1,0:T(8,128)} %get-tuple-element.43) | copy-start | bytes 196612
  105.5 16.5 %copy-start.10 = (f32[128,128]{1,0:T(8,128)S(1)}, f32[128,128]{1,0:T(8,128)}, u32[]{:S(2)}) copy-start(f32[128,128]{1,0:T(8,128)} %get-tuple-element.45) | copy-start | bytes 196612
  105.5 16.5 %copy-start.11 = (f32[128,128]{1,0:T(8,128)S(1)}, f32[128,128]{1,0:T(8,128)}, u32[]{:S(2)}) copy-start(f32[128,128]{1,0:T(8,128)} %get-tuple-element.44) | copy-start | bytes 196612
  105.5 17.7 %copy-start.12 = (f32[16,256]{1,0:T(8,128)S(1)}, f32[16,256]{1,0:T(8,128)}, u32[]{:S(2)}) copy-start(f32[16,256]{1,0:T(8,128)} %get-tuple-element.47) | copy-start | bytes 49156
  105.5 17.7 %copy-start.13 = (f32[16,256]{1,0:T(8,128)S(1)}, f32[16,256]{1,0:T(8,128)}, u32[]{:S(2)}) copy-start(f32[16,256]{1,0:T(8,128)} %get-tuple-element.49) | copy-start | bytes 49156
  105.5 17.7 %copy-start.14 = (f32[16,256]{1,0:T(8,128)S(1)}, f32[16,256]{1,0:T(8,128)}, u32[]{:S(2)}) copy-start(f32[16,256]{1,0:T(8,128)} %get-tuple-element.48) | copy-start | bytes 49156
  145.3 2.5 collective-permute-start.12
  145.4 21.1 %collective-permute-start.13 = (f32[21,2,8,640]{3,2,1,0:T(8,128)S(1)}, f32[21,2,8,640]{3,2,1,0:T(8,128)S(1)}, u32[]{:S(2)}, u32[]{:S(2)}) collective-permute-start(f32[21,2,8,640]{3,2,1,0:T(8,128)S(1)} %get-tuple-element.60), channel_id=1, source_target_pairs={{0,3},{1,2},{2,1},{3,0},{4,7},{5,6},{6,5},{7,4},{8,11},{9,10},{10,... | collective-permute-start | bytes 2580488 | tf_op jit(solution)/shard_map/ppermute | solution.py:657
  147.0 38.3 %collective-permute-start.11 = (f32[21,2,8,640]{3,2,1,0:T(8,128)S(1)}, f32[21,2,8,640]{3,2,1,0:T(8,128)S(1)}, u32[]{:S(2)}, u32[]{:S(2)}) collective-permute-start(f32[21,2,8,640]{3,2,1,0:T(8,128)S(1)} %get-tuple-element.61), channel_id=1, source_target_pairs={{0,2},{1,3},{2,0},{3,1},{4,6},{5,7},{6,4},{7,5},{8,10},{9,11},{10,... | collective-permute-start | bytes 2580488 | tf_op jit(solution)/shard_map/ppermute | solution.py:657
  189.4 41.5 %all-to-all-start.1 = ((f32[8,2,37,640]{3,1,2,0:T(2,128)}), f32[8,2,37,640]{3,1,2,0:T(2,128)S(1)}, u32[]{:S(2)}, u32[]{:S(2)}) async-start(f32[8,2,37,640]{3,1,2,0:T(2,128)} %copy.133), calls=%async_computation.1 | async-start | bytes 3031040 | tf_op jit(solution)/shard_map/all_to_all | solution.py:666
  230.9 35.5 %all-to-all-start = ((f32[8,2,32,640]{3,1,2,0:T(2,128)}), f32[8,2,32,640]{3,1,2,0:T(2,128)}, u32[]{:S(2)}, u32[]{:S(2)}) async-start(f32[8,2,32,640]{3,1,2,0:T(2,128)} %copy.129), calls=%async_computation | async-start | bytes 2621440 | tf_op jit(solution)/shard_map/all_to_all | solution.py:666
  268.9 1.2 copy-start.5
  272.5 21.8 %all-to-all-start.2 = ((f32[32,2,2,1280]{3,2,1,0:T(2,128)}), f32[32,2,2,1280]{3,2,1,0:T(2,128)S(1)}, u32[]{:S(2)}, u32[]{:S(2)}) async-start(f32[32,2,2,1280]{3,2,1,0:T(2,128)} %concatenate.80), calls=%async_computation.2 | async-start | bytes 1310720 | tf_op jit(solution)/shard_map/all_to_all | solution.py:397
  344.5 67.2 %copy-start.2 = (f32[8,416,128]{2,1,0:T(8,128)}, f32[8,416,128]{2,1,0:T(8,128)S(1)}, u32[]{:S(2)}) copy-start(f32[8,416,128]{2,1,0:T(8,128)S(1)} %all_to_all.25) | copy-start | bytes 5111812
  344.5 29.1 %all-to-all-start.4 = ((f32[8,256,128]{2,1,0:T(8,128)}), f32[8,256,128]{2,1,0:T(8,128)S(1)}, u32[]{:S(2)}, u32[]{:S(2)}) async-start(f32[8,256,128]{2,1,0:T(8,128)} %get-tuple-element.54), calls=%async_computation.4 | async-start | bytes 2097152 | tf_op jit(solution)/shard_map/all_to_all | solution.py:410
  348.1 40.3 %collective-permute-start.15 = (f32[8,416,128]{2,1,0:T(8,128)S(1)}, f32[8,416,128]{2,1,0:T(8,128)}, u32[]{:S(2)}, u32[]{:S(2)}) collective-permute-start(f32[8,416,128]{2,1,0:T(8,128)S(1)} %all_to_all.25), channel_id=1, source_target_pairs={{0,2},{1,3},{2,0},{3,1},{4,6},{5,7},{6,4},{7,5},{8,10},{9,11},{10,... | collective-permute-start | bytes 5111816 | tf_op jit(solution)/shard_map/ppermute | solution.py:650
  349.3 60.5 %collective-permute-start.14 = (f32[8,416,128]{2,1,0:T(8,128)S(1)}, f32[8,416,128]{2,1,0:T(8,128)}, u32[]{:S(2)}, u32[]{:S(2)}) collective-permute-start(f32[8,416,128]{2,1,0:T(8,128)S(1)} %all_to_all.25), channel_id=1, source_target_pairs={{0,1},{1,0},{2,3},{3,2},{4,5},{5,4},{6,7},{7,6},{8,9},{9,8},{10,11... | collective-permute-start | bytes 5111816 | tf_op jit(solution)/shard_map/ppermute | solution.py:650
  373.6 38.2 %copy-start.6 = (f32[8,256,128]{2,1,0:T(8,128)}, f32[8,256,128]{2,1,0:T(8,128)S(1)}, u32[]{:S(2)}) copy-start(f32[8,256,128]{2,1,0:T(8,128)S(1)} %all-to-all-done.4) | copy-start | bytes 3145732
  373.6 35.3 %collective-permute-start.18 = (f32[8,256,128]{2,1,0:T(8,128)S(1)}, f32[8,256,128]{2,1,0:T(8,128)}, u32[]{:S(2)}, u32[]{:S(2)}) collective-permute-start(f32[8,256,128]{2,1,0:T(8,128)S(1)} %all-to-all-done.4), channel_id=1, source_target_pairs={{0,2},{1,3},{2,0},{3,1},{4,6},{5,7},{6,4},{7,5},{8,10},{9,11},{10,... | collective-permute-start | bytes 3145736 | tf_op jit(solution)/shard_map/ppermute | solution.py:650
  388.4 22.3 %collective-permute-start.16 = (f32[8,416,128]{2,1,0:T(8,128)}, f32[8,416,128]{2,1,0:T(8,128)}, u32[]{:S(2)}, u32[]{:S(2)}) collective-permute-start(f32[8,416,128]{2,1,0:T(8,128)} %collective-permute-done.15), channel_id=1, source_target_pairs={{0,1},{1,0},{2,3},{3,2},{4,5},{5,4},{6,7},{7,6},{8,9},{9,8},{10,11... | collective-permute-start | bytes 5111816 | tf_op jit(solution)/shard_map/ppermute | solution.py:650
  390.4 26.6 %collective-permute-start.17 = (f32[8,256,128]{2,1,0:T(8,128)S(1)}, f32[8,256,128]{2,1,0:T(8,128)}, u32[]{:S(2)}, u32[]{:S(2)}) collective-permute-start(f32[8,256,128]{2,1,0:T(8,128)S(1)} %all-to-all-done.4), channel_id=1, source_target_pairs={{0,1},{1,0},{2,3},{3,2},{4,5},{5,4},{6,7},{7,6},{8,9},{9,8},{10,11... | collective-permute-start | bytes 3145736 | tf_op jit(solution)/shard_map/ppermute | solution.py:650
  408.9 8.2 %collective-permute-start.19 = (f32[8,256,128]{2,1,0:T(8,128)}, f32[8,256,128]{2,1,0:T(8,128)}, u32[]{:S(2)}, u32[]{:S(2)}) collective-permute-start(f32[8,256,128]{2,1,0:T(8,128)} %collective-permute-done.18), channel_id=1, source_target_pairs={{0,1},{1,0},{2,3},{3,2},{4,5},{5,4},{6,7},{7,6},{8,9},{9,8},{10,11... | collective-permute-start | bytes 3145736 | tf_op jit(solution)/shard_map/ppermute | solution.py:650
